TPU v7x, 32 devices: a whole 2x2x4 slice. The times are simulated.
32 devices in a mesh: rep: 8 (over y, x, core), fsdp: 4 (over z).
Axes of the slice: x: 2, y: 2, z: 4, core: 2. Of those that a mesh axis runs over, the one named last changes fastest.
Arguments:
- tokens: bfloat16 [32768, 768], P(('rep', 'fsdp')), may hold values from -6 to 6
- prev_logits: bfloat16 [32768, 8], P(('rep', 'fsdp')), may hold values from -3 to 3
- out_grad: bfloat16 [32768, 768], P(('rep', 'fsdp')), may hold values from -6 to 6
- routes: int32 [32768, 2], P(('rep', 'fsdp')), may hold values from 0 to 7, all different within a row; in each aligned block of 1024 rows (0 to 1023, 1024 to 2047, ...) at most 384 rows name the same one
- doc_ids: int32 [32, 1024], P(('rep', 'fsdp')), may hold values from 0 to 5, never falling along the last dimension, each value on 1 to 512 neighbouring positions
- valid_mask: int32 [32, 1024], P(('rep', 'fsdp')), may hold values 0 or 1
- qkv_weight: bfloat16 [768, 2304], P('fsdp'), may hold values from -0.21875 to 0.21875
- proj_weight: bfloat16 [768, 768], P('fsdp'), may hold values from -0.875 to 0.875
- gain_attn: bfloat16 [768], P('fsdp'), may hold values from 0.5 to 1.5
- gain_ffn: bfloat16 [768], P('fsdp'), may hold values from 0.5 to 1.5
- router: bfloat16 [768, 8], P('fsdp'), may hold values from -0.15625 to 0.15625
- const_mix: bfloat16 [768, 4], P('fsdp'), may hold values from -0.21875 to 0.21875
- prev_mix: bfloat16 [8, 8], P('fsdp'), may hold values from -2 to 2
- const_vec: bfloat16 [768, 2], P('fsdp'), may hold values from -6 to 6
- expert_in: bfloat16 [768, 4, 4096], P('fsdp'), may hold values from -0.21875 to 0.21875
- expert_out: bfloat16 [2048, 4, 768], P('fsdp'), may hold values from -1 to 1
Outputs:
- layer_out: bfloat16 [32768, 768], P(('rep', 'fsdp'))
- input_grad: bfloat16 [32768, 768], P(('rep', 'fsdp'))
- qkv_grad: float32 [768, 2304], P('fsdp')
- proj_grad: float32 [768, 768], P('fsdp')
- gain_attn_grad: float32 [768], P('fsdp')
- gain_ffn_grad: float32 [768], P('fsdp')
- router_grad: float32 [768, 8], P('fsdp')
- const_mix_grad: float32 [768, 4], P('fsdp')
- prev_mix_grad: float32 [8, 8], P('fsdp')
- const_vec_grad: float32 [768, 2], P('fsdp')
- expert_in_grad: float32 [768, 4, 4096], P('fsdp')
- expert_out_grad: float32 [2048, 4, 768], P('fsdp')
Inputs may be any that keep to these rules, and one draw needn't show every extreme that they name: `routes`: within the rows of one device no choice is named more than 384 times, a bound that some block reaches; the two choices of a row differ; choice 4 is the zero expert, 5 the copy expert, 6 and 7 the constant experts. `doc_ids`: within a sequence the ids never fall; a document has 1 to 512 positions, one exactly 512.
All inputs are finite; a program needn't handle non-finite values. No bound on the sum of `valid_mask` on one device may be relied on, other than what follows from the above.
Results may differ from a plain program's by a relative error of at most 0.015.
Values may be sent and summed in bfloat16 or wider, within the bound.
No kernel may reach another device: no remote copies, remote signals or barrier semaphores. Data moves between devices by JAX's collectives and lax.ppermute only.
A program may use at most 320 MiB of HBM per device.

v0:
```python
from functools import partial
import math

import jax
import jax.numpy as jnp
from jax import lax
from jax.experimental import pallas as pl
from jax.experimental.pallas import tpu as pltpu
from jax.sharding import PartitionSpec as P

D = 768
HEADS = 12
HDIM = 64
EXPERTS = 4
NCH = 8
CAP = 384
LANES = 128
QB = 256
REACH = 512
VMEM_BYTES = 58 * 1024 * 1024
EPS = 1e-06
COST_SCALE = 0.02
f32 = jnp.float32
bf16 = jnp.bfloat16

NT = (((1,), (1,)), ((), ()))
TN = (((0,), (0,)), ((), ()))


def mm(a, b):
    return jnp.dot(a, b, preferred_element_type=f32)


def mm_nt(a, b):
    return lax.dot_general(a, b, NT, preferred_element_type=f32)


def mm_tn(a, b):
    return lax.dot_general(a, b, TN, preferred_element_type=f32)


def params(steps=1):
    return pltpu.CompilerParams(
        dimension_semantics=("arbitrary",) * steps, vmem_limit_bytes=VMEM_BYTES
    )


def cost(flops, nbytes):
    return pl.CostEstimate(
        flops=int(flops * COST_SCALE), bytes_accessed=int(nbytes * COST_SCALE), transcendentals=0
    )


def launch(kernel, operands, in_specs, out_specs, out_shape, after=(), **kw):
    n, skip = len(operands), len(after)

    def run(*refs):
        kernel(*refs[:n], *refs[n + skip :])

    kw.setdefault("compiler_params", pltpu.CompilerParams(vmem_limit_bytes=VMEM_BYTES))
    return pl.pallas_call(
        run,
        in_specs=list(in_specs) + [pl.BlockSpec(memory_space=pl.ANY)] * skip,
        out_specs=out_specs,
        out_shape=out_shape,
        **kw,
    )(*operands, *after)


def tie(value, *others):
    return lax.optimization_barrier((value, others))[0]


VM = pl.BlockSpec(memory_space=pltpu.VMEM)
SMEM = pl.BlockSpec(memory_space=pltpu.SMEM)
CVEC, GAIN_A, GAIN_F = NCH + 4, NCH + 6, NCH + 7


def row_of(ref, row):
    return ref[:16, :].astype(f32)[row : row + 1]


def whole(shape):
    return pl.BlockSpec(shape, lambda *_: (0,) * len(shape), pipeline_mode=pl.Buffered(1))


def rows_of(block, width):
    return pl.BlockSpec((block, width), lambda i: (i, 0))


def swap_halves(v):
    lane = lax.broadcasted_iota(jnp.int32, v.shape, 1)
    half = HDIM // 2
    ahead = pltpu.roll(v, LANES - half, 1)
    behind = pltpu.roll(v, half, 1)
    return jnp.where(lane % HDIM < half, ahead, behind)


def lay_columns(full_ref, pieces, part):
    width = pieces[0].shape[1]
    for p in range(len(pieces)):
        chosen = pieces[0][...]
        for m in range(1, len(pieces)):
            chosen = jnp.where(part == (p ^ m), pieces[m][...], chosen)
        full_ref[:, p * width : (p + 1) * width] = chosen


def qkv_kernel(count, part_ref, x_ref, small_ref, cos_ref, sin_ref, *refs):
    pieces = refs[:count]
    h_ref, q_ref, k_ref, v_ref, w_ref = refs[count:]

    @pl.when(pl.program_id(0) == 0)
    def _():
        lay_columns(w_ref, pieces, part_ref[0])

    x = x_ref[...].astype(f32)
    inverse = lax.rsqrt(jnp.mean(x * x, axis=-1, keepdims=True) + EPS)
    h = (x * inverse * row_of(small_ref, GAIN_A)).astype(bf16)
    h_ref[...] = h
    cosine, sine = cos_ref[...], sin_ref[...]
    mixed = mm(h, w_ref[...])
    for out_ref, base, scale in ((q_ref, 0, HDIM**-0.5), (k_ref, D, 1.0)):
        for c in range(0, D, LANES):
            v = mixed[:, base + c : base + c + LANES]
            turned = v * cosine + swap_halves(v) * sine
            out_ref[:, c : c + LANES] = (turned.astype(bf16).astype(f32) * scale).astype(bf16)
    v_ref[...] = mixed[:, 2 * D :].astype(bf16)


def qkv_call(part, x, small, cosine, sine, pieces, after):
    rows = x.shape[0]
    block = 256
    wide = jax.ShapeDtypeStruct((rows, D), bf16)
    return launch(
        partial(qkv_kernel, len(pieces)),
        [part, x, small, cosine, sine, *pieces],
        [
            SMEM,
            rows_of(block, D),
            whole(small.shape),
            rows_of(block, LANES),
            rows_of(block, LANES),
        ]
        + [whole(p.shape) for p in pieces],
        [rows_of(block, D)] * 4,
        [wide] * 4,
        after,
        grid=(rows // block,),
        scratch_shapes=[pltpu.VMEM((D, 3 * D), bf16)],
        compiler_params=params(),
        cost_estimate=cost(2 * rows * D * 3 * D, 2 * (5 * rows * D + 3 * D * D)),
        name="qkv_rope",
    )


def fill_bias(bias_ref, dcol_ref, drow_ref, vcol_ref, length):
    for i in range(length // QB):
        start = i * QB
        low = max(0, start - REACH)
        size = start + QB - low
        key = low + lax.broadcasted_iota(jnp.int32, (size, QB), 0)
        query = start + lax.broadcasted_iota(jnp.int32, (size, QB), 1)
        same = dcol_ref[low : low + size, :] == drow_ref[:, start : start + QB]
        usable = (vcol_ref[low : low + size, :] > 0) | (key == query)
        allowed = same & (key <= query) & usable
        bias_ref[i, :size, :] = jnp.where(allowed, 0.0, -1e30)


def lane_head(shape, head):
    lane = lax.broadcasted_iota(jnp.int32, shape, 1)
    return (lane // HDIM) == head


def attend_kernel(q_ref, k_ref, v_ref, dcol_ref, drow_ref, vcol_ref, ctx_ref, lse_ref, bias_ref):
    length = q_ref.shape[0]

    @pl.when(pl.program_id(0) == 0)
    def _():
        fill_bias(bias_ref, dcol_ref, drow_ref, vcol_ref, length)

    values_t = v_ref[...].astype(f32).T.astype(bf16)
    for i in range(length // QB):
        start = i * QB
        low = max(0, start - REACH)
        size = start + QB - low
        keys = k_ref[low : low + size, :]
        query = q_ref[start : start + QB, :]
        parts = []
        for head in range(2):
            masked = jnp.where(lane_head(query.shape, head), query, jnp.zeros_like(query))
            scores = mm_nt(keys, masked) + bias_ref[i, :size, :]
            largest = jnp.max(scores, axis=0, keepdims=True)
            raised = jnp.exp(scores - largest)
            total = jnp.sum(raised, axis=0, keepdims=True)
            part = mm(
                values_t[head * HDIM : (head + 1) * HDIM, low : low + size], raised.astype(bf16)
            )
            parts.append(part * (1.0 / total))
            lse_ref[0, head : head + 1, start : start + QB] = largest + jnp.log(total)
        ctx_ref[start : start + QB, :] = jnp.concatenate(parts, axis=0).T.astype(bf16)


def attend_call(q, k, v, dcol, drow, vcol, after):
    length = q.shape[0]
    pairs = HEADS // 2
    column = pl.BlockSpec((length, LANES), lambda p: (0, p))
    return launch(
        attend_kernel,
        [q, k, v, dcol, drow, vcol],
        [column, column, column, whole(dcol.shape), whole(drow.shape), whole(vcol.shape)],
        [column, pl.BlockSpec((1, 2, length), lambda p: (p, 0, 0))],
        [
            jax.ShapeDtypeStruct((length, D), bf16),
            jax.ShapeDtypeStruct((pairs, 2, length), f32),
        ],
        after,
        grid=(pairs,),
        scratch_shapes=[pltpu.VMEM((length // QB, REACH + QB, QB), f32)],
        compiler_params=params(),
        cost_estimate=cost(20e9, 8 * length * D),
        name="attend",
    )


def attend_back_kernel(
    q_ref,
    k_ref,
    v_ref,
    g_ref,
    lse_ref,
    dcol_ref,
    drow_ref,
    vcol_ref,
    cos_ref,
    sin_ref,
    dq_ref,
    dk_ref,
    dv_ref,
    bias_ref,
    gk_ref,
    gv_ref,
    gq_ref,
):
    length = q_ref.shape[0]

    @pl.when(pl.program_id(0) == 0)
    def _():
        fill_bias(bias_ref, dcol_ref, drow_ref, vcol_ref, length)

    gk_ref[...] = jnp.zeros_like(gk_ref)
    gv_ref[...] = jnp.zeros_like(gv_ref)
    keys_t = k_ref[...].astype(f32).T.astype(bf16)
    for i in range(length // QB):
        start = i * QB
        low = max(0, start - REACH)
        size = start + QB - low
        span = slice(low, low + size)
        keys = k_ref[span, :]
        values = v_ref[span, :]
        query = q_ref[start : start + QB, :]
        grads = g_ref[start : start + QB, :]
        for head in range(2):
            own = lane_head(query.shape, head)
            query_h = jnp.where(own, query, jnp.zeros_like(query))
            grads_h = jnp.where(own, grads, jnp.zeros_like(grads))
            scores = mm_nt(keys, query_h) + bias_ref[i, :size, :]
            probs = jnp.exp(scores - lse_ref[0, head : head + 1, start : start + QB])
            grad_probs = mm_nt(values, grads_h)
            inner = jnp.sum(probs * grad_probs, axis=0, keepdims=True)
            grad_scores = (probs * (grad_probs - inner)).astype(bf16)
            gv_ref[span, :] += mm(probs.astype(bf16), grads_h)
            gk_ref[span, :] += mm(grad_scores, query_h)
            gq_ref[head * HDIM : (head + 1) * HDIM, start : start + QB] = mm(
                keys_t[head * HDIM : (head + 1) * HDIM, span], grad_scores
            )
    cosine, sine = cos_ref[...], sin_ref[...]
    grad_q = gq_ref[...].T * HDIM**-0.5
    grad_k = gk_ref[...]
    dq_ref[...] = (grad_q * cosine - swap_halves(grad_q) * sine).astype(bf16)
    dk_ref[...] = (grad_k * cosine - swap_halves(grad_k) * sine).astype(bf16)
    dv_ref[...] = gv_ref[...].astype(bf16)


def attend_back_call(q, k, v, g, lse, dcol, drow, vcol, cosine, sine, after):
    length = q.shape[0]
    pairs = HEADS // 2
    column = pl.BlockSpec((length, LANES), lambda p: (0, p))
    return launch(
        attend_back_kernel,
        [q, k, v, g, lse, dcol, drow, vcol, cosine, sine],
        [column] * 4
        + [pl.BlockSpec((1, 2, length), lambda p: (p, 0, 0))]
        + [whole(a.shape) for a in (dcol, drow, vcol, cosine, sine)],
        [column] * 3,
        [jax.ShapeDtypeStruct((length, D), bf16)] * 3,
        after,
        grid=(pairs,),
        scratch_shapes=[
            pltpu.VMEM((length // QB, REACH + QB, QB), f32),
            pltpu.VMEM((length, LANES), f32),
            pltpu.VMEM((length, LANES), f32),
            pltpu.VMEM((LANES, length), f32),
        ],
        compiler_params=params(),
        cost_estimate=cost(45e9, 14 * length * D),
        name="attend_back",
    )


def cut_dense_kernel(quarter, widths, who_ref, qkv_ref, proj_ref, small_ref, out_ref, token_ref):
    token_ref[0] = who_ref[0]
    row = pl.multiple_of(who_ref[0] * quarter, quarter)
    start = 0
    for ref, width in zip((qkv_ref, proj_ref), widths, strict=True):
        column = pl.multiple_of(who_ref[1] * width, LANES)
        out_ref[:quarter, start : start + width] = ref[pl.ds(row, quarter), pl.ds(column, width)]
        start += width
    shard = small_ref.shape[1]
    out_ref[quarter:, :] = jnp.zeros((16, start), bf16)
    out_ref[quarter:, :shard] = small_ref[:16, :]
    out_ref[quarter:, 2 * LANES : 3 * LANES] = small_ref[16:, :LANES]


def cut_dense(who, qkv, proj, small, copies):
    shard = qkv.shape[0]
    quarter = shard // EXPERTS
    widths = (qkv.shape[1] // copies, proj.shape[1] // copies)
    total = sum(widths)
    if quarter % 16 == 0 and all(w % LANES == 0 for w in widths):
        return launch(
            partial(cut_dense_kernel, quarter, widths),
            [who, qkv, proj, small],
            [SMEM, VM, VM, VM],
            [VM, SMEM],
            [
                jax.ShapeDtypeStruct((quarter + 16, total), bf16),
                jax.ShapeDtypeStruct((1,), jnp.int32),
            ],
            name="cut_dense",
        )
    row = who[0] * quarter
    cuts = [
        lax.dynamic_slice(w, (row, who[1] * width), (quarter, width))
        for w, width in zip((qkv, proj), widths, strict=True)
    ]
    spare = total - 3 * LANES
    below = jnp.concatenate(
        [
            jnp.pad(small[:16], ((0, 0), (0, 2 * LANES - shard))),
            jnp.pad(small[16:], ((0, 0), (0, 2 * LANES - shard)))[:, :LANES],
            jnp.zeros((16, spare), bf16),
        ],
        axis=1,
    )
    return jnp.concatenate([jnp.concatenate(cuts, axis=1), below]), who[:1]


def lay_shards_kernel(count, shard, quarter, width, zi_ref, *refs):
    pieces = refs[:count]
    qkv_ref, small_ref, prev_ref = refs[count:]
    for k in range(count):
        at = lax.rem(zi_ref[0] + count - k, count)
        qkv_ref[at] = pieces[k][:quarter, :width]
        prev_ref[at] = pieces[k][quarter:, 2 * LANES : 3 * LANES]
    small_ref[16:, :] = jnp.zeros((LANES - 16, D), bf16)
    for z in range(count):
        chosen = pieces[0][quarter:, : 2 * LANES].astype(f32)
        for k in range(1, count):
            here = lax.rem(zi_ref[0] + count - k, count) == z
            chosen = jnp.where(here, pieces[k][quarter:, : 2 * LANES].astype(f32), chosen)
        small_ref[:16, z * shard : (z + 1) * shard] = chosen[:, :shard].astype(bf16)


def lay_shards(zi, pieces, shard, quarter, width, after):
    count = len(pieces)
    return launch(
        partial(lay_shards_kernel, count, shard, quarter, width),
        [zi, *pieces],
        [SMEM] + [VM] * count,
        [VM] * 3,
        [
            jax.ShapeDtypeStruct((count, quarter, width), bf16),
            jax.ShapeDtypeStruct((LANES, D), bf16),
            jax.ShapeDtypeStruct((count, 16, LANES), bf16),
        ],
        after,
        name="lay_shards",
    )


def lay_proj_kernel(count, quarter, width, zi_ref, *refs):
    pieces, out = refs[:count], refs[count]
    for k in range(count):
        at = lax.rem(zi_ref[0] + count - k, count)
        out[at] = pieces[k][:quarter, width:]


def lay_proj(zi, pieces, quarter, width, after):
    count = len(pieces)
    rest = pieces[0].shape[1] - width
    return launch(
        partial(lay_proj_kernel, count, quarter, width),
        [zi, *pieces],
        [SMEM] + [VM] * count,
        VM,
        jax.ShapeDtypeStruct((count, quarter, rest), bf16),
        after,
        name="lay_proj",
    )


def lay_xor_kernel(count, own_ref, *refs):
    pieces, out = refs[:count], refs[count]
    for k in range(count):
        out[:, own_ref[0] ^ k] = pieces[k][...]


def lay_xor(own, pieces, after=()):
    count = len(pieces)
    first, rows, columns = pieces[0].shape
    return launch(
        partial(lay_xor_kernel, count),
        [own, *pieces],
        [SMEM] + [VM] * count,
        VM,
        jax.ShapeDtypeStruct((first, count, rows, columns), bf16),
        after,
        name="lay_xor",
    )


def lanes_of(shape):
    return lax.broadcasted_iota(jnp.int32, shape, 1)


def partner(v, lane):
    return jnp.where(lane % 2 == 0, pltpu.roll(v, LANES - 1, 1), pltpu.roll(v, 1, 1))


def selected(choice_ref, lane):
    return (lane == choice_ref[:, 0:1]) | (lane == choice_ref[:, 1:2])


def after_kernel(
    count, part_ref, ctx_ref, x_ref, wsmall_ref, prev_ref, pmix_ref, choice_ref, *refs
):
    pieces = refs[:count]
    res_ref, h_ref, one_ref, gate_ref, w_ref = refs[count:]

    @pl.when(pl.program_id(0) == 0)
    def _():
        lay_columns(w_ref, pieces, part_ref[0])

    res = x_ref[...].astype(f32) + mm(ctx_ref[...], w_ref[...])
    res_ref[...] = res
    inverse = lax.rsqrt(jnp.mean(res * res, axis=-1, keepdims=True) + EPS)
    low = (res * inverse * row_of(wsmall_ref, GAIN_F)).astype(bf16)
    h_ref[...] = low
    small = mm_nt(low, wsmall_ref[...])
    logits = small + mm_tn(prev_ref[...], pmix_ref[...])
    lane = lanes_of(small.shape)
    choice = lane < NCH
    top = jnp.max(jnp.where(choice, logits, -1e30), axis=-1, keepdims=True)
    raised = jnp.where(choice, jnp.exp(jnp.where(choice, logits - top, 0.0)), 0.0)
    gates = raised / jnp.sum(raised, axis=-1, keepdims=True)
    mixing = 1.0 / (1.0 + jnp.exp(partner(small, lane) - small))
    is_mix = (lane >= NCH) & (lane < NCH + 4)
    one_ref[...] = jnp.where(choice, gates, jnp.where(is_mix, mixing, 0.0))
    taken = jnp.where(selected(choice_ref, lane), gates, 0.0).T[:NCH]
    high = taken.astype(bf16).astype(f32)
    gate_ref[...] = jnp.concatenate([high, taken - high], axis=0).astype(bf16)


def after_call(part, ctx, x, small, prev, pmix, choices, pieces):
    rows = x.shape[0]
    block = 256
    return launch(
        partial(after_kernel, len(pieces)),
        [part, ctx, x, small, prev, pmix, choices, *pieces],
        [SMEM]
        + [rows_of(block, D)] * 2
        + [
            whole(small.shape),
            pl.BlockSpec((NCH, block), lambda i: (0, i)),
            whole(pmix.shape),
            rows_of(block, 2),
        ]
        + [whole(p.shape) for p in pieces],
        [rows_of(block, D)] * 2
        + [rows_of(block, LANES), pl.BlockSpec((2 * NCH, block), lambda i: (0, i))],
        [
            jax.ShapeDtypeStruct((rows, D), f32),
            jax.ShapeDtypeStruct((rows, D), bf16),
            jax.ShapeDtypeStruct((rows, LANES), f32),
            jax.ShapeDtypeStruct((2 * NCH, rows), bf16),
        ],
        grid=(rows // block,),
        scratch_shapes=[pltpu.VMEM((D, D), bf16)],
        compiler_params=params(),
        cost_estimate=cost(2 * rows * D * D, 10 * rows * D),
        name="after_attention",
    )


EXTRA = 16


def dispatch_kernel(gated, mine_ref, spot_ref, v_ref, *refs):
    if gated:
        gate_ref, refs = refs[0], refs[1:]
    rows = v_ref.shape[0]
    slot = lax.broadcasted_iota(jnp.int32, (CAP, rows), 0)
    for k in range(EXPERTS):
        hits = jnp.where(slot == spot_ref[k : k + 1, :], 1.0, 0.0).astype(bf16)
        refs[k][:CAP, :] = mm(hits, v_ref[...]).astype(bf16)
        if gated:
            moved = mm_nt(gate_ref[...], hits)
            row = lax.broadcasted_iota(jnp.int32, moved.shape, 0) % NCH
            moved = jnp.where(row == (mine_ref[0] ^ k), moved, 0.0)
            high = jnp.sum(moved[:NCH], axis=0, keepdims=True)
            rest = jnp.sum(moved[NCH:], axis=0, keepdims=True)
            tail = jnp.concatenate(
                [high, rest, jnp.zeros((EXTRA - 2, CAP), f32)], axis=0
            ).astype(bf16)
            refs[k][CAP:, :CAP] = tail
            refs[k][CAP:, CAP:] = jnp.zeros((EXTRA, D - CAP), bf16)


def dispatch_call(mine, spot, values, gates=None, after=()):
    size = CAP + (0 if gates is None else EXTRA)
    operands = [mine, spot, values] + ([] if gates is None else [gates])
    rows = values.shape[0]
    return launch(
        partial(dispatch_kernel, gates is not None),
        operands,
        [SMEM] + [VM] * (len(operands) - 1),
        [VM] * EXPERTS,
        [jax.ShapeDtypeStruct((size, D), bf16)] * EXPERTS,
        after,
        cost_estimate=cost(2 * rows * D * CAP * EXPERTS, 2 * rows * D + 2 * EXPERTS * CAP * D),
        name="dispatch",
    )


class Plan:
    def __init__(self, replicas, shards, shard, hidden, chunks):
        self.copies = replicas // EXPERTS
        self.shards = shards
        self.shard = shard
        self.hidden = hidden
        self.chunks = chunks
        self.seg = hidden // (shards * self.copies * chunks)
        self.width = self.seg * shards
        self.wide = min(256, self.width)
        self.tiles = self.width // self.wide
        self.spans = self.wide // self.seg
        self.downs = D // self.wide
        self.rows = 2 * self.tiles * shard + self.downs * self.seg

    def column(self, half, tile, span, part, chunk):
        z = tile * self.spans + span
        base = half * self.hidden + z * (self.hidden // self.shards)
        return base + (part * self.chunks + chunk) * self.seg

    def down_row(self, part, chunk):
        return (part * self.chunks + chunk) * self.seg


def pack_kernel(plan, part_ref, in_ref, out_ref, *packs):
    part = part_ref[0]
    seg, shard = plan.seg, plan.shard
    for chunk in range(plan.chunks):
        pack = packs[chunk]
        for half in range(2):
            for tile in range(plan.tiles):
                row = (half * plan.tiles + tile) * shard
                for span in range(plan.spans):
                    at = pl.multiple_of(plan.column(half, tile, span, part, chunk), LANES)
                    pack[row : row + shard, span * seg : (span + 1) * seg] = in_ref[
                        :, pl.ds(at, seg)
                    ]
        row = 2 * plan.tiles * shard
        at = pl.multiple_of(plan.down_row(part, chunk), seg)
        for down in range(plan.downs):
            pack[row + down * seg : row + (down + 1) * seg, :] = out_ref[
                pl.ds(at, seg), down * plan.wide : (down + 1) * plan.wide
            ]


def pack_pieces(plan, part, own_in, own_out):
    if plan.seg % LANES == 0:
        vmem = pl.BlockSpec(memory_space=pltpu.VMEM)
        return pl.pallas_call(
            partial(pack_kernel, plan),
            in_specs=[SMEM, vmem, vmem],
            out_specs=[vmem] * plan.chunks,
            out_shape=[jax.ShapeDtypeStruct((plan.rows, plan.wide), bf16)] * plan.chunks,
            compiler_params=pltpu.CompilerParams(vmem_limit_bytes=VMEM_BYTES),
            name="pack",
        )(part, own_in, own_out)
    packs = []
    for chunk in range(plan.chunks):
        blocks = []
        for half in range(2):
            for tile in range(plan.tiles):
                spans = [
                    lax.dynamic_slice_in_dim(
                        own_in, plan.column(half, tile, span, part[0], chunk), plan.seg, 1
                    )
                    for span in range(plan.spans)
                ]
                blocks.append(jnp.concatenate(spans, axis=1))
        rows = lax.dynamic_slice_in_dim(own_out, plan.down_row(part[0], chunk), plan.seg, 0)
        blocks += [rows[:, d * plan.wide : (d + 1) * plan.wide] for d in range(plan.downs)]
        packs.append(jnp.concatenate(blocks, axis=0))
    return packs


def unpack_kernel(plan, begun, who_ref, *refs):
    copies, seg = plan.copies, plan.seg
    ins, downs = refs[:copies], refs[copies : 2 * copies]
    in_out, down_out = refs[2 * copies + 2 * begun :]
    mine, part = who_ref[0], who_ref[1]
    step = pl.program_id(0)
    p = step % copies
    z = (step // copies) % plan.shards
    for j in range(EXPERTS):
        chosen = ins[0][j ^ mine].astype(f32)
        for m in range(1, copies):
            chosen = jnp.where(part == (p ^ m), ins[m][j ^ mine].astype(f32), chosen)
        piece = chosen[:, :seg]
        for span in range(1, plan.spans):
            here = z % plan.spans == span
            piece = jnp.where(here, chosen[:, span * seg : (span + 1) * seg], piece)
        in_out[:, j, :] = piece

    @pl.when(step < copies)
    def _():
        for j in range(EXPERTS):
            for down in range(plan.downs):
                rows = slice(down * seg, (down + 1) * seg)
                chosen = downs[0][j ^ mine, rows, :].astype(f32)
                for m in range(1, copies):
                    chosen = jnp.where(
                        part == (p ^ m), downs[m][j ^ mine, rows, :].astype(f32), chosen
                    )
                down_out[:, j, down * plan.wide : (down + 1) * plan.wide] = chosen


def unpack_chunk(plan, who, chunk, sums, begun):
    copies, shards = plan.copies, plan.shards
    per = plan.hidden // shards
    start = 2 * plan.tiles * plan.shard
    down_rows = plan.downs * plan.seg

    def in_block(i):
        half, z = i // (shards * copies), (i // copies) % shards
        return (0, half * plan.tiles + z // plan.spans, 0)

    def down_block(i):
        return (jnp.minimum(i, copies - 1) * plan.chunks + chunk, 0, 0)

    hbm = pl.BlockSpec(memory_space=pl.ANY)
    operands = [who, *sums, *[s[:, start:, :] for s in sums], *begun]
    return launch(
        partial(unpack_kernel, plan, len(begun) // 2),
        operands,
        [SMEM]
        + [pl.BlockSpec((EXPERTS, plan.shard, plan.wide), in_block)] * copies
        + [whole((EXPERTS, down_rows, plan.wide))] * copies
        + [hbm] * len(begun),
        [
            pl.BlockSpec((plan.shard, EXPERTS, plan.seg), lambda i: (0, 0, i * plan.chunks + chunk)),
            pl.BlockSpec((plan.seg, EXPERTS, D), down_block),
        ],
        [
            jax.ShapeDtypeStruct((plan.shard, EXPERTS, 2 * plan.hidden), f32),
            jax.ShapeDtypeStruct((per, EXPERTS, D), f32),
        ],
        grid=(2 * shards * copies,),
        input_output_aliases={len(operands) - 2 + i: i for i in range(len(begun))},
        compiler_params=params(),
        cost_estimate=cost(0, 12 * plan.shard * plan.hidden * EXPERTS),
        name="unpack",
    )


def unpack_grads(plan, who, sums, begun):
    if begun:
        for chunk in range(1, plan.chunks):
            begun = unpack_chunk(plan, who, chunk, sums[chunk], begun)
        return begun
    mine, part = who[0], who[1]
    ins, outs = [], []
    for j in range(EXPERTS):
        columns = {}
        rows = []
        for p in range(plan.copies):
            for chunk in range(plan.chunks):
                stacked = jnp.stack(sums[chunk])
                piece = lax.dynamic_index_in_dim(stacked, part ^ p, 0, keepdims=False)
                piece = lax.dynamic_index_in_dim(piece, mine ^ j, 0, keepdims=False)
                for half in range(2):
                    for tile in range(plan.tiles):
                        row = (half * plan.tiles + tile) * plan.shard
                        for span in range(plan.spans):
                            columns[plan.column(half, tile, span, p, chunk)] = piece[
                                row : row + plan.shard, span * plan.seg : (span + 1) * plan.seg
                            ]
                row = 2 * plan.tiles * plan.shard
                rows.append(
                    jnp.concatenate(
                        [
                            piece[row + d * plan.seg : row + (d + 1) * plan.seg]
                            for d in range(plan.downs)
                        ],
                        axis=1,
                    )
                )
        ins.append(jnp.concatenate([columns[c] for c in sorted(columns)], axis=1))
        outs.append(jnp.concatenate(rows, axis=0))
    return jnp.stack(ins, axis=1).astype(f32), jnp.stack(outs, axis=1).astype(f32)


def expert_kernel(plan, first, last, *refs):
    refs = list(refs)

    def take(n):
        out = refs[:n]
        del refs[:n]
        return out

    copies = plan.copies
    x_refs, y_refs = take(EXPERTS), take(EXPERTS)
    w_refs = take(copies)
    carry_in = [] if first else take(2)
    grad_outs = take(copies)
    if last:
        dx_outs, ret_outs = take(EXPERTS), take(EXPERTS)
        carry_out = []
    else:
        carry_out = take(2)
    xs, ds, xt, gcol, ret_acc, dx_acc, wg, wu, wo, act_s, dg_s, du_s, grads, sems = refs
    rows = EXPERTS * CAP
    shard, seg, wide, tiles = plan.shard, plan.seg, plan.wide, plan.tiles

    carries = [
        pltpu.make_async_copy(src, dst, sems.at[i])
        for i, (src, dst) in enumerate(zip(carry_in, (ret_acc, dx_acc)))
    ]
    for copy in carries:
        copy.start()
    for k in range(EXPERTS):
        span = slice(k * CAP, (k + 1) * CAP)
        x = x_refs[k][:CAP, :]
        xs[span, :] = x
        xt[:, span] = x.astype(f32).T.astype(bf16)
        extra = x_refs[k][CAP:, :CAP].astype(f32)
        gate = (extra[0:1] + extra[1:2]).T
        gcol[span, :] = jnp.broadcast_to(gate, (CAP, LANES))
        ds[span, :] = (y_refs[k][...].astype(f32) * gate).astype(bf16)
    if first:
        ret_acc[...] = jnp.zeros_like(ret_acc)
        dx_acc[...] = jnp.zeros_like(dx_acc)
    for copy in carries:
        copy.wait()

    sends = []
    for m in range(copies):
        w = w_refs[m]
        for z in range(plan.shards):
            for tile in range(tiles):
                for half, target in ((0, wg), (1, wu)):
                    row = (half * tiles + tile) * shard
                    target[z * shard : (z + 1) * shard, tile * wide : (tile + 1) * wide] = w[
                        z, row : row + shard, :
                    ]
            for down in range(plan.downs):
                row = 2 * tiles * shard + down * seg
                wo[z * seg : (z + 1) * seg, down * wide : (down + 1) * wide] = w[
                    z, row : row + seg, :
                ]

        def block(b, _):
            span = pl.ds(pl.multiple_of(b * CAP, CAP), CAP)
            x, d = xs[span, :], ds[span, :]
            gate = mm(x, wg[...])
            up = mm(x, wu[...])
            grad_act = mm_nt(d, wo[...])
            sig = 1.0 / (1.0 + jnp.exp(-gate))
            silu = gate * sig
            act = (silu * up).astype(bf16)
            grad_up = (grad_act * silu).astype(bf16)
            grad_gate = (grad_act * up * (sig + silu * (1.0 - sig))).astype(bf16)
            act_s[span, :] = act
            du_s[span, :] = grad_up
            dg_s[span, :] = grad_gate
            ret_acc[span, :] += mm(act, wo[...])
            dx_acc[span, :] += mm_nt(grad_gate, wg[...]) + mm_nt(grad_up, wu[...])
            return 0

        lax.fori_loop(0, EXPERTS, block, 0)
        if m == copies - 1 and not last:
            for i, (src, dst) in enumerate(zip((ret_acc, dx_acc), carry_out, strict=True)):
                copy = pltpu.make_async_copy(src, dst, sems.at[2 + i])
                copy.start()
                sends.append(copy)
        if m == copies - 1 and last:
            for k in range(EXPERTS):
                span = slice(k * CAP, (k + 1) * CAP)
                ret = ret_acc[span, :]
                dgate = jnp.sum(ret * y_refs[k][...].astype(f32), axis=-1, keepdims=True)
                dgate = jnp.broadcast_to(dgate, (CAP, LANES)).T[:1]
                ret_outs[k][...] = (ret * gcol[span, :1]).astype(bf16)
                dx_outs[k][:CAP, :] = dx_acc[span, :].astype(bf16)
                high = dgate.astype(bf16).astype(f32)
                tail = jnp.concatenate(
                    [high, dgate - high, jnp.zeros((EXTRA - 2, CAP), f32)], axis=0
                ).astype(bf16)
                dx_outs[k][CAP:, :CAP] = tail
                dx_outs[k][CAP:, CAP:] = jnp.zeros((EXTRA, D - CAP), bf16)
        for half, source in ((0, dg_s), (1, du_s)):
            for tile in range(tiles):
                made = mm(xt[...], source[:, tile * wide : (tile + 1) * wide]).astype(bf16)
                row = (half * tiles + tile) * shard
                for z in range(plan.shards):
                    grads[m, z, row : row + shard, :] = made[z * shard : (z + 1) * shard, :]
        for tile in range(tiles):
            made = mm_tn(act_s[:, tile * wide : (tile + 1) * wide], ds[...]).astype(bf16)
            for span in range(plan.spans):
                z = tile * plan.spans + span
                for down in range(plan.downs):
                    row = 2 * tiles * shard + down * seg
                    grads[m, z, row : row + seg, :] = made[
                        span * seg : (span + 1) * seg, down * wide : (down + 1) * wide
                    ]
        copy = pltpu.make_async_copy(grads.at[m], grad_outs[m], sems.at[4 + m])
        copy.start()
        sends.append(copy)
    for copy in sends:
        copy.wait()


def expert_call(plan, xs, ys, weights, carried, last):
    first = carried is None
    rows = EXPERTS * CAP
    vmem = pl.BlockSpec(memory_space=pltpu.VMEM)
    hbm = pl.BlockSpec(memory_space=pl.ANY)
    copies = plan.copies
    in_specs = [vmem] * (2 * EXPERTS + copies)
    operands = list(xs) + list(ys) + list(weights)
    if not first:
        in_specs += [hbm] * 2
        operands += list(carried)
    out_specs = [hbm] * copies
    out_shape = [jax.ShapeDtypeStruct((plan.shards, plan.rows, plan.wide), bf16)] * copies
    if last:
        out_specs += [vmem] * (2 * EXPERTS)
        out_shape += [jax.ShapeDtypeStruct((CAP + EXTRA, D), bf16)] * EXPERTS
        out_shape += [jax.ShapeDtypeStruct((CAP, D), bf16)] * EXPERTS
    else:
        out_specs += [hbm] * 2
        out_shape += [jax.ShapeDtypeStruct((rows, D), f32)] * 2
    made = pl.pallas_call(
        partial(expert_kernel, plan, first, last),
        in_specs=in_specs,
        out_specs=out_specs,
        out_shape=out_shape,
        scratch_shapes=[
            pltpu.VMEM((rows, D), bf16),
            pltpu.VMEM((rows, D), bf16),
            pltpu.VMEM((D, rows), bf16),
            pltpu.VMEM((rows, LANES), f32),
            pltpu.VMEM((rows, D), f32),
            pltpu.VMEM((rows, D), f32),
            pltpu.VMEM((D, plan.width), bf16),
            pltpu.VMEM((D, plan.width), bf16),
            pltpu.VMEM((plan.width, D), bf16),
            pltpu.VMEM((rows, plan.width), bf16),
            pltpu.VMEM((rows, plan.width), bf16),
            pltpu.VMEM((rows, plan.width), bf16),
            pltpu.VMEM((copies, plan.shards, plan.rows, plan.wide), bf16),
            pltpu.SemaphoreType.DMA((4 + copies,)),
        ],
        compiler_params=pltpu.CompilerParams(vmem_limit_bytes=VMEM_BYTES),
        cost_estimate=cost(
            18 * rows * D * plan.width * copies, 12 * D * plan.width * copies + 12 * rows * D
        ),
        name="experts",
    )(*operands)
    return made[:copies], made[copies:]


def spots_of(place_ref, rows):
    slot = lax.broadcasted_iota(jnp.int32, (rows, EXPERTS * CAP), 1)
    hit = (slot == place_ref[:, 0:1]) | (slot == place_ref[:, 1:2])
    return jnp.where(hit, 1.0, 0.0).astype(bf16)


def constant_gates(one, chosen, m):
    a0 = one[:, NCH + 2 * m : NCH + 2 * m + 1]
    a1 = one[:, NCH + 2 * m + 1 : NCH + 2 * m + 2]
    gate = chosen[:, EXPERTS + 2 + m : EXPERTS + 3 + m]
    return gate, a0, a1


def back_kernel(
    count,
    who_ref,
    res_ref,
    h_ref,
    dy_ref,
    one_ref,
    place_ref,
    choice_ref,
    prev_ref,
    wsmall_ref,
    *refs,
):
    dx_refs, refs = refs[:EXPERTS], refs[EXPERTS:]
    pieces, refs = refs[:count], refs[count:]
    (
        dres_ref,
        branch_ref,
        dctx_ref,
        dsmall_ref,
        gain_out,
        prev_out,
        cvec_out,
        w_ref,
        dg_ref,
    ) = refs

    @pl.when(pl.program_id(0) == 0)
    def _():
        gain_out[...] = jnp.zeros_like(gain_out)
        prev_out[...] = jnp.zeros_like(prev_out)
        cvec_out[...] = jnp.zeros_like(cvec_out)
        dsmall_ref[...] = jnp.zeros_like(dsmall_ref)
        lay_columns(w_ref, pieces, who_ref[1])
        lane = lanes_of((CAP, LANES))
        for k in range(EXPERTS):
            columns = dx_refs[k][CAP:, :CAP].astype(f32).T
            at = who_ref[0] ^ k
            made = jnp.where(lane == at, columns[:, 0:1], 0.0)
            made = jnp.where(lane == at + 16, columns[:, 1:2], made)
            dg_ref[k * CAP : (k + 1) * CAP, :] = made.astype(bf16)

    res = res_ref[...]
    rows = res.shape[0]
    one = one_ref[...]
    lane = lanes_of(one.shape)
    chosen = jnp.where(selected(choice_ref, lane), one, 0.0)
    choice = lane < NCH
    is_mix = (lane >= NCH) & (lane < NCH + 4)
    spots = spots_of(place_ref, rows)
    moved = jnp.zeros(res.shape, f32)
    for k in range(EXPERTS):
        moved = moved + mm(spots[:, k * CAP : (k + 1) * CAP], dx_refs[k][:CAP, :])
    from_experts = mm(spots, dg_ref[...])
    from_experts = from_experts + pltpu.roll(from_experts, LANES - 16, 1)

    inverse = lax.rsqrt(jnp.mean(res * res, axis=-1, keepdims=True) + EPS)
    dy = dy_ref[...]
    dyf = dy.astype(f32)
    gain = row_of(wsmall_ref, GAIN_F)
    spread = res * inverse * gain
    hd = jnp.sum(spread * dyf, axis=-1, keepdims=True)
    cd = mm_nt(dy, wsmall_ref[...])
    coef = chosen[:, EXPERTS + 1 : EXPERTS + 2]
    grads = jnp.where(lane < EXPERTS, from_experts, 0.0)
    grads = jnp.where(lane == EXPERTS + 1, hd, grads)
    made = jnp.zeros_like(one)
    for m in range(2):
        gate, a0, a1 = constant_gates(one, chosen, m)
        dot = cd[:, CVEC + m : CVEC + m + 1]
        coef = coef + gate * a0
        grads = jnp.where(lane == EXPERTS + 2 + m, a0 * hd + a1 * dot, grads)
        grads = jnp.where(lane == NCH + 2 * m, gate * hd, grads)
        grads = jnp.where(lane == NCH + 2 * m + 1, gate * dot, grads)
        made = jnp.where(lane == m, gate * a1, made)
    grads = jnp.where(is_mix | selected(choice_ref, lane), grads, 0.0)
    weighted = one * grads
    mean_choice = jnp.sum(jnp.where(choice, weighted, 0.0), axis=-1, keepdims=True)
    d_logits = jnp.where(choice, one * (grads - mean_choice), 0.0)
    d_mix = one * (grads - (weighted + partner(weighted, lane)))
    d_small = jnp.where(choice, d_logits, jnp.where(is_mix, d_mix, 0.0))
    low = d_small.astype(bf16)
    spread_grad = moved + mm(low, wsmall_ref[...]) + coef * dyf
    scaled = spread_grad * gain
    mean_dot = jnp.mean(res * scaled, axis=-1, keepdims=True)
    d_res = dyf + inverse * scaled - res * (inverse * inverse * inverse * mean_dot)
    dres_ref[...] = d_res
    gain_out[...] += jnp.sum(spread_grad * res * inverse, axis=0, keepdims=True)
    branch = d_res.astype(bf16)
    branch_ref[...] = branch
    dctx_ref[...] = mm_nt(branch, w_ref[...]).astype(bf16)
    dsmall_ref[...] += mm_tn(low, h_ref[...])
    high = d_logits.astype(bf16)
    rest = (d_logits - high.astype(f32)).astype(bf16)
    prev = prev_ref[...]
    prev_out[...] += mm(prev, high) + mm(prev, rest)
    high = made.astype(bf16)
    rest = (made - high.astype(f32)).astype(bf16)
    cvec_out[...] += mm_tn(high, dy) + mm_tn(rest, dy)


def back_call(who, res, h, dy, one, places, choices, prev, small, dx, pieces, after):
    rows = res.shape[0]
    block = 256
    tall = jax.ShapeDtypeStruct((LANES, D), f32)
    return launch(
        partial(back_kernel, len(pieces)),
        [who, res, h, dy, one, places, choices, prev, small, *dx, *pieces],
        [SMEM]
        + [rows_of(block, D)] * 3
        + [rows_of(block, LANES)]
        + [rows_of(block, 2)] * 2
        + [pl.BlockSpec((NCH, block), lambda i: (0, i))]
        + [whole(a.shape) for a in (small, *dx, *pieces)],
        [rows_of(block, D)] * 3
        + [whole((LANES, D)), whole((1, D)), whole((NCH, LANES)), whole((LANES, D))],
        [
            jax.ShapeDtypeStruct((rows, D), f32),
            jax.ShapeDtypeStruct((rows, D), bf16),
            jax.ShapeDtypeStruct((rows, D), bf16),
            tall,
            jax.ShapeDtypeStruct((1, D), f32),
            jax.ShapeDtypeStruct((NCH, LANES), f32),
            tall,
        ],
        after,
        grid=(rows // block,),
        scratch_shapes=[pltpu.VMEM((D, D), bf16), pltpu.VMEM((EXPERTS * CAP, LANES), bf16)],
        compiler_params=params(),
        cost_estimate=cost(2 * rows * D * (D + 2048), 20 * rows * D),
        name="combine_back",
    )


def finish_kernel(res_ref, one_ref, place_ref, choice_ref, small_ref, *refs):
    ret_refs, out_ref = refs[:EXPERTS], refs[EXPERTS]
    res = res_ref[...]
    one = one_ref[...]
    lane = lanes_of(one.shape)
    chosen = jnp.where(selected(choice_ref, lane), one, 0.0)
    inverse = lax.rsqrt(jnp.mean(res * res, axis=-1, keepdims=True) + EPS)
    total = res
    coef = chosen[:, EXPERTS + 1 : EXPERTS + 2]
    for m in range(2):
        gate, a0, a1 = constant_gates(one, chosen, m)
        coef = coef + gate * a0
        total = total + (gate * a1) * row_of(small_ref, CVEC + m)
    total = total + (coef * inverse) * res * row_of(small_ref, GAIN_F)
    spots = spots_of(place_ref, res.shape[0])
    for k in range(EXPERTS):
        total = total + mm(spots[:, k * CAP : (k + 1) * CAP], ret_refs[k][...])
    out_ref[...] = total.astype(bf16)


def finish_call(res, one, places, choices, small, ret, after):
    rows = res.shape[0]
    block = 256
    return launch(
        finish_kernel,
        [res, one, places, choices, small, *ret],
        [rows_of(block, D), rows_of(block, LANES)]
        + [rows_of(block, 2)] * 2
        + [whole(a.shape) for a in (small, *ret)],
        rows_of(block, D),
        jax.ShapeDtypeStruct((rows, D), bf16),
        after,
        grid=(rows // block,),
        compiler_params=params(),
        cost_estimate=cost(2 * rows * D * 1536, 10 * rows * D),
        name="layer_out",
    )


def dense_kernel(copies, h_ref, ctx_ref, dq_ref, dk_ref, dv_ref, branch_ref, *outs):
    cut = 4 * D // copies
    ht = h_ref[...].astype(f32).T.astype(bf16)
    ct = ctx_ref[...].astype(f32).T.astype(bf16)
    step = 384
    for index, (left, right) in enumerate(
        ((ht, dq_ref), (ht, dk_ref), (ht, dv_ref), (ct, branch_ref))
    ):
        for c in range(0, D, step):
            made = mm(left, right[:, c : c + step]).astype(bf16)
            at = index * D + c
            done = 0
            while done < step:
                owner, column = (at + done) // cut, (at + done) % cut
                size = min(step - done, cut - column)
                outs[owner][:, column : column + size] = made[:, done : done + size]
                done += size


def dense_call(copies, h, ctx, dq, dk, dv, branch, after):
    rows = h.shape[0]
    return launch(
        partial(dense_kernel, copies),
        [h, ctx, dq, dk, dv, branch],
        [VM] * 6,
        [VM] * copies,
        [jax.ShapeDtypeStruct((D, 4 * D // copies), bf16)] * copies,
        after,
        cost_estimate=cost(8 * rows * D * D, 12 * rows * D + 8 * D * D),
        name="dense_grads",
    )


def fold_parts_kernel(copies, who_ref, *refs):
    dense, got = refs[:copies], refs[copies : 2 * copies - 1]
    small, outs = refs[2 * copies - 1], refs[2 * copies :]
    cut = dense[0].shape[-1]
    for k in range(EXPERTS):
        at = who_ref[0] ^ k
        own = dense[0][:, at].astype(f32)
        for p in range(1, copies):
            own = jnp.where(who_ref[1] == p, dense[p][:, at].astype(f32), own)
        for piece in got:
            own = own + piece[:, at].astype(f32)
        outs[k][:, :, :cut] = own.astype(bf16)
        outs[k][:, :, cut:] = small[:, at]


def fold_parts(who, dense, got, small, shards):
    copies = len(dense)
    cut = dense[0].shape[1]
    quarter = D // (shards * EXPERTS)
    shape = (shards, EXPERTS, quarter, cut)
    operands = [who] + [a.reshape(shape) for a in (*dense, *got)]
    operands.append(small.reshape(shards, EXPERTS, quarter, LANES))
    return launch(
        partial(fold_parts_kernel, copies),
        operands,
        [SMEM] + [VM] * (len(operands) - 1),
        [VM] * EXPERTS,
        [jax.ShapeDtypeStruct((shards, quarter, cut + LANES), bf16)] * EXPERTS,
        name="fold_parts",
    )


def fold_quarters_kernel(count, zi_ref, *refs):
    pieces, outs = refs[:count], refs[count:]
    for k, out in enumerate(outs):
        at = lax.rem(zi_ref[0] + k, len(outs))
        total = pieces[0][at].astype(f32)
        for piece in pieces[1:]:
            total = total + piece[at].astype(f32)
        out[...] = total.astype(bf16)


def fold_quarters(zi, pieces, after=()):
    shards, rows, columns = pieces[0].shape
    return launch(
        partial(fold_quarters_kernel, len(pieces)),
        [zi, *pieces],
        [SMEM] + [VM] * len(pieces),
        [VM] * shards,
        [jax.ShapeDtypeStruct((rows, columns), bf16)] * shards,
        after,
        name="fold_quarters",
    )


def fold_copies(pieces):
    shape = pieces[0].shape
    block = pl.BlockSpec((1,) + shape[1:], lambda i: (i, 0, 0))
    return launch(
        fold_shards_kernel,
        pieces,
        [block] * len(pieces),
        block,
        jax.ShapeDtypeStruct(shape, bf16),
        grid=(shape[0],),
        compiler_params=params(),
        cost_estimate=cost(0, 0),
        name="fold_copies",
    )


def fold_shards_kernel(*refs):
    total = refs[0][...].astype(f32)
    for ref in refs[1:-1]:
        total = total + ref[...].astype(f32)
    refs[-1][...] = total.astype(bf16)


def fold_shards(pieces):
    return launch(
        fold_shards_kernel,
        pieces,
        [VM] * len(pieces),
        VM,
        jax.ShapeDtypeStruct(pieces[0].shape, bf16),
        name="fold_shards",
    )


def unpack_dense_kernel(count, part_ref, *refs):
    pieces, (qkv_ref, proj_ref, small_ref) = refs[:count], refs[count:]
    cut = pieces[0].shape[1] - LANES
    small = pieces[0][:, cut:].astype(f32)
    for piece in pieces[1:]:
        small = small + piece[:, cut:].astype(f32)
    small_ref[...] = small
    for p in range(count):
        chosen = pieces[0][:, :cut].astype(f32)
        for m in range(1, count):
            chosen = jnp.where(part_ref[0] == (p ^ m), pieces[m][:, :cut].astype(f32), chosen)
        start = p * cut
        in_qkv = max(0, min(cut, 3 * D - start))
        if in_qkv:
            qkv_ref[:, start : start + in_qkv] = chosen[:, :in_qkv]
        if in_qkv < cut:
            at = start + in_qkv - 3 * D
            proj_ref[:, at : at + cut - in_qkv] = chosen[:, in_qkv:]


def unpack_dense(part, pieces):
    rows = pieces[0].shape[0]
    return launch(
        partial(unpack_dense_kernel, len(pieces)),
        [part, *pieces],
        [SMEM] + [VM] * len(pieces),
        [VM] * 3,
        [
            jax.ShapeDtypeStruct((rows, 3 * D), f32),
            jax.ShapeDtypeStruct((rows, D), f32),
            jax.ShapeDtypeStruct((rows, LANES), f32),
        ],
        name="unpack_dense",
    )


def last_kernel(
    count,
    shards,
    part_ref,
    dq_ref,
    dk_ref,
    dv_ref,
    x_ref,
    dres_ref,
    small_ref,
    dsmall_ref,
    gain_f_ref,
    prev_ref,
    cvec_ref,
    *refs,
):
    pieces = refs[:count]
    out_ref, small_out, w_ref, gain_ref = refs[count:]

    @pl.when(pl.program_id(0) == 0)
    def _():
        gain_ref[...] = jnp.zeros_like(gain_ref)
        lay_columns(w_ref, pieces, part_ref[0])

    grad = mm_nt(dq_ref[...], w_ref[:, :D])
    grad = grad + mm_nt(dk_ref[...], w_ref[:, D : 2 * D])
    grad = grad + mm_nt(dv_ref[...], w_ref[:, 2 * D :])
    x = x_ref[...].astype(f32)
    inverse = lax.rsqrt(jnp.mean(x * x, axis=-1, keepdims=True) + EPS)
    scaled = grad * row_of(small_ref, GAIN_A)
    mean_dot = jnp.mean(x * scaled, axis=-1, keepdims=True)
    d_x = inverse * scaled - x * (inverse * inverse * inverse * mean_dot)
    out_ref[...] = (dres_ref[...] + d_x).astype(bf16)
    gain_ref[...] += jnp.sum(grad * x * inverse, axis=0, keepdims=True)

    @pl.when(pl.program_id(0) == pl.num_programs(0) - 1)
    def _():
        row = lax.broadcasted_iota(jnp.int32, (LANES, D), 0)
        total = jnp.where(row < CVEC, dsmall_ref[...], 0.0)
        for m in range(2):
            total = jnp.where(row == CVEC + m, cvec_ref[m : m + 1, :], total)
        total = jnp.where(row == GAIN_A, gain_ref[...], total)
        total = jnp.where(row == GAIN_F, gain_f_ref[...], total)
        total = total.T
        owned = NCH // shards
        shard = D // shards
        row = lax.broadcasted_iota(jnp.int32, total.shape, 0)
        lane = lanes_of((NCH, LANES))
        prev = pltpu.roll(jnp.where(lane < NCH, prev_ref[...], 0.0), 16, 1)
        for index in range(NCH):
            at = (index // owned) * shard + index % owned
            total = jnp.where(row == at, total + prev[index : index + 1, :], total)
        small_out[...] = total.astype(bf16)


def last_call(part, shards, dq, dk, dv, x, dres, small, smalls, pieces, after):
    rows = x.shape[0]
    block = 256
    return launch(
        partial(last_kernel, len(pieces), shards),
        [part, dq, dk, dv, x, dres, small, *smalls, *pieces],
        [SMEM]
        + [rows_of(block, D)] * 5
        + [whole(a.shape) for a in (small, *smalls, *pieces)],
        [rows_of(block, D), whole((D, LANES))],
        [jax.ShapeDtypeStruct((rows, D), bf16), jax.ShapeDtypeStruct((D, LANES), bf16)],
        after,
        grid=(rows // block,),
        scratch_shapes=[pltpu.VMEM((D, 3 * D), bf16), pltpu.VMEM((1, D), f32)],
        compiler_params=params(),
        cost_estimate=cost(6 * rows * D * D, 14 * rows * D),
        name="input_grad",
    )


def body(
    replicas,
    shards,
    tokens,
    prev_logits,
    out_grad,
    routes,
    doc_ids,
    valid_mask,
    qkv_weight,
    proj_weight,
    gain_attn,
    gain_ffn,
    router,
    const_mix,
    prev_mix,
    const_vec,
    expert_in,
    expert_out,
):
    me = lax.axis_index("rep")
    zi = lax.axis_index("fsdp")
    copies = replicas // EXPERTS
    mine = me // copies
    part = me % copies
    rows = tokens.shape[0]
    shard = qkv_weight.shape[0]
    hidden = expert_in.shape[2] // 2
    quarter = shard // EXPERTS
    plan = Plan(replicas, shards, shard, hidden, 2)
    zi_s = zi.reshape(1).astype(jnp.int32)
    mine_s = mine.reshape(1).astype(jnp.int32)
    part_s = part.reshape(1).astype(jnp.int32)
    who = jnp.concatenate([mine_s, part_s])

    def to_expert(a, k):
        return lax.ppermute(a, "rep", [(i, i ^ (k * copies)) for i in range(replicas)])

    def to_part(a, m):
        return lax.ppermute(a, "rep", [(i, i ^ m) for i in range(replicas)])

    def spin(a, k):
        return lax.ppermute(a, "fsdp", [(i, (i + k) % shards) for i in range(shards)])

    def by_xor(pieces, own, axis):
        size = pieces[0].shape[axis]
        shape = list(pieces[0].shape)
        shape[axis] = size * len(pieces)
        full = jnp.zeros(shape, pieces[0].dtype)
        for k, piece in enumerate(pieces):
            full = lax.dynamic_update_slice_in_dim(full, piece, (own ^ k) * size, axis)
        return full

    width = 3 * D // copies
    owned = prev_mix.shape[0]
    smalls = jnp.concatenate(
        [
            router.T,
            const_mix.T,
            const_vec.T,
            gain_attn[None],
            gain_ffn[None],
            jnp.pad(prev_mix, ((0, 16 - owned), (0, shard - NCH))),
        ]
    )
    piece, mine_late = cut_dense(who, qkv_weight, proj_weight, smalls, copies)
    spun = [piece] + [spin(piece, k) for k in range(1, shards)]

    own_in = lax.dynamic_index_in_dim(expert_in, mine_late[0], 1, keepdims=False)
    own_out = lax.dynamic_index_in_dim(expert_out, mine_late[0], 1, keepdims=False)
    packs = pack_pieces(plan, part_s, own_in, own_out)
    gathered = [lax.all_gather(p, "fsdp", axis=0, tiled=False) for p in packs]

    def weights_after(chunk, done):
        full = tie(gathered[chunk], done)
        return [full] + [to_part(full, m) for m in range(1, copies)]

    docs = doc_ids.reshape(-1)
    drow = docs[None, :]
    dcol = docs[:, None]
    vcol = valid_mask.reshape(-1)[:, None]
    first_place = jnp.sum((drow < dcol).astype(jnp.int32), axis=1)
    offset = (jnp.arange(rows, dtype=jnp.int32) - first_place).astype(f32)
    frequency = jnp.exp(
        jnp.arange(HDIM // 2, dtype=f32) * (-2.0 * math.log(10000.0) / HDIM)
    )
    angles = offset[:, None] * frequency[None, :]
    cosine, sine = jnp.cos(angles), jnp.sin(angles)
    cosine = jnp.concatenate([cosine] * 4, axis=1)
    sine = jnp.concatenate([-sine, sine, -sine, sine], axis=1)

    routes_t = routes.T
    chosen = jnp.where(routes_t < EXPERTS, routes_t ^ mine, routes_t)
    kinds = jnp.arange(EXPERTS, dtype=jnp.int32)
    named = jnp.any(chosen[:, None, :] == kinds[None, :, None], axis=0)
    later = jnp.triu(jnp.ones((rows, rows), bf16), 1)
    rank = mm(named.astype(bf16), later).astype(jnp.int32)
    spot = jnp.where(named, rank, CAP)
    hit = chosen[:, None, :] == kinds[None, :, None]
    places = jnp.sum(jnp.where(hit, (kinds[:, None] * CAP + rank)[None], 0), axis=1)
    places = jnp.where(chosen < EXPERTS, places, -1).T

    qkv_part, small, prevs = lay_shards(
        zi_s, spun, shard, quarter, width, (packs[0],)
    )
    pmix = prevs[:, :owned].reshape(NCH, LANES)

    def exchanged(blocks):
        return [blocks[0]] + [to_expert(blocks[k], k) for k in range(1, EXPERTS)]

    def over_parts(half):
        half = half.reshape(D, half.shape[3])
        pieces = [half] + [to_part(half, m) for m in range(1, copies)]
        if half.shape[1] % LANES == 0:
            return pieces
        return [by_xor(pieces, part, 1)]

    qkv_half = lay_xor(
        mine_s, exchanged([qkv_part] * EXPERTS), (cosine, sine, spot, dcol, vcol, places)
    )
    qkv_pieces = over_parts(qkv_half)
    part_q = part_s if len(qkv_pieces) == copies else jnp.zeros_like(part_s)
    ys = dispatch_call(mine_s, spot, out_grad, after=(qkv_half,))
    proj_part = lay_proj(zi_s, spun, quarter, width, (ys[0],))

    prev = prev_logits.T
    h1, q, k, v = qkv_call(
        part_q, tokens, small, cosine, sine, qkv_pieces, (ys[0], proj_part)
    )
    proj_half = lay_xor(mine_s, exchanged([proj_part] * EXPERTS), (h1,))
    proj_pieces = over_parts(proj_half)
    part_p = part_s if len(proj_pieces) == copies else jnp.zeros_like(part_s)
    ctx, lse = attend_call(q, k, v, dcol, drow, vcol, (proj_half,))
    ys = exchanged(ys)
    ctx = tie(ctx, ys)
    res, h2, one, gates = after_call(
        part_p, ctx, tokens, small, prev, pmix, routes, proj_pieces
    )

    xs = dispatch_call(mine_s, spot, h2, gates)
    weights = [weights_after(0, ctx)] + [
        weights_after(c, xs[0]) for c in range(1, plan.chunks)
    ]
    xs = exchanged(xs)
    carried = None
    chunk_grads = []
    for chunk in range(plan.chunks):
        grads, carried = expert_call(
            plan, xs, ys, weights[chunk], carried, chunk == plan.chunks - 1
        )
        chunk_grads.append(grads)
    dx = exchanged(carried[:EXPERTS])

    totals = [
        fold_copies([grads[0]] + [to_part(grads[m], m) for m in range(1, copies)])
        for grads in chunk_grads
    ]
    summed = [lax.psum_scatter(t, "fsdp", scatter_dimension=0, tiled=False) for t in totals]

    who_p = jnp.concatenate([mine_s, part_p])
    dres, branch, dctx, dsmall, gain_f_grad, prev_grad, cvec_grad = back_call(
        who_p,
        res,
        h2,
        out_grad,
        one,
        places,
        routes,
        prev,
        small,
        dx,
        proj_pieces,
        totals,
    )
    ret = exchanged(tie(carried[EXPERTS:], branch))
    dq, dk, dv = attend_back_call(q, k, v, dctx, lse, dcol, drow, vcol, cosine, sine, ())
    spread = [exchanged([tie(summed[0], dq)] * EXPERTS)]
    dense = dense_call(copies, h1, ctx, tie(dq, ret), dk, dv, branch, ())

    def columns(index):
        if copies == 2:
            return jnp.where(index == 0, dense[0], dense[1])
        return lax.dynamic_index_in_dim(jnp.stack(dense), index, 0, keepdims=False)

    got = [to_part(columns(part ^ m), m) for m in range(1, copies)]
    input_grad, smalls = last_call(
        part_q,
        shards,
        dq,
        dk,
        dv,
        tokens,
        dres,
        small,
        (dsmall, gain_f_grad, prev_grad, cvec_grad),
        qkv_pieces,
        (dense[0],),
    )
    quarters = fold_parts(who, dense, got, smalls, shards)
    quarters = tie(quarters, spread[0])

    def over_copies(pieces):
        stacked = jnp.stack(pieces)
        return [stacked] + [to_part(stacked, m) for m in range(1, copies)]

    spread[0] = over_copies(tie(spread[0], quarters))
    begun = ()
    if plan.seg % LANES == 0:
        begun = unpack_chunk(plan, who, 0, spread[0], begun)
    bands = fold_quarters(zi_s, exchanged(quarters), begun)
    spread += [exchanged([tie(piece, bands)] * EXPERTS) for piece in summed[1:]]
    out = finish_call(res, one, places, routes, small, tie(ret, bands), ())
    tail = fold_shards(
        [bands[0]] + tie([spin(bands[k], k) for k in range(1, shards)], out)
    )
    spread[1:] = [over_copies(tie(pieces, tail)) for pieces in spread[1:]]
    tail = lay_xor(mine_s, [t[None] for t in exchanged([tail] * EXPERTS)])
    tail = tail.reshape(shard, tail.shape[3])
    tails = [tail] + [to_part(tail, m) for m in range(1, copies)]
    qkv_grad, proj_grad, small_grad = unpack_dense(part_s, tails)

    full_in, full_out = unpack_grads(plan, who, spread, begun)
    return (
        out,
        input_grad,
        qkv_grad,
        proj_grad,
        small_grad[:, GAIN_A],
        small_grad[:, GAIN_F],
        small_grad[:, :NCH],
        small_grad[:, NCH : NCH + 4],
        small_grad[:owned, 16 : 16 + NCH],
        small_grad[:, CVEC : CVEC + 2],
        full_in,
        full_out,
    )


def solution(mesh):
    replicas, shards = mesh.shape["rep"], mesh.shape["fsdp"]
    split = P(("rep", "fsdp"), None)
    matrix = P("fsdp", None)
    cube = P("fsdp", None, None)
    in_specs = (split,) * 6 + (matrix, matrix, P("fsdp"), P("fsdp")) + (matrix,) * 4 + (cube, cube)
    out_specs = (split, split, matrix, matrix, P("fsdp"), P("fsdp")) + (matrix,) * 4 + (cube, cube)
    return jax.shard_map(
        partial(body, replicas, shards),
        mesh=mesh,
        in_specs=in_specs,
        out_specs=out_specs,
        check_vma=False,
    )
```

profile of v0, /device:TPU:0, one launch (start us, length us, event | category | flops | bytes accessed | tf_op | source)
XLA Modules:
  0.0 524.5 jit_solution(5453512600552585129)
XLA Ops:
  10.0 3.2 concatenate.14.refs_3_
  13.2 2.0 cut_dense.1
  15.2 3.1 collective-permute-start
  18.3 2.6 collective-permute-start.1
  24.1 6.5 %constant_dynamic-slice_fusion.1 = bf16[192,1,4096]{2,1,0:T(2,128)(2,1)S(1)} fusion(bf16[192,4,4096]{2,1,0:T(4,128)(2,1)} %param.30, s32[]{:T(128)S(6)} %select_n.51), kind=kLoop, calls=%fused_computation.34 | loop fusion | bytes 3145732 | tf_op jit(solution)/shard_map/jit(dynamic_index_in_dim)/dynamic_slice | solution.py:1381
  30.7 2.9 copy.102
  36.2 2.9 pack.1
  40.9 1.9 fusion.9
  43.6 2.1 lay_shards.1
  54.9 4.3 collective-permute-done.3.refs_2_
  59.1 8.6 %collective-permute-done.4.refs_3_ = bf16[4,48,1152]{2,1,0:T(8,128)(2,1)} collective-permute-done((bf16[4,48,1152]{2,1,0:T(8,128)(2,1)}, bf16[4,48,1152]{2,1,0:T(8,128)(2,1)}, u32[]{:S(2)}, u32[]{:S(2)}) %collective-permute-start.4) | collective-permute-done | bytes 442400 | tf_op jit(solution)/shard_map/ppermute | solution.py:1349
  67.7 2.7 lay_xor.3.refs_3_
  70.5 4.9 dispatch.2
  82.2 24.9 %collective-permute-done.7.refs_2_ = bf16[4,48,384]{2,1,0:T(8,128)(2,1)S(1)} collective-permute-done((bf16[4,48,384]{2,1,0:T(8,128)(2,1)}, bf16[4,48,384]{2,1,0:T(8,128)(2,1)S(1)}, u32[]{:S(2)}, u32[]{:S(2)}) %collective-permute-start.7) | collective-permute-done | bytes 147488 | tf_op jit(solution)/shard_map/ppermute | solution.py:1349
  109.8 8.8 %qkv_rope.1 = (bf16[1024,768]{1,0:T(8,128)(2,1)}, bf16[1024,768]{1,0:T(8,128)(2,1)}, bf16[1024,768]{1,0:T(8,128)(2,1)}, bf16[1024,768]{1,0:T(8,128)(2,1)}) custom-call(s32[1]{0:T(128)} %bitcast.part_ref.refs_0_, bf16[1024,768]{1,0:T(8,128)(2,1)} %refs_4_.3, bf16[128,768]{1,0:T(8,128)(2,1)} %get-tuple-element.112.refs_2_.refs_3_.refs_8_.refs_6_.refs_4_, ...), custom_call_target="tpu_custom_call" | custom-call | flops 72477576 | bytes 228065 | tf_op jit(solution)/shard_map/qkv_rope/pallas_call | solution.py:61
  119.4 2.0 lay_xor.4.refs_6_
  121.4 25.9 %attend.1 = (bf16[1024,768]{1,0:T(8,128)(2,1)}, f32[6,2,1024]{2,1,0:T(2,128)}) custom-call(bf16[1024,768]{1,0:T(8,128)(2,1)} %get-tuple-element.115.refs_0_, bf16[1024,768]{1,0:T(8,128)(2,1)} %get-tuple-element.116.refs_1_, bf16[1024,768]{1,0:T(8,128)(2,1)} %get-tuple-element.117.refs_2_, s32[1024,1]{1,0:T(8,128)} %copy.85.refs_8_.refs_3_.refs_5_, ...), custom_call_target="tpu_custom_call" | custom-call | flops 400000000 | bytes 125829 | tf_op jit(solution)/shard_map/attend/pallas_call | solution.py:61
  149.2 3.2 collective-permute-done.13.refs_8_.refs_14_
  153.2 8.2 %after_attention.1 = (f32[1024,768]{1,0:T(8,128)}, bf16[1024,768]{1,0:T(8,128)(2,1)}, f32[1024,128]{1,0:T(8,128)}, bf16[16,1024]{1,0:T(8,128)(2,1)}) custom-call(s32[1]{0:T(128)} %bitcast.part_ref.refs_0_, bf16[1024,768]{1,0:T(8,128)(2,1)} %get-tuple-element.123.refs_1_, bf16[1024,768]{1,0:T(8,128)(2,1)} %refs_4_.3, ...), custom_call_target="tpu_custom_call" | custom-call | flops 24159192 | bytes 157286 | tf_op jit(solution)/shard_map/after_attention/pallas_call | solution.py:61
  161.5 6.1 %dispatch.3 = (bf16[400,768]{1,0:T(8,128)(2,1)}, bf16[400,768]{1,0:T(8,128)(2,1)}, bf16[400,768]{1,0:T(8,128)(2,1)}, bf16[400,768]{1,0:T(8,128)(2,1)}) custom-call(s32[1]{0:T(128)} %bitcast.2.refs_0_, s32[4,1024]{1,0:T(4,128)} %get-tuple-element.257.refs_7_.refs_1_, bf16[1024,768]{1,0:T(8,128)(2,1)} %get-tuple-element.127.refs_2_, ...), custom_call_target="tpu_custom_call" | custom-call | flops 48318384 | bytes 78643 | tf_op jit(solution)/shard_map/dispatch/pallas_call | solution.py:61
  171.0 13.4 %collective-permute-done.14.refs_1_ = bf16[400,768]{1,0:T(8,128)(2,1)S(1)} collective-permute-done((bf16[400,768]{1,0:T(8,128)(2,1)}, bf16[400,768]{1,0:T(8,128)(2,1)S(1)}, u32[]{:S(2)}, u32[]{:S(2)}) %collective-permute-start.14) | collective-permute-done | bytes 614432 | tf_op jit(solution)/shard_map/ppermute | solution.py:1349
  184.4 13.1 %collective-permute-done.15.refs_2_ = bf16[400,768]{1,0:T(8,128)(2,1)S(1)} collective-permute-done((bf16[400,768]{1,0:T(8,128)(2,1)}, bf16[400,768]{1,0:T(8,128)(2,1)S(1)}, u32[]{:S(2)}, u32[]{:S(2)}) %collective-permute-start.15) | collective-permute-done | bytes 614432 | tf_op jit(solution)/shard_map/ppermute | solution.py:1349
  199.3 31.9 %experts.2 = (bf16[4,1152,256]{2,1,0:T(8,128)(2,1)}, bf16[4,1152,256]{2,1,0:T(8,128)(2,1)}, f32[1536,768]{1,0:T(8,128)}, f32[1536,768]{1,0:T(8,128)}) custom-call(bf16[400,768]{1,0:T(8,128)(2,1)} %get-tuple-element.129.refs_0_, bf16[400,768]{1,0:T(8,128)(2,1)} %copy-done.8, bf16[400,768]{1,0:T(8,128)(2,1)} %copy-done.9, bf16[400,768]{1,0:T(8,128)(2,1)} %copy-done.10, ...), custom_call_target="tpu_custom_call" | custom-call | flops 434865440 | bytes 471859 | tf_op jit(solution)/shard_map/experts/pallas_call | solution.py:864
  231.8 6.6 %collective-permute-done.22.refs_1_ = bf16[4,1152,256]{2,1,0:T(8,128)(2,1)} collective-permute-done((bf16[4,1152,256]{2,1,0:T(8,128)(2,1)}, bf16[4,1152,256]{2,1,0:T(8,128)(2,1)}, u32[]{:S(2)}, u32[]{:S(2)}) %collective-permute-start.22) | collective-permute-done | bytes 2359328 | tf_op jit(solution)/shard_map/ppermute | solution.py:1352
  238.4 4.5 fold_copies.2.refs_15_
  244.4 36.6 %experts.3 = (bf16[4,1152,256]{2,1,0:T(8,128)(2,1)}, bf16[4,1152,256]{2,1,0:T(8,128)(2,1)}, bf16[400,768]{1,0:T(8,128)(2,1)}, bf16[400,768]{1,0:T(8,128)(2,1)}, ...) custom-call(bf16[400,768]{1,0:T(8,128)(2,1)} %get-tuple-element.129., ...), custom_call_target="tpu_custom_call" | custom-call | flops 434865440 | bytes 471859 | tf_op jit(solution)/shard_map/experts/pallas_call | solution.py:864
  287.3 4.5 fold_copies.3.refs_16_
  291.8 6.4 %collective-permute-done.19.refs_10_ = bf16[400,768]{1,0:T(8,128)(2,1)S(1)} collective-permute-done((bf16[400,768]{1,0:T(8,128)(2,1)}, bf16[400,768]{1,0:T(8,128)(2,1)S(1)}, u32[]{:S(2)}, u32[]{:S(2)}) %collective-permute-start.19) | collective-permute-done | bytes 614432 | tf_op jit(solution)/shard_map/ppermute | solution.py:1349
  299.0 12.8 %collective-permute-done.21.refs_12_ = bf16[400,768]{1,0:T(8,128)(2,1)} collective-permute-done((bf16[400,768]{1,0:T(8,128)(2,1)}, bf16[400,768]{1,0:T(8,128)(2,1)}, u32[]{:S(2)}, u32[]{:S(2)}) %collective-permute-start.21) | collective-permute-done | bytes 614432 | tf_op jit(solution)/shard_map/ppermute | solution.py:1349
  311.8 18.9 %combine_back.1 = (f32[1024,768]{1,0:T(8,128)}, bf16[1024,768]{1,0:T(8,128)(2,1)}, bf16[1024,768]{1,0:T(8,128)(2,1)}, f32[128,768]{1,0:T(8,128)}, f32[1,768]{1,0...) custom-call(s32[2]{0:T(128)} %pad_add_fusion.refs_0_, f32[1024,768]{1,0:T(8,128)} %get-tuple-element.125.refs_1_.refs_0_, ...), custom_call_target="tpu_custom_call" | custom-call | flops 88583696 | bytes 314572 | tf_op jit(solution)/shard_map/combine_back/pallas_call | solution.py:61
  334.3 31.3 %attend_back.1 = (bf16[1024,768]{1,0:T(8,128)(2,1)}, bf16[1024,768]{1,0:T(8,128)(2,1)}, bf16[1024,768]{1,0:T(8,128)(2,1)}) custom-call(bf16[1024,768]{1,0:T(8,128)(2,1)} %get-tuple-element.115.refs_0_, bf16[1024,768]{1,0:T(8,128)(2,1)} %get-tuple-element.116.refs_1_, bf16[1024,768]{1,0:T(8,128)(2,1)} %get-tuple-element.117.refs_2_, ...), custom_call_target="tpu_custom_call" | custom-call | flops 900000000 | bytes 220200 | tf_op jit(solution)/shard_map/attend_back/pallas_call | solution.py:61
  365.7 12.4 %dense_grads.1 = (bf16[768,1536]{1,0:T(8,128)(2,1)}, bf16[768,1536]{1,0:T(8,128)(2,1)}) custom-call(bf16[1024,768]{1,0:T(8,128)(2,1)} %get-tuple-element.118.refs_5_.refs_0_, bf16[1024,768]{1,0:T(8,128)(2,1)} %get-tuple-element.123.refs_1_, bf16[1024,768]{1,0:T(8,128)(2,1)} %get-tuple-element.158.refs_2_.refs_1_, ...), custom_call_target="tpu_custom_call" | custom-call | flops 96636768 | bytes 283115 | tf_op jit(solution)/shard_map/dense_grads/pallas_call | solution.py:61
  378.1 3.4 broadcast_select_fusion
  385.2 10.6 %input_grad.1 = (bf16[1024,768]{1,0:T(8,128)(2,1)}, bf16[768,128]{1,0:T(8,128)(2,1)}) custom-call(s32[1]{0:T(128)} %bitcast.part_ref.refs_0_, bf16[1024,768]{1,0:T(8,128)(2,1)} %get-tuple-element.158.refs_2_.refs_1_, bf16[1024,768]{1,0:T(8,128)(2,1)} %get-tuple-element.159.refs_3_.refs_2_, bf16[1024,768]{1,0:T(8,128)(2,1)} %get-tuple-element.160.refs_4_.refs_3_, ...), custom_call_target="tpu_custom_call" | custom-call | flops 72477576 | bytes 220200 | tf_op jit(solution)/shard_map/input_grad/pallas_call | solution.py:61
  397.2 5.1 fold_parts.1
  402.4 8.5 %collective-permute-done.29 = bf16[1152,256]{1,0:T(8,128)(2,1)S(1)} collective-permute-done((bf16[1152,256]{1,0:T(8,128)(2,1)}, bf16[1152,256]{1,0:T(8,128)(2,1)S(1)}, u32[]{:S(2)}, u32[]{:S(2)}) %collective-permute-start.29) | collective-permute-done | bytes 589856 | tf_op jit(solution)/shard_map/ppermute | solution.py:1349
  417.5 13.5 %unpack.2 = (f32[192,4,4096]{2,1,0:T(4,128)}, f32[512,4,768]{2,1,0:T(4,128)}) custom-call(s32[2]{0:T(128)} %pad_add_fusion.refs_0_, bf16[4,1152,256]{2,1,0:T(8,128)(2,1)} %copy-done.3, bf16[4,1152,256]{2,1,0:T(8,128)(2,1)} %copy-done.7, bf16[4,384,256]{2,1,0:T(8,128)(2,1)} %slice.44.refs_3_, bf16[4,384,256]{2,1,0:T(8,128)(2,1)} %slice.45.refs_4_), custom_call_target="tpu_custom_call" | custom-call | bytes 377487 | tf_op jit(solution)/shard_map/unpack/pallas_call | solution.py:61
  431.0 11.9 %collective-permute-done.33.refs_4_ = bf16[4,48,1664]{2,1,0:T(8,128)(2,1)} collective-permute-done((bf16[4,48,1664]{2,1,0:T(8,128)(2,1)}, bf16[4,48,1664]{2,1,0:T(8,128)(2,1)}, u32[]{:S(2)}, u32[]{:S(2)}) %collective-permute-start.33) | collective-permute-done | bytes 639008 | tf_op jit(solution)/shard_map/ppermute | solution.py:1349
  443.0 2.7 fold_quarters.1
  450.2 8.1 %collective-permute-done.35.refs_1_ = bf16[48,1664]{1,0:T(8,128)(2,1)S(1)} collective-permute-done((bf16[48,1664]{1,0:T(8,128)(2,1)}, bf16[48,1664]{1,0:T(8,128)(2,1)S(1)}, u32[]{:S(2)}, u32[]{:S(2)}) %collective-permute-start.35) | collective-permute-done | bytes 159776 | tf_op jit(solution)/shard_map/ppermute | solution.py:1355
  458.3 8.0 %layer_out.1 = bf16[1024,768]{1,0:T(8,128)(2,1)} custom-call(f32[1024,768]{1,0:T(8,128)} %get-tuple-element.125.refs_1_.refs_0_, f32[1024,128]{1,0:T(8,128)} %get-tuple-element.126.refs_4_.refs_1_, s32[1024,2]{1,0:T(8,128)} %bitcast_select_fusion.refs_10_.refs_5_.refs_2_, s32[1024,2]{1,0:T(8,128)} %copy-done.2, ...), custom_call_target="tpu_custom_call" | custom-call | flops 48318384 | bytes 157286 | tf_op jit(solution)/shard_map/layer_out/pallas_call | solution.py:61
  469.6 4.1 collective-permute-done.43
  478.1 3.5 collective-permute-done.38
  481.6 3.6 collective-permute-done.39
  485.9 2.0 lay_xor.5
  491.1 2.8 unpack_dense.1
  501.9 2.1 slice.47.refs_4_
  503.9 13.6 %unpack.3 = (f32[192,4,4096]{2,1,0:T(4,128)}, f32[512,4,768]{2,1,0:T(4,128)}) custom-call(s32[2]{0:T(128)} %pad_add_fusion.refs_0_, bf16[4,1152,256]{2,1,0:T(8,128)(2,1)} %copy-done.4, bf16[4,1152,256]{2,1,0:T(8,128)(2,1)} %collective-permute-done.45.refs_2_, bf16[4,384,256]{2,1,0:T(8,128)(2,1)} %slice.46.refs_3_, ...), custom_call_target="tpu_custom_call", output_to_operand_aliasing={{0}: (5, {}), {1}: (6, {})} | custom-call | bytes 377487 | tf_op jit(solution)/shard_map/unpack/pallas_call | solution.py:61
  (210 shorter events, 84.8 us)
Async XLA Ops:
  7.2 140.1 %all-gather.7.cloned.1.call-start = ((), (), s32[]{:S(2)}) async-start(), calls=%async_computation.5 | async-start | bytes 2949120 | tf_op jit(solution)/shard_map/all_gather | solution.py:1384
  15.2 27.6 %collective-permute-start = (bf16[64,1536]{1,0:T(8,128)(2,1)}, bf16[64,1536]{1,0:T(8,128)(2,1)S(1)}, u32[]{:S(2)}, u32[]{:S(2)}) collective-permute-start(bf16[64,1536]{1,0:T(8,128)(2,1)} %get-tuple-element.109.refs_1_), channel_id=1, source_target_pairs={{0,1},{1,2},{2,3},{3,0},{4,5},{5,6},{6,7},{7,4},{8,9},{9,10},{10,1... | collective-permute-start | bytes 589832 | tf_op jit(solution)/shard_map/ppermute | solution.py:1355
  18.3 24.6 %collective-permute-start.1 = (bf16[64,1536]{1,0:T(8,128)(2,1)}, bf16[64,1536]{1,0:T(8,128)(2,1)S(1)}, u32[]{:S(2)}, u32[]{:S(2)}) collective-permute-start(bf16[64,1536]{1,0:T(8,128)(2,1)} %get-tuple-element.109.refs_1_), channel_id=1, source_target_pairs={{0,2},{1,3},{2,0},{3,1},{4,6},{5,7},{6,4},{7,5},{8,10},{9,11},{10,... | collective-permute-start | bytes 589832 | tf_op jit(solution)/shard_map/ppermute | solution.py:1355
  20.8 22.0 %collective-permute-start.2 = (bf16[64,1536]{1,0:T(8,128)(2,1)}, bf16[64,1536]{1,0:T(8,128)(2,1)}, u32[]{:S(2)}, u32[]{:S(2)}) collective-permute-start(bf16[64,1536]{1,0:T(8,128)(2,1)} %get-tuple-element.109.refs_1_), channel_id=1, source_target_pairs={{0,3},{1,0},{2,1},{3,2},{4,7},{5,4},{6,5},{7,6},{8,11},{9,8},{10,9... | collective-permute-start | bytes 589832 | tf_op jit(solution)/shard_map/ppermute | solution.py:1355
  39.1 192.2 %all-gather.5.cloned.1.call-start = ((), (), s32[]{:S(2)}) async-start(), calls=%async_computation.4 | async-start | bytes 2949120 | tf_op jit(solution)/shard_map/all_gather | solution.py:1384
  45.7 13.4 %collective-permute-start.3 = (bf16[4,48,1152]{2,1,0:T(8,128)(2,1)}, bf16[4,48,1152]{2,1,0:T(8,128)(2,1)}, u32[]{:S(2)}, u32[]{:S(2)}) collective-permute-start(bf16[4,48,1152]{2,1,0:T(8,128)(2,1)} %get-tuple-element.113.refs_1_), channel_id=1, source_target_pairs={{0,8},{4,12},{8,0},{12,4},{16,24},{20,28},{24,16},{28,20},{1,9},{5... | collective-permute-start | bytes 1327112 | tf_op jit(solution)/shard_map/ppermute | solution.py:1349
  47.2 20.5 %collective-permute-start.4 = (bf16[4,48,1152]{2,1,0:T(8,128)(2,1)}, bf16[4,48,1152]{2,1,0:T(8,128)(2,1)}, u32[]{:S(2)}, u32[]{:S(2)}) collective-permute-start(bf16[4,48,1152]{2,1,0:T(8,128)(2,1)} %get-tuple-element.113.refs_1_), channel_id=1, source_target_pairs={{0,16},{4,20},{8,24},{12,28},{16,0},{20,4},{24,8},{28,12},{1,17},{... | collective-permute-start | bytes 1327112 | tf_op jit(solution)/shard_map/ppermute | solution.py:1349
  48.7 19.0 %collective-permute-start.5 = (bf16[4,48,1152]{2,1,0:T(8,128)(2,1)}, bf16[4,48,1152]{2,1,0:T(8,128)(2,1)}, u32[]{:S(2)}, u32[]{:S(2)}) collective-permute-start(bf16[4,48,1152]{2,1,0:T(8,128)(2,1)} %get-tuple-element.113.refs_1_), channel_id=1, source_target_pairs={{0,24},{4,28},{8,16},{12,20},{16,8},{20,12},{24,0},{28,4},{1,25},{... | collective-permute-start | bytes 1327112 | tf_op jit(solution)/shard_map/ppermute | solution.py:1349
  70.5 38.1 %collective-permute-start.6 = (bf16[768,1152]{1,0:T(8,128)(2,1)}, bf16[768,1152]{1,0:T(8,128)(2,1)S(1)}, u32[]{:S(2)}, u32[]{:S(2)}) collective-permute-start(bf16[768,1152]{1,0:T(8,128)(2,1)} %bitcast.47), channel_id=1, source_target_pairs={{0,4},{4,0},{8,12},{12,8},{16,20},{20,16},{24,28},{28,24},{1,5},{5... | collective-permute-start | bytes 5308424 | tf_op jit(solution)/shard_map/ppermute | solution.py:1352
  75.3 71.9 %collective-permute-start.10 = (bf16[384,768]{1,0:T(8,128)(2,1)}, bf16[384,768]{1,0:T(8,128)(2,1)S(1)}, u32[]{:S(2)}, u32[]{:S(2)}) collective-permute-start(bf16[384,768]{1,0:T(8,128)(2,1)} %get-tuple-element.120), channel_id=1, source_target_pairs={{0,8},{4,12},{8,0},{12,4},{16,24},{20,28},{24,16},{28,20},{1,9},{5... | collective-permute-start | bytes 1769480 | tf_op jit(solution)/shard_map/ppermute | solution.py:1349
  76.6 70.7 %collective-permute-start.11 = (bf16[384,768]{1,0:T(8,128)(2,1)}, bf16[384,768]{1,0:T(8,128)(2,1)S(1)}, u32[]{:S(2)}, u32[]{:S(2)}) collective-permute-start(bf16[384,768]{1,0:T(8,128)(2,1)} %get-tuple-element.121), channel_id=1, source_target_pairs={{0,16},{4,20},{8,24},{12,28},{16,0},{20,4},{24,8},{28,12},{1,17},{... | collective-permute-start | bytes 1769480 | tf_op jit(solution)/shard_map/ppermute | solution.py:1349
  77.4 69.9 %collective-permute-start.12 = (bf16[384,768]{1,0:T(8,128)(2,1)}, bf16[384,768]{1,0:T(8,128)(2,1)}, u32[]{:S(2)}, u32[]{:S(2)}) collective-permute-start(bf16[384,768]{1,0:T(8,128)(2,1)} %get-tuple-element.122), channel_id=1, source_target_pairs={{0,24},{4,28},{8,16},{12,20},{16,8},{20,12},{24,0},{28,4},{1,25},{... | collective-permute-start | bytes 1769480 | tf_op jit(solution)/shard_map/ppermute | solution.py:1349
  78.8 302.8 %reduce-scatter.3.cloned.1.call-start = ((), (), s32[]{:S(2)}) async-start(), calls=%async_computation.2 | async-start | bytes 2949120 | tf_op jit(solution)/shard_map/reduce_scatter | solution.py:1470
  81.0 26.1 %collective-permute-start.7 = (bf16[4,48,384]{2,1,0:T(8,128)(2,1)}, bf16[4,48,384]{2,1,0:T(8,128)(2,1)S(1)}, u32[]{:S(2)}, u32[]{:S(2)}) collective-permute-start(bf16[4,48,384]{2,1,0:T(8,128)(2,1)} %lay_proj.1.refs_8_.refs_1_), channel_id=1, source_target_pairs={{0,8},{4,12},{8,0},{12,4},{16,24},{20,28},{24,16},{28,20},{1,9},{5... | collective-permute-start | bytes 442376 | tf_op jit(solution)/shard_map/ppermute | solution.py:1349
  107.1 11.5 %collective-permute-start.8 = (bf16[4,48,384]{2,1,0:T(8,128)(2,1)}, bf16[4,48,384]{2,1,0:T(8,128)(2,1)S(1)}, u32[]{:S(2)}, u32[]{:S(2)}) collective-permute-start(bf16[4,48,384]{2,1,0:T(8,128)(2,1)} %lay_proj.1.refs_8_.refs_1_), channel_id=1, source_target_pairs={{0,16},{4,20},{8,24},{12,28},{16,0},{20,4},{24,8},{28,12},{1,17},{... | collective-permute-start | bytes 442376 | tf_op jit(solution)/shard_map/ppermute | solution.py:1349
  108.6 10.1 %collective-permute-start.9 = (bf16[4,48,384]{2,1,0:T(8,128)(2,1)}, bf16[4,48,384]{2,1,0:T(8,128)(2,1)S(1)}, u32[]{:S(2)}, u32[]{:S(2)}) collective-permute-start(bf16[4,48,384]{2,1,0:T(8,128)(2,1)} %lay_proj.1.refs_8_.refs_1_), channel_id=1, source_target_pairs={{0,24},{4,28},{8,16},{12,20},{16,8},{20,12},{24,0},{28,4},{1,25},{... | collective-permute-start | bytes 442376 | tf_op jit(solution)/shard_map/ppermute | solution.py:1349
  147.3 50.2 %collective-permute-start.18 = (bf16[4,1152,256]{2,1,0:T(8,128)(2,1)}, bf16[4,1152,256]{2,1,0:T(8,128)(2,1)S(1)}, u32[]{:S(2)}, u32[]{:S(2)}) collective-permute-start(bf16[4,1152,256]{2,1,0:T(8,128)(2,1)} %bitcast.63), channel_id=1, source_target_pairs={{0,4},{4,0},{8,12},{12,8},{16,20},{20,16},{24,28},{28,24},{1,5},{5... | collective-permute-start | bytes 7077896 | tf_op jit(solution)/shard_map/ppermute | solution.py:1352
  147.4 5.0 collective-permute-start.13
  167.5 16.9 %collective-permute-start.14 = (bf16[400,768]{1,0:T(8,128)(2,1)}, bf16[400,768]{1,0:T(8,128)(2,1)S(1)}, u32[]{:S(2)}, u32[]{:S(2)}) collective-permute-start(bf16[400,768]{1,0:T(8,128)(2,1)} %get-tuple-element.130), channel_id=1, source_target_pairs={{0,8},{4,12},{8,0},{12,4},{16,24},{20,28},{24,16},{28,20},{1,9},{5... | collective-permute-start | bytes 1843208 | tf_op jit(solution)/shard_map/ppermute | solution.py:1349
  168.3 29.2 %collective-permute-start.15 = (bf16[400,768]{1,0:T(8,128)(2,1)}, bf16[400,768]{1,0:T(8,128)(2,1)S(1)}, u32[]{:S(2)}, u32[]{:S(2)}) collective-permute-start(bf16[400,768]{1,0:T(8,128)(2,1)} %get-tuple-element.131), channel_id=1, source_target_pairs={{0,16},{4,20},{8,24},{12,28},{16,0},{20,4},{24,8},{28,12},{1,17},{... | collective-permute-start | bytes 1843208 | tf_op jit(solution)/shard_map/ppermute | solution.py:1349
  169.8 27.7 %collective-permute-start.16 = (bf16[400,768]{1,0:T(8,128)(2,1)}, bf16[400,768]{1,0:T(8,128)(2,1)S(1)}, u32[]{:S(2)}, u32[]{:S(2)}) collective-permute-start(bf16[400,768]{1,0:T(8,128)(2,1)} %get-tuple-element.132), channel_id=1, source_target_pairs={{0,24},{4,28},{8,16},{12,20},{16,8},{20,12},{24,0},{28,4},{1,25},{... | collective-permute-start | bytes 1843208 | tf_op jit(solution)/shard_map/ppermute | solution.py:1349
  231.2 7.2 %collective-permute-start.22 = (bf16[4,1152,256]{2,1,0:T(8,128)(2,1)}, bf16[4,1152,256]{2,1,0:T(8,128)(2,1)}, u32[]{:S(2)}, u32[]{:S(2)}) collective-permute-start(bf16[4,1152,256]{2,1,0:T(8,128)(2,1)} %get-tuple-element.147), channel_id=1, source_target_pairs={{0,4},{4,0},{8,12},{12,8},{16,20},{20,16},{24,28},{28,24},{1,5},{5... | collective-permute-start | bytes 7077896 | tf_op jit(solution)/shard_map/ppermute | solution.py:1352
  231.3 11.7 %collective-permute-start.17 = (bf16[4,1152,256]{2,1,0:T(8,128)(2,1)}, bf16[4,1152,256]{2,1,0:T(8,128)(2,1)S(1)}, u32[]{:S(2)}, u32[]{:S(2)}) collective-permute-start(bf16[4,1152,256]{2,1,0:T(8,128)(2,1)} %bitcast.60), channel_id=1, source_target_pairs={{0,4},{4,0},{8,12},{12,8},{16,20},{20,16},{24,28},{28,24},{1,5},{5... | collective-permute-start | bytes 7077896 | tf_op jit(solution)/shard_map/ppermute | solution.py:1352
  242.9 202.7 %reduce-scatter.5.cloned.1.call-start = ((), (), s32[]{:S(2)}) async-start(), calls=%async_computation.3 | async-start | bytes 2949120 | tf_op jit(solution)/shard_map/reduce_scatter | solution.py:1470
  281.0 4.8 collective-permute-start.23
  281.3 16.9 %collective-permute-start.19 = (bf16[400,768]{1,0:T(8,128)(2,1)}, bf16[400,768]{1,0:T(8,128)(2,1)S(1)}, u32[]{:S(2)}, u32[]{:S(2)}) collective-permute-start(bf16[400,768]{1,0:T(8,128)(2,1)} %get-tuple-element.143), channel_id=1, source_target_pairs={{0,8},{4,12},{8,0},{12,4},{16,24},{20,28},{24,16},{28,20},{1,9},{5... | collective-permute-start | bytes 1843208 | tf_op jit(solution)/shard_map/ppermute | solution.py:1349
  282.3 16.7 %collective-permute-start.20 = (bf16[400,768]{1,0:T(8,128)(2,1)}, bf16[400,768]{1,0:T(8,128)(2,1)}, u32[]{:S(2)}, u32[]{:S(2)}) collective-permute-start(bf16[400,768]{1,0:T(8,128)(2,1)} %get-tuple-element.144), channel_id=1, source_target_pairs={{0,16},{4,20},{8,24},{12,28},{16,0},{20,4},{24,8},{28,12},{1,17},{... | collective-permute-start | bytes 1843208 | tf_op jit(solution)/shard_map/ppermute | solution.py:1349
  283.2 28.6 %collective-permute-start.21 = (bf16[400,768]{1,0:T(8,128)(2,1)}, bf16[400,768]{1,0:T(8,128)(2,1)}, u32[]{:S(2)}, u32[]{:S(2)}) collective-permute-start(bf16[400,768]{1,0:T(8,128)(2,1)} %get-tuple-element.145), channel_id=1, source_target_pairs={{0,24},{4,28},{8,16},{12,20},{16,8},{20,12},{24,0},{28,4},{1,25},{... | collective-permute-start | bytes 1843208 | tf_op jit(solution)/shard_map/ppermute | solution.py:1349
  330.7 34.9 %collective-permute-start.24 = (bf16[384,768]{1,0:T(8,128)(2,1)}, bf16[384,768]{1,0:T(8,128)(2,1)S(1)}, u32[]{:S(2)}, u32[]{:S(2)}) collective-permute-start(bf16[384,768]{1,0:T(8,128)(2,1)} %get-tuple-element.152), channel_id=1, source_target_pairs={{0,8},{4,12},{8,0},{12,4},{16,24},{20,28},{24,16},{28,20},{1,9},{5... | collective-permute-start | bytes 1769480 | tf_op jit(solution)/shard_map/ppermute | solution.py:1349
  331.7 34.0 %collective-permute-start.25 = (bf16[384,768]{1,0:T(8,128)(2,1)}, bf16[384,768]{1,0:T(8,128)(2,1)S(1)}, u32[]{:S(2)}, u32[]{:S(2)}) collective-permute-start(bf16[384,768]{1,0:T(8,128)(2,1)} %get-tuple-element.153), channel_id=1, source_target_pairs={{0,16},{4,20},{8,24},{12,28},{16,0},{20,4},{24,8},{28,12},{1,17},{... | collective-permute-start | bytes 1769480 | tf_op jit(solution)/shard_map/ppermute | solution.py:1349
  333.1 32.5 %collective-permute-start.26 = (bf16[384,768]{1,0:T(8,128)(2,1)S(1)}, bf16[384,768]{1,0:T(8,128)(2,1)S(1)}, u32[]{:S(2)}, u32[]{:S(2)}) collective-permute-start(bf16[384,768]{1,0:T(8,128)(2,1)S(1)} %copy-done.42), channel_id=1, source_target_pairs={{0,24},{4,28},{8,16},{12,20},{16,8},{20,12},{24,0},{28,4},{1,25},{... | collective-permute-start | bytes 1769480 | tf_op jit(solution)/shard_map/ppermute | solution.py:1349
  381.6 14.3 %collective-permute-start.27 = (bf16[768,1536]{1,0:T(8,128)(2,1)}, bf16[768,1536]{1,0:T(8,128)(2,1)S(1)}, u32[]{:S(2)}, u32[]{:S(2)}) collective-permute-start(bf16[768,1536]{1,0:T(8,128)(2,1)} %broadcast_select_fusion), channel_id=1, source_target_pairs={{0,4},{4,0},{8,12},{12,8},{16,20},{20,16},{24,28},{28,24},{1,5},{5... | collective-permute-start | bytes 7077896 | tf_op jit(solution)/shard_map/ppermute | solution.py:1352
  381.6 20.7 %collective-permute-start.28 = (bf16[1152,256]{1,0:T(8,128)(2,1)}, bf16[1152,256]{1,0:T(8,128)(2,1)S(1)}, u32[]{:S(2)}, u32[]{:S(2)}) collective-permute-start(bf16[1152,256]{1,0:T(8,128)(2,1)} %bitcast.66), channel_id=1, source_target_pairs={{0,8},{4,12},{8,0},{12,4},{16,24},{20,28},{24,16},{28,20},{1,9},{5... | collective-permute-start | bytes 1769480 | tf_op jit(solution)/shard_map/ppermute | solution.py:1349
  382.5 28.3 %collective-permute-start.29 = (bf16[1152,256]{1,0:T(8,128)(2,1)}, bf16[1152,256]{1,0:T(8,128)(2,1)S(1)}, u32[]{:S(2)}, u32[]{:S(2)}) collective-permute-start(bf16[1152,256]{1,0:T(8,128)(2,1)} %bitcast.67), channel_id=1, source_target_pairs={{0,16},{4,20},{8,24},{12,28},{16,0},{20,4},{24,8},{28,12},{1,17},{... | collective-permute-start | bytes 1769480 | tf_op jit(solution)/shard_map/ppermute | solution.py:1349
  384.0 26.8 %collective-permute-start.30 = (bf16[1152,256]{1,0:T(8,128)(2,1)}, bf16[1152,256]{1,0:T(8,128)(2,1)S(1)}, u32[]{:S(2)}, u32[]{:S(2)}) collective-permute-start(bf16[1152,256]{1,0:T(8,128)(2,1)} %bitcast.68), channel_id=1, source_target_pairs={{0,24},{4,28},{8,16},{12,20},{16,8},{20,12},{24,0},{28,4},{1,25},{... | collective-permute-start | bytes 1769480 | tf_op jit(solution)/shard_map/ppermute | solution.py:1349
  411.3 19.7 %collective-permute-start.31 = (bf16[4,48,1664]{2,1,0:T(8,128)(2,1)}, bf16[4,48,1664]{2,1,0:T(8,128)(2,1)S(1)}, u32[]{:S(2)}, u32[]{:S(2)}) collective-permute-start(bf16[4,48,1664]{2,1,0:T(8,128)(2,1)} %get-tuple-element.175), channel_id=1, source_target_pairs={{0,8},{4,12},{8,0},{12,4},{16,24},{20,28},{24,16},{28,20},{1,9},{5... | collective-permute-start | bytes 1916936 | tf_op jit(solution)/shard_map/ppermute | solution.py:1349
  412.5 18.5 %collective-permute-start.32 = (bf16[4,48,1664]{2,1,0:T(8,128)(2,1)}, bf16[4,48,1664]{2,1,0:T(8,128)(2,1)S(1)}, u32[]{:S(2)}, u32[]{:S(2)}) collective-permute-start(bf16[4,48,1664]{2,1,0:T(8,128)(2,1)} %get-tuple-element.176), channel_id=1, source_target_pairs={{0,16},{4,20},{8,24},{12,28},{16,0},{20,4},{24,8},{28,12},{1,17},{... | collective-permute-start | bytes 1916936 | tf_op jit(solution)/shard_map/ppermute | solution.py:1349
  413.3 29.6 %collective-permute-start.33 = (bf16[4,48,1664]{2,1,0:T(8,128)(2,1)}, bf16[4,48,1664]{2,1,0:T(8,128)(2,1)}, u32[]{:S(2)}, u32[]{:S(2)}) collective-permute-start(bf16[4,48,1664]{2,1,0:T(8,128)(2,1)} %get-tuple-element.177), channel_id=1, source_target_pairs={{0,24},{4,28},{8,16},{12,20},{16,8},{20,12},{24,0},{28,4},{1,25},{... | collective-permute-start | bytes 1916936 | tf_op jit(solution)/shard_map/ppermute | solution.py:1349
  445.6 23.9 %collective-permute-start.42 = (bf16[1152,256]{1,0:T(8,128)(2,1)}, bf16[1152,256]{1,0:T(8,128)(2,1)S(1)}, u32[]{:S(2)}, u32[]{:S(2)}) collective-permute-start(bf16[1152,256]{1,0:T(8,128)(2,1)} %bitcast.69), channel_id=1, source_target_pairs={{0,8},{4,12},{8,0},{12,4},{16,24},{20,28},{24,16},{28,20},{1,9},{5... | collective-permute-start | bytes 1769480 | tf_op jit(solution)/shard_map/ppermute | solution.py:1349
  447.2 26.5 %collective-permute-start.43 = (bf16[1152,256]{1,0:T(8,128)(2,1)}, bf16[1152,256]{1,0:T(8,128)(2,1)S(1)}, u32[]{:S(2)}, u32[]{:S(2)}) collective-permute-start(bf16[1152,256]{1,0:T(8,128)(2,1)} %bitcast.70), channel_id=1, source_target_pairs={{0,16},{4,20},{8,24},{12,28},{16,0},{20,4},{24,8},{28,12},{1,17},{... | collective-permute-start | bytes 1769480 | tf_op jit(solution)/shard_map/ppermute | solution.py:1349
  448.7 25.0 %collective-permute-start.44 = (bf16[1152,256]{1,0:T(8,128)(2,1)}, bf16[1152,256]{1,0:T(8,128)(2,1)S(1)}, u32[]{:S(2)}, u32[]{:S(2)}) collective-permute-start(bf16[1152,256]{1,0:T(8,128)(2,1)} %bitcast.71), channel_id=1, source_target_pairs={{0,24},{4,28},{8,16},{12,20},{16,8},{20,12},{24,0},{28,4},{1,25},{... | collective-permute-start | bytes 1769480 | tf_op jit(solution)/shard_map/ppermute | solution.py:1349
  449.2 9.2 %collective-permute-start.35 = (bf16[48,1664]{1,0:T(8,128)(2,1)}, bf16[48,1664]{1,0:T(8,128)(2,1)S(1)}, u32[]{:S(2)}, u32[]{:S(2)}) collective-permute-start(bf16[48,1664]{1,0:T(8,128)(2,1)} %get-tuple-element.185), channel_id=1, source_target_pairs={{0,1},{1,2},{2,3},{3,0},{4,5},{5,6},{6,7},{7,4},{8,9},{9,10},{10,1... | collective-permute-start | bytes 479240 | tf_op jit(solution)/shard_map/ppermute | solution.py:1355
  449.9 16.5 %collective-permute-start.36 = (bf16[48,1664]{1,0:T(8,128)(2,1)}, bf16[48,1664]{1,0:T(8,128)(2,1)S(1)}, u32[]{:S(2)}, u32[]{:S(2)}) collective-permute-start(bf16[48,1664]{1,0:T(8,128)(2,1)} %get-tuple-element.186), channel_id=1, source_target_pairs={{0,2},{1,3},{2,0},{3,1},{4,6},{5,7},{6,4},{7,5},{8,10},{9,11},{10,... | collective-permute-start | bytes 479240 | tf_op jit(solution)/shard_map/ppermute | solution.py:1355
  458.3 8.0 %collective-permute-start.37 = (bf16[48,1664]{1,0:T(8,128)(2,1)}, bf16[48,1664]{1,0:T(8,128)(2,1)S(1)}, u32[]{:S(2)}, u32[]{:S(2)}) collective-permute-start(bf16[48,1664]{1,0:T(8,128)(2,1)} %get-tuple-element.187), channel_id=1, source_target_pairs={{0,3},{1,0},{2,1},{3,2},{4,7},{5,4},{6,5},{7,6},{8,11},{9,8},{10,9... | collective-permute-start | bytes 479240 | tf_op jit(solution)/shard_map/ppermute | solution.py:1355
  474.0 27.8 %collective-permute-start.45 = (bf16[4,1152,256]{2,1,0:T(8,128)(2,1)S(1)}, bf16[4,1152,256]{2,1,0:T(8,128)(2,1)}, u32[]{:S(2)}, u32[]{:S(2)}) collective-permute-start(bf16[4,1152,256]{2,1,0:T(8,128)(2,1)S(1)} %pad_maximum_fusion.1.refs_1_), channel_id=1, source_target_pairs={{0,4},{4,0},{8,12},{12,8},{16,20},{20,16},{24,28},{28,24},{1,5},{5... | collective-permute-start | bytes 7077896 | tf_op jit(solution)/shard_map/ppermute | solution.py:1352
  474.6 7.0 %collective-permute-start.38 = (bf16[48,1664]{1,0:T(8,128)(2,1)S(1)}, bf16[48,1664]{1,0:T(8,128)(2,1)S(1)}, u32[]{:S(2)}, u32[]{:S(2)}) collective-permute-start(bf16[48,1664]{1,0:T(8,128)(2,1)S(1)} %copy-done.20), channel_id=1, source_target_pairs={{0,8},{4,12},{8,0},{12,4},{16,24},{20,28},{24,16},{28,20},{1,9},{5... | collective-permute-start | bytes 479240 | tf_op jit(solution)/shard_map/ppermute | solution.py:1349
  476.1 9.1 %collective-permute-start.39 = (bf16[48,1664]{1,0:T(8,128)(2,1)S(1)}, bf16[48,1664]{1,0:T(8,128)(2,1)S(1)}, u32[]{:S(2)}, u32[]{:S(2)}) collective-permute-start(bf16[48,1664]{1,0:T(8,128)(2,1)S(1)} %copy-done.20), channel_id=1, source_target_pairs={{0,16},{4,20},{8,24},{12,28},{16,0},{20,4},{24,8},{28,12},{1,17},{... | collective-permute-start | bytes 479240 | tf_op jit(solution)/shard_map/ppermute | solution.py:1349
  476.7 8.6 %collective-permute-start.40 = (bf16[48,1664]{1,0:T(8,128)(2,1)S(1)}, bf16[48,1664]{1,0:T(8,128)(2,1)S(1)}, u32[]{:S(2)}, u32[]{:S(2)}) collective-permute-start(bf16[48,1664]{1,0:T(8,128)(2,1)S(1)} %copy-done.20), channel_id=1, source_target_pairs={{0,24},{4,28},{8,16},{12,20},{16,8},{20,12},{24,0},{28,4},{1,25},{... | collective-permute-start | bytes 479240 | tf_op jit(solution)/shard_map/ppermute | solution.py:1349
  (45 other events, 348.8 us)
Sparse Core Ops, SparseCore 0:
  39.2 48.8 all-gather.6
  89.6 49.2 all-gather.4
  243.1 45.4 reduce-scatter.2
  381.7 45.8 reduce-scatter.4
where the time goes:
time: 532 us; the launch traced here: 525 us
  Pallas kernels  268 us (50%)
  waiting for transfers between devices  137 us (26%)
  local copies, waits for them, and re-layouts  46.7 us (9%)
  starting transfers between devices  45.7 us (9%)
  between operations  16.9 us (3%)
  other arithmetic  9.9 us (2%)
    pallas_call x24, Pallas kernels, launch(): pl.pallas_call(run, in_specs=list(in_specs) + [pl.BlockSpec(memory_space=...  197 us
    ppermute x30, waiting for transfers between devices, to_expert(): lax.ppermute(a, 'rep', [(i, i ^ k * copies) for i in range(replicas)])  116 us
    pallas_call x2, Pallas kernels, expert_call(): pl.pallas_call(partial(expert_kernel, plan, first, last), in_specs=in_spe...  68.6 us
    ppermute x30, starting transfers between devices, to_expert(): lax.ppermute(a, 'rep', [(i, i ^ k * copies) for i in range(replicas)])  35.6 us
    unnamed x92, local copies, waits for them, and re-layouts  19.3 us
    ppermute x10, waiting for transfers between devices, to_part(): return lax.ppermute(a, 'rep', [(i, i ^ m) for i in range(replicas)])  12.4 us
  transfers between devices with their start and end apart: 50, of which 18 were waited for; matrix products, arithmetic and copies ran while one was open for 7% of the time, Pallas kernels for 48%

commit v1 on v0

--- a/solution.py
+++ b/solution.py
@@ -357,10 +357,11 @@
 
 def lay_shards_kernel(count, shard, quarter, width, zi_ref, *refs):
     pieces = refs[:count]
-    qkv_ref, small_ref, prev_ref = refs[count:]
+    qkv_ref, proj_ref, small_ref, prev_ref = refs[count:]
     for k in range(count):
         at = lax.rem(zi_ref[0] + count - k, count)
         qkv_ref[at] = pieces[k][:quarter, :width]
+        proj_ref[at] = pieces[k][:quarter, width:]
         prev_ref[at] = pieces[k][quarter:, 2 * LANES : 3 * LANES]
     small_ref[16:, :] = jnp.zeros((LANES - 16, D), bf16)
     for z in range(count):
@@ -377,35 +378,15 @@
         partial(lay_shards_kernel, count, shard, quarter, width),
         [zi, *pieces],
         [SMEM] + [VM] * count,
-        [VM] * 3,
+        [VM] * 4,
         [
             jax.ShapeDtypeStruct((count, quarter, width), bf16),
+            jax.ShapeDtypeStruct((count, quarter, pieces[0].shape[1] - width), bf16),
             jax.ShapeDtypeStruct((LANES, D), bf16),
             jax.ShapeDtypeStruct((count, 16, LANES), bf16),
         ],
         after,
         name="lay_shards",
-    )
-
-
-def lay_proj_kernel(count, quarter, width, zi_ref, *refs):
-    pieces, out = refs[:count], refs[count]
-    for k in range(count):
-        at = lax.rem(zi_ref[0] + count - k, count)
-        out[at] = pieces[k][:quarter, width:]
-
-
-def lay_proj(zi, pieces, quarter, width, after):
-    count = len(pieces)
-    rest = pieces[0].shape[1] - width
-    return launch(
-        partial(lay_proj_kernel, count, quarter, width),
-        [zi, *pieces],
-        [SMEM] + [VM] * count,
-        VM,
-        jax.ShapeDtypeStruct((count, quarter, rest), bf16),
-        after,
-        name="lay_proj",
     )
 
 
@@ -426,6 +407,29 @@
         jax.ShapeDtypeStruct((first, count, rows, columns), bf16),
         after,
         name="lay_xor",
+    )
+
+
+def lay_riders_kernel(shape, own_ref, *refs):
+    pieces, out = refs[:-1], refs[-1]
+    shards, quarter, width = shape
+    per = D // width
+    for k, piece in enumerate(pieces):
+        for z in range(shards):
+            row, column = z // per * quarter, z % per * width
+            out[z, own_ref[0] ^ k] = piece[CAP + row : CAP + row + quarter, column : column + width]
+
+
+def lay_riders(own, blocks, shape, after):
+    shards, quarter, width = shape
+    return launch(
+        partial(lay_riders_kernel, shape),
+        [own, *blocks],
+        [SMEM] + [VM] * len(blocks),
+        VM,
+        jax.ShapeDtypeStruct((shards, len(blocks), quarter, width), bf16),
+        after,
+        name="lay_riders",
     )
 
 
@@ -508,6 +512,8 @@
 def dispatch_kernel(gated, mine_ref, spot_ref, v_ref, *refs):
     if gated:
         gate_ref, refs = refs[0], refs[1:]
+    else:
+        rider, refs = refs[0], refs[1:]
     rows = v_ref.shape[0]
     slot = lax.broadcasted_iota(jnp.int32, (CAP, rows), 0)
     for k in range(EXPERTS):
@@ -524,11 +530,13 @@
             ).astype(bf16)
             refs[k][CAP:, :CAP] = tail
             refs[k][CAP:, CAP:] = jnp.zeros((EXTRA, D - CAP), bf16)
-
-
-def dispatch_call(mine, spot, values, gates=None, after=()):
-    size = CAP + (0 if gates is None else EXTRA)
-    operands = [mine, spot, values] + ([] if gates is None else [gates])
+        else:
+            refs[k][CAP:, :] = rider[...]
+
+
+def dispatch_call(mine, spot, values, gates=None, rider=None, after=()):
+    size = CAP + (EXTRA if rider is None else rider.shape[0])
+    operands = [mine, spot, values] + [rider if gates is None else gates]
     rows = values.shape[0]
     return launch(
         partial(dispatch_kernel, gates is not None),
@@ -758,7 +766,7 @@
         extra = x_refs[k][CAP:, :CAP].astype(f32)
         gate = (extra[0:1] + extra[1:2]).T
         gcol[span, :] = jnp.broadcast_to(gate, (CAP, LANES))
-        ds[span, :] = (y_refs[k][...].astype(f32) * gate).astype(bf16)
+        ds[span, :] = (y_refs[k][:CAP, :].astype(f32) * gate).astype(bf16)
     if first:
         ret_acc[...] = jnp.zeros_like(ret_acc)
         dx_acc[...] = jnp.zeros_like(dx_acc)
@@ -809,7 +817,7 @@
             for k in range(EXPERTS):
                 span = slice(k * CAP, (k + 1) * CAP)
                 ret = ret_acc[span, :]
-                dgate = jnp.sum(ret * y_refs[k][...].astype(f32), axis=-1, keepdims=True)
+                dgate = jnp.sum(ret * y_refs[k][:CAP, :].astype(f32), axis=-1, keepdims=True)
                 dgate = jnp.broadcast_to(dgate, (CAP, LANES)).T[:1]
                 ret_outs[k][...] = (ret * gcol[span, :1]).astype(bf16)
                 dx_outs[k][:CAP, :] = dx_acc[span, :].astype(bf16)
@@ -1077,7 +1085,7 @@
     )
 
 
-def dense_kernel(copies, h_ref, ctx_ref, dq_ref, dk_ref, dv_ref, branch_ref, *outs):
+def dense_kernel(copies, part_ref, h_ref, ctx_ref, dq_ref, dk_ref, dv_ref, branch_ref, *outs):
     cut = 4 * D // copies
     ht = h_ref[...].astype(f32).T.astype(bf16)
     ct = ctx_ref[...].astype(f32).T.astype(bf16)
@@ -1092,16 +1100,21 @@
             while done < step:
                 owner, column = (at + done) // cut, (at + done) % cut
                 size = min(step - done, cut - column)
-                outs[owner][:, column : column + size] = made[:, done : done + size]
+                for m in range(copies):
+
+                    @pl.when(part_ref[0] == (owner ^ m))
+                    def _(m=m, column=column, size=size, piece=made[:, done : done + size]):
+                        outs[m][:, column : column + size] = piece
+
                 done += size
 
 
-def dense_call(copies, h, ctx, dq, dk, dv, branch, after):
+def dense_call(copies, part, h, ctx, dq, dk, dv, branch, after):
     rows = h.shape[0]
     return launch(
         partial(dense_kernel, copies),
-        [h, ctx, dq, dk, dv, branch],
-        [VM] * 6,
+        [part, h, ctx, dq, dk, dv, branch],
+        [SMEM] + [VM] * 6,
         [VM] * copies,
         [jax.ShapeDtypeStruct((D, 4 * D // copies), bf16)] * copies,
         after,
@@ -1110,71 +1123,94 @@
     )
 
 
-def fold_parts_kernel(copies, who_ref, *refs):
-    dense, got = refs[:copies], refs[copies : 2 * copies - 1]
-    small, outs = refs[2 * copies - 1], refs[2 * copies :]
-    cut = dense[0].shape[-1]
+def fold_parts_kernel(who_ref, *refs):
+    pieces, outs = refs[:-EXPERTS], refs[-EXPERTS:]
     for k in range(EXPERTS):
         at = who_ref[0] ^ k
-        own = dense[0][:, at].astype(f32)
-        for p in range(1, copies):
-            own = jnp.where(who_ref[1] == p, dense[p][:, at].astype(f32), own)
-        for piece in got:
-            own = own + piece[:, at].astype(f32)
-        outs[k][:, :, :cut] = own.astype(bf16)
-        outs[k][:, :, cut:] = small[:, at]
-
-
-def fold_parts(who, dense, got, small, shards):
-    copies = len(dense)
-    cut = dense[0].shape[1]
+        total = pieces[0][:, at].astype(f32)
+        for piece in pieces[1:]:
+            total = total + piece[:, at].astype(f32)
+        outs[k][...] = total.astype(bf16)
+
+
+def fold_parts(who, pieces, shards):
+    cut = pieces[0].shape[1]
     quarter = D // (shards * EXPERTS)
     shape = (shards, EXPERTS, quarter, cut)
-    operands = [who] + [a.reshape(shape) for a in (*dense, *got)]
-    operands.append(small.reshape(shards, EXPERTS, quarter, LANES))
-    return launch(
-        partial(fold_parts_kernel, copies),
+    operands = [who] + [a.reshape(shape) for a in pieces]
+    return launch(
+        fold_parts_kernel,
         operands,
-        [SMEM] + [VM] * (len(operands) - 1),
+        [SMEM] + [VM] * len(pieces),
         [VM] * EXPERTS,
-        [jax.ShapeDtypeStruct((shards, quarter, cut + LANES), bf16)] * EXPERTS,
+        [jax.ShapeDtypeStruct((shards, quarter, cut), bf16)] * EXPERTS,
         name="fold_parts",
     )
 
 
-def fold_quarters_kernel(count, zi_ref, *refs):
+def fold_quarters_kernel(count, zi_ref, small_ref, *refs):
     pieces, outs = refs[:count], refs[count:]
+    rows, cut = pieces[0].shape[1:]
+    spare = outs[0].shape[0] - rows
     for k, out in enumerate(outs):
         at = lax.rem(zi_ref[0] + k, len(outs))
         total = pieces[0][at].astype(f32)
         for piece in pieces[1:]:
             total = total + piece[at].astype(f32)
-        out[...] = total.astype(bf16)
-
-
-def fold_quarters(zi, pieces, after=()):
-    shards, rows, columns = pieces[0].shape
+        out[:rows, :] = total.astype(bf16)
+        for c in range(cut // LANES):
+            out[rows:, c * LANES : (c + 1) * LANES] = small_ref[at, c * spare : (c + 1) * spare, :]
+
+
+def fold_quarters(zi, small, pieces, after=()):
+    shards, rows, cut = pieces[0].shape
+    spare = D // shards * LANES // cut
     return launch(
         partial(fold_quarters_kernel, len(pieces)),
-        [zi, *pieces],
-        [SMEM] + [VM] * len(pieces),
+        [zi, small.reshape(shards, D // shards, LANES), *pieces],
+        [SMEM] + [VM] * (len(pieces) + 1),
         [VM] * shards,
-        [jax.ShapeDtypeStruct((rows, columns), bf16)] * shards,
+        [jax.ShapeDtypeStruct((rows + spare, cut), bf16)] * shards,
         after,
         name="fold_quarters",
     )
 
 
+def lay_tail_kernel(count, rows, own_ref, *refs):
+    pieces, out = refs[:count], refs[count]
+    total = pieces[0][rows:, :].astype(f32)
+    for k in range(count):
+        at = pl.multiple_of((own_ref[0] ^ k) * rows, rows)
+        out[pl.ds(at, rows), :] = pieces[k][:rows, :]
+        if k:
+            total = total + pieces[k][rows:, :].astype(f32)
+    out[count * rows :, :] = total.astype(bf16)
+
+
+def lay_tail(own, pieces, rows, after):
+    count = len(pieces)
+    size, cut = pieces[0].shape
+    return launch(
+        partial(lay_tail_kernel, count, rows),
+        [own, *pieces],
+        [SMEM] + [VM] * count,
+        VM,
+        jax.ShapeDtypeStruct((count * rows + size - rows, cut), bf16),
+        after,
+        name="lay_tail",
+    )
+
+
 def fold_copies(pieces):
-    shape = pieces[0].shape
-    block = pl.BlockSpec((1,) + shape[1:], lambda i: (i, 0, 0))
+    shards, rows, wide = pieces[0].shape
+    block = pl.BlockSpec((1, rows // 2, wide), lambda i: (i // 2, i % 2, 0))
     return launch(
         fold_shards_kernel,
         pieces,
         [block] * len(pieces),
         block,
-        jax.ShapeDtypeStruct(shape, bf16),
-        grid=(shape[0],),
+        jax.ShapeDtypeStruct(pieces[0].shape, bf16),
+        grid=(2 * shards,),
         compiler_params=params(),
         cost_estimate=cost(0, 0),
         name="fold_copies",
@@ -1199,17 +1235,19 @@
     )
 
 
-def unpack_dense_kernel(count, part_ref, *refs):
+def unpack_dense_kernel(count, rows, part_ref, *refs):
     pieces, (qkv_ref, proj_ref, small_ref) = refs[:count], refs[count:]
-    cut = pieces[0].shape[1] - LANES
-    small = pieces[0][:, cut:].astype(f32)
+    cut = pieces[0].shape[1]
+    small = pieces[0][rows:, :].astype(f32)
     for piece in pieces[1:]:
-        small = small + piece[:, cut:].astype(f32)
-    small_ref[...] = small
+        small = small + piece[rows:, :].astype(f32)
+    spare = small.shape[0]
+    for c in range(cut // LANES):
+        small_ref[c * spare : (c + 1) * spare, :] = small[:, c * LANES : (c + 1) * LANES]
     for p in range(count):
-        chosen = pieces[0][:, :cut].astype(f32)
+        chosen = pieces[0][:rows, :].astype(f32)
         for m in range(1, count):
-            chosen = jnp.where(part_ref[0] == (p ^ m), pieces[m][:, :cut].astype(f32), chosen)
+            chosen = jnp.where(part_ref[0] == (p ^ m), pieces[m][:rows, :].astype(f32), chosen)
         start = p * cut
         in_qkv = max(0, min(cut, 3 * D - start))
         if in_qkv:
@@ -1219,10 +1257,9 @@
             proj_ref[:, at : at + cut - in_qkv] = chosen[:, in_qkv:]
 
 
-def unpack_dense(part, pieces):
-    rows = pieces[0].shape[0]
-    return launch(
-        partial(unpack_dense_kernel, len(pieces)),
+def unpack_dense(part, pieces, rows):
+    return launch(
+        partial(unpack_dense_kernel, len(pieces), rows),
         [part, *pieces],
         [SMEM] + [VM] * len(pieces),
         [VM] * 3,
@@ -1412,7 +1449,7 @@
     places = jnp.sum(jnp.where(hit, (kinds[:, None] * CAP + rank)[None], 0), axis=1)
     places = jnp.where(chosen < EXPERTS, places, -1).T
 
-    qkv_part, small, prevs = lay_shards(
+    qkv_part, proj_part, small, prevs = lay_shards(
         zi_s, spun, shard, quarter, width, (packs[0],)
     )
     pmix = prevs[:, :owned].reshape(NCH, LANES)
@@ -1432,19 +1469,19 @@
     )
     qkv_pieces = over_parts(qkv_half)
     part_q = part_s if len(qkv_pieces) == copies else jnp.zeros_like(part_s)
-    ys = dispatch_call(mine_s, spot, out_grad, after=(qkv_half,))
-    proj_part = lay_proj(zi_s, spun, quarter, width, (ys[0],))
+    per = D // proj_part.shape[2]
+    rider = proj_part.reshape(-1, per, quarter, D // per).transpose(0, 2, 1, 3)
+    rider = rider.reshape(-1, D)
+    rider = jnp.pad(rider, ((0, -rider.shape[0] % 16), (0, 0)))
+    ys = dispatch_call(mine_s, spot, out_grad, rider=rider, after=(qkv_half,))
 
     prev = prev_logits.T
-    h1, q, k, v = qkv_call(
-        part_q, tokens, small, cosine, sine, qkv_pieces, (ys[0], proj_part)
-    )
-    proj_half = lay_xor(mine_s, exchanged([proj_part] * EXPERTS), (h1,))
+    h1, q, k, v = qkv_call(part_q, tokens, small, cosine, sine, qkv_pieces, (ys[0],))
+    ys = exchanged(ys)
+    ctx, lse = attend_call(q, k, v, dcol, drow, vcol, ())
+    proj_half = lay_riders(mine_s, ys, proj_part.shape, (ctx,))
     proj_pieces = over_parts(proj_half)
     part_p = part_s if len(proj_pieces) == copies else jnp.zeros_like(part_s)
-    ctx, lse = attend_call(q, k, v, dcol, drow, vcol, (proj_half,))
-    ys = exchanged(ys)
-    ctx = tie(ctx, ys)
     res, h2, one, gates = after_call(
         part_p, ctx, tokens, small, prev, pmix, routes, proj_pieces
     )
@@ -1458,16 +1495,23 @@
     chunk_grads = []
     for chunk in range(plan.chunks):
         grads, carried = expert_call(
-            plan, xs, ys, weights[chunk], carried, chunk == plan.chunks - 1
+            plan,
+            xs,
+            ys,
+            weights[chunk] if chunk else tie(weights[0], weights[1:]),
+            carried,
+            chunk == plan.chunks - 1,
         )
         chunk_grads.append(grads)
     dx = exchanged(carried[:EXPERTS])
 
-    totals = [
-        fold_copies([grads[0]] + [to_part(grads[m], m) for m in range(1, copies)])
-        for grads in chunk_grads
+    chunk_grads = [
+        [grads[0]] + [to_part(grads[m], m) for m in range(1, copies)] for grads in chunk_grads
     ]
-    summed = [lax.psum_scatter(t, "fsdp", scatter_dimension=0, tiled=False) for t in totals]
+    total = fold_copies(chunk_grads[0])
+
+    def over_shards(t):
+        return lax.psum_scatter(t, "fsdp", scatter_dimension=0, tiled=False)
 
     who_p = jnp.concatenate([mine_s, part_p])
     dres, branch, dctx, dsmall, gain_f_grad, prev_grad, cvec_grad = back_call(
@@ -1482,19 +1526,27 @@
         small,
         dx,
         proj_pieces,
-        totals,
-    )
+        (total,),
+    )
+    summed = [over_shards(total)]
+    summed += [over_shards(fold_copies(tie(grads, branch))) for grads in chunk_grads[1:]]
     ret = exchanged(tie(carried[EXPERTS:], branch))
+    first = tie(summed[0], branch)
+    spread = [[first] + [to_expert(first, k) for k in range(1, EXPERTS - 1)]]
     dq, dk, dv = attend_back_call(q, k, v, dctx, lse, dcol, drow, vcol, cosine, sine, ())
-    spread = [exchanged([tie(summed[0], dq)] * EXPERTS)]
-    dense = dense_call(copies, h1, ctx, tie(dq, ret), dk, dv, branch, ())
-
-    def columns(index):
-        if copies == 2:
-            return jnp.where(index == 0, dense[0], dense[1])
-        return lax.dynamic_index_in_dim(jnp.stack(dense), index, 0, keepdims=False)
-
-    got = [to_part(columns(part ^ m), m) for m in range(1, copies)]
+    dense = dense_call(
+        copies, part_s, h1, ctx, tie(dq, ret, spread[0]), dk, dv, branch, ()
+    )
+    spread[0].append(to_expert(tie(first, dq), EXPERTS - 1))
+    dense = tie(list(dense), summed[1:])
+    dense = [dense[0]] + [to_part(dense[m], m) for m in range(1, copies)]
+    quarters = tie(fold_parts(who, dense, shards), spread[0])
+
+    def over_copies(pieces):
+        stacked = jnp.stack(pieces)
+        return [stacked] + [to_part(stacked, m) for m in range(1, copies)]
+
+    spread[0] = over_copies(tie(spread[0], quarters))
     input_grad, smalls = last_call(
         part_q,
         shards,
@@ -1502,34 +1554,26 @@
         dk,
         dv,
         tokens,
-        dres,
+        tie(dres, quarters),
         small,
         (dsmall, gain_f_grad, prev_grad, cvec_grad),
         qkv_pieces,
-        (dense[0],),
-    )
-    quarters = fold_parts(who, dense, got, smalls, shards)
-    quarters = tie(quarters, spread[0])
-
-    def over_copies(pieces):
-        stacked = jnp.stack(pieces)
-        return [stacked] + [to_part(stacked, m) for m in range(1, copies)]
-
-    spread[0] = over_copies(tie(spread[0], quarters))
+        (),
+    )
     begun = ()
     if plan.seg % LANES == 0:
         begun = unpack_chunk(plan, who, 0, spread[0], begun)
-    bands = fold_quarters(zi_s, exchanged(quarters), begun)
-    spread += [exchanged([tie(piece, bands)] * EXPERTS) for piece in summed[1:]]
-    out = finish_call(res, one, places, routes, small, tie(ret, bands), ())
-    tail = fold_shards(
-        [bands[0]] + tie([spin(bands[k], k) for k in range(1, shards)], out)
-    )
+    out = finish_call(res, one, places, routes, small, tie(ret, quarters), ())
+    bands = fold_quarters(zi_s, smalls, exchanged(quarters), (*begun, out))
+    tail = fold_shards([bands[0]] + [spin(bands[k], k) for k in range(1, shards)])
+    for piece in summed[1:]:
+        piece = tie(piece, bands)
+        late = [to_expert(tie(piece, tail), k) for k in range(EXPERTS - 1, EXPERTS)]
+        spread.append([piece] + [to_expert(piece, k) for k in range(1, EXPERTS - 1)] + late)
+    tail = lay_tail(mine_s, exchanged([tail] * EXPERTS), quarter, ())
     spread[1:] = [over_copies(tie(pieces, tail)) for pieces in spread[1:]]
-    tail = lay_xor(mine_s, [t[None] for t in exchanged([tail] * EXPERTS)])
-    tail = tail.reshape(shard, tail.shape[3])
     tails = [tail] + [to_part(tail, m) for m in range(1, copies)]
-    qkv_grad, proj_grad, small_grad = unpack_dense(part_s, tails)
+    qkv_grad, proj_grad, small_grad = unpack_dense(part_s, tails, shard)
 
     full_in, full_out = unpack_grads(plan, who, spread, begun)
     return (

time: 532 us -> 552 us (1.038)
  starting transfers between devices: 45.7 us -> 55.6 us
    ppermute x30 -> x27, waiting for transfers between devices: 116 us -> 93.8 us  [to_expert(): lax.ppermute(a, 'rep', [(i, i ^ k * copies) for i in range(replicas)])]
    ppermute x6, waiting for transfers between devices: 8.09 us -> 24.8 us  [spin(): lax.ppermute(a, 'fsdp', [(i, (i + k) % shards) for i in range(shards)])]
    ppermute x6, starting transfers between devices: 8.09 us -> 21.5 us  [spin(): lax.ppermute(a, 'fsdp', [(i, (i + k) % shards) for i in range(shards)])]
    pallas_call x24 -> x23, Pallas kernels: 197 us -> 201 us  [launch(): pl.pallas_call(run, in_specs=list(in_specs) + [pl.BlockSpec(memory_space=...]
    unnamed x92 -> x103, local copies, waits for them, and re-layouts: 19.3 us -> 23.6 us
    ppermute x30 -> x27, starting transfers between devices: 35.6 us -> 32.8 us  [to_expert(): lax.ppermute(a, 'rep', [(i, i ^ k * copies) for i in range(replicas)])]
  transfers between devices with their start and end apart: 50 -> 47, of which waited for: 18 -> 26; matrix products, arithmetic and copies ran while one was open for 7% -> 4% of each run, Pallas kernels for 48% -> 39%
where the time goes in v1:
time: 552 us; the launch traced here: 542 us
  Pallas kernels  272 us (49%)
  waiting for transfers between devices  139 us (25%)
  starting transfers between devices  55.6 us (10%)
  local copies, waits for them, and re-layouts  51.2 us (9%)
  between operations  16.7 us (3%)
  other arithmetic  6.56 us (1%)
    pallas_call x23, Pallas kernels, launch(): pl.pallas_call(run, in_specs=list(in_specs) + [pl.BlockSpec(memory_space=...  201 us
    ppermute x27, waiting for transfers between devices, to_expert(): lax.ppermute(a, 'rep', [(i, i ^ k * copies) for i in range(replicas)])  93.8 us
    pallas_call x2, Pallas kernels, expert_call(): pl.pallas_call(partial(expert_kernel, plan, first, last), in_specs=in_spe...  68.3 us
    ppermute x27, starting transfers between devices, to_expert(): lax.ppermute(a, 'rep', [(i, i ^ k * copies) for i in range(replicas)])  32.8 us
    ppermute x6, waiting for transfers between devices, spin(): lax.ppermute(a, 'fsdp', [(i, (i + k) % shards) for i in range(shards)])  24.8 us
    unnamed x103, local copies, waits for them, and re-layouts  23.6 us
    ppermute x6, starting transfers between devices, spin(): lax.ppermute(a, 'fsdp', [(i, (i + k) % shards) for i in range(shards)])  21.5 us
    ppermute x10, waiting for transfers between devices, to_part(): return lax.ppermute(a, 'rep', [(i, i ^ m) for i in range(replicas)])  15.3 us
  transfers between devices with their start and end apart: 47, of which 26 were waited for; matrix products, arithmetic and copies ran while one was open for 4% of the time, Pallas kernels for 39%

profile of v1, /device:TPU:0, one launch (start us, length us, event | category | flops | bytes accessed | tf_op | source)
XLA Modules:
  0.0 541.9 jit_solution(8643411909758899883)
XLA Ops:
  10.1 3.2 concatenate.14.refs_3_
  17.2 6.5 %constant_dynamic-slice_fusion.1 = bf16[192,1,4096]{2,1,0:T(2,128)(2,1)S(1)} fusion(bf16[192,4,4096]{2,1,0:T(4,128)(2,1)} %param.30, s32[]{:T(128)S(6)} %select_n.43), kind=kLoop, calls=%fused_computation.33 | loop fusion | bytes 3145732 | tf_op jit(solution)/shard_map/jit(dynamic_index_in_dim)/dynamic_slice | solution.py:1418
  23.7 2.9 copy.107
  29.3 2.9 pack.1
  32.2 3.1 collective-permute-start
  35.3 2.6 collective-permute-start.1
  43.2 16.1 %collective-permute-done.1.refs_3_ = bf16[64,1536]{1,0:T(8,128)(2,1)S(1)} collective-permute-done((bf16[64,1536]{1,0:T(8,128)(2,1)S(1)}, bf16[64,1536]{1,0:T(8,128)(2,1)S(1)}, u32[]{:S(2)}, u32[]{:S(2)}) %collective-permute-start.1) | collective-permute-done | bytes 196640 | tf_op jit(solution)/shard_map/ppermute | solution.py:1392
  71.3 4.2 collective-permute-done.3.refs_2_
  75.5 8.4 %collective-permute-done.4.refs_3_ = bf16[4,48,1152]{2,1,0:T(8,128)(2,1)} collective-permute-done((bf16[4,48,1152]{2,1,0:T(8,128)(2,1)}, bf16[4,48,1152]{2,1,0:T(8,128)(2,1)}, u32[]{:S(2)}, u32[]{:S(2)}) %collective-permute-start.4) | collective-permute-done | bytes 442400 | tf_op jit(solution)/shard_map/ppermute | solution.py:1386
  84.7 2.8 lay_xor.1.refs_4_
  88.3 5.5 %dispatch.2 = (bf16[480,768]{1,0:T(8,128)(2,1)}, bf16[480,768]{1,0:T(8,128)(2,1)}, bf16[480,768]{1,0:T(8,128)(2,1)}, bf16[480,768]{1,0:T(8,128)(2,1)}) custom-call(s32[1]{0:T(128)} %bitcast.2.refs_0_, s32[4,1024]{1,0:T(4,128)} %get-tuple-element.269.refs_7_.refs_1_, bf16[1024,768]{1,0:T(8,128)(2,1)} %refs_3_.2, bf16[96,768]{1,0:T(8,128)(2,1)} %bitcast.73, ...), custom_call_target="tpu_custom_call" | custom-call | flops 48318384 | bytes 78643 | tf_op jit(solution)/shard_map/dispatch/pallas_call | solution.py:61
  98.5 9.0 %qkv_rope.1 = (bf16[1024,768]{1,0:T(8,128)(2,1)}, bf16[1024,768]{1,0:T(8,128)(2,1)}, bf16[1024,768]{1,0:T(8,128)(2,1)}, bf16[1024,768]{1,0:T(8,128)(2,1)}) custom-call(s32[1]{0:T(128)} %bitcast.part_ref.refs_0_, bf16[1024,768]{1,0:T(8,128)(2,1)} %refs_4_.3, bf16[128,768]{1,0:T(8,128)(2,1)} %get-tuple-element.118.refs_2_.refs_3_.refs_8_.refs_4_.refs_6_, ...), custom_call_target="tpu_custom_call" | custom-call | flops 72477576 | bytes 228065 | tf_op jit(solution)/shard_map/qkv_rope/pallas_call | solution.py:61
  107.6 25.9 %attend.1 = (bf16[1024,768]{1,0:T(8,128)(2,1)}, f32[6,2,1024]{2,1,0:T(2,128)}) custom-call(bf16[1024,768]{1,0:T(8,128)(2,1)} %get-tuple-element.122.refs_0_, bf16[1024,768]{1,0:T(8,128)(2,1)} %get-tuple-element.123.refs_1_, bf16[1024,768]{1,0:T(8,128)(2,1)} %get-tuple-element.124.refs_2_, s32[1024,1]{1,0:T(8,128)} %copy.88.refs_8_.refs_3_.refs_5_, ...), custom_call_target="tpu_custom_call" | custom-call | flops 400000000 | bytes 125829 | tf_op jit(solution)/shard_map/attend/pallas_call | solution.py:61
  134.8 2.7 lay_riders.1
  140.5 8.2 %after_attention.1 = (f32[1024,768]{1,0:T(8,128)}, bf16[1024,768]{1,0:T(8,128)(2,1)}, f32[1024,128]{1,0:T(8,128)}, bf16[16,1024]{1,0:T(8,128)(2,1)}) custom-call(s32[1]{0:T(128)} %bitcast.part_ref.refs_0_, bf16[1024,768]{1,0:T(8,128)(2,1)} %get-tuple-element.125.refs_5_.refs_1_.refs_2_, bf16[1024,768]{1,0:T(8,128)(2,1)} %refs_4_.3, ...), custom_call_target="tpu_custom_call" | custom-call | flops 24159192 | bytes 157286 | tf_op jit(solution)/shard_map/after_attention/pallas_call | solution.py:61
  148.7 6.0 %dispatch.3 = (bf16[400,768]{1,0:T(8,128)(2,1)}, bf16[400,768]{1,0:T(8,128)(2,1)}, bf16[400,768]{1,0:T(8,128)(2,1)}, bf16[400,768]{1,0:T(8,128)(2,1)}) custom-call(s32[1]{0:T(128)} %bitcast.2.refs_0_, s32[4,1024]{1,0:T(4,128)} %get-tuple-element.269.refs_7_.refs_1_, bf16[1024,768]{1,0:T(8,128)(2,1)} %get-tuple-element.132.refs_2_, ...), custom_call_target="tpu_custom_call" | custom-call | flops 48318384 | bytes 78643 | tf_op jit(solution)/shard_map/dispatch/pallas_call | solution.py:61
  158.8 2.8 collective-permute-done.14.refs_9_
  162.9 9.3 %collective-permute-done.11.refs_1_ = bf16[400,768]{1,0:T(8,128)(2,1)S(1)} collective-permute-done((bf16[400,768]{1,0:T(8,128)(2,1)}, bf16[400,768]{1,0:T(8,128)(2,1)S(1)}, u32[]{:S(2)}, u32[]{:S(2)}) %collective-permute-start.11) | collective-permute-done | bytes 614432 | tf_op jit(solution)/shard_map/ppermute | solution.py:1386
  172.2 12.0 %collective-permute-done.12.refs_2_ = bf16[400,768]{1,0:T(8,128)(2,1)S(1)} collective-permute-done((bf16[400,768]{1,0:T(8,128)(2,1)}, bf16[400,768]{1,0:T(8,128)(2,1)S(1)}, u32[]{:S(2)}, u32[]{:S(2)}) %collective-permute-start.12) | collective-permute-done | bytes 614432 | tf_op jit(solution)/shard_map/ppermute | solution.py:1386
  186.6 32.0 %experts.2 = (bf16[4,1152,256]{2,1,0:T(8,128)(2,1)}, bf16[4,1152,256]{2,1,0:T(8,128)(2,1)}, f32[1536,768]{1,0:T(8,128)}, f32[1536,768]{1,0:T(8,128)}) custom-call(bf16[400,768]{1,0:T(8,128)(2,1)} %get-tuple-element.134.refs_0_, bf16[400,768]{1,0:T(8,128)(2,1)} %copy-done.11, bf16[400,768]{1,0:T(8,128)(2,1)} %copy-done.12, bf16[400,768]{1,0:T(8,128)(2,1)} %copy-done.13, ...), custom_call_target="tpu_custom_call" | custom-call | flops 434865440 | bytes 471859 | tf_op jit(solution)/shard_map/experts/pallas_call | solution.py:872
  218.7 4.7 collective-permute-done.19.refs_1_
  224.8 6.4 %fold_copies.2.refs_15_ = bf16[4,1152,256]{2,1,0:T(8,128)(2,1)} custom-call(bf16[4,1152,256]{2,1,0:T(8,128)(2,1)} %get-tuple-element.153.refs_0_, bf16[4,1152,256]{2,1,0:T(8,128)(2,1)} %copy-done.17), custom_call_target="tpu_custom_call" | custom-call | tf_op jit(solution)/shard_map/fold_copies/pallas_call | solution.py:61
  231.2 36.3 %experts.3 = (bf16[4,1152,256]{2,1,0:T(8,128)(2,1)}, bf16[4,1152,256]{2,1,0:T(8,128)(2,1)}, bf16[400,768]{1,0:T(8,128)(2,1)}, bf16[400,768]{1,0:T(8,128)(2,1)}, ...) custom-call(bf16[400,768]{1,0:T(8,128)(2,1)} %get-tuple-element.134., ...), custom_call_target="tpu_custom_call" | custom-call | flops 434865440 | bytes 471859 | tf_op jit(solution)/shard_map/experts/pallas_call | solution.py:872
  268.6 2.3 collective-permute-start.17
  271.3 13.4 %collective-permute-done.16.refs_10_ = bf16[400,768]{1,0:T(8,128)(2,1)S(1)} collective-permute-done((bf16[400,768]{1,0:T(8,128)(2,1)}, bf16[400,768]{1,0:T(8,128)(2,1)S(1)}, u32[]{:S(2)}, u32[]{:S(2)}) %collective-permute-start.16) | collective-permute-done | bytes 614432 | tf_op jit(solution)/shard_map/ppermute | solution.py:1386
  284.7 13.1 %collective-permute-done.17.refs_11_ = bf16[400,768]{1,0:T(8,128)(2,1)S(1)} collective-permute-done((bf16[400,768]{1,0:T(8,128)(2,1)}, bf16[400,768]{1,0:T(8,128)(2,1)S(1)}, u32[]{:S(2)}, u32[]{:S(2)}) %collective-permute-start.17) | collective-permute-done | bytes 614432 | tf_op jit(solution)/shard_map/ppermute | solution.py:1386
  299.2 19.0 %combine_back.1 = (f32[1024,768]{1,0:T(8,128)}, bf16[1024,768]{1,0:T(8,128)(2,1)}, bf16[1024,768]{1,0:T(8,128)(2,1)}, f32[128,768]{1,0:T(8,128)}, f32[1,768]{1,0...) custom-call(s32[2]{0:T(128)} %pad_add_fusion.refs_0_, f32[1024,768]{1,0:T(8,128)} %get-tuple-element.130.refs_1_.refs_0_, ...), custom_call_target="tpu_custom_call" | custom-call | flops 88583696 | bytes 314572 | tf_op jit(solution)/shard_map/combine_back/pallas_call | solution.py:61
  319.6 6.4 %fold_copies.3 = bf16[4,1152,256]{2,1,0:T(8,128)(2,1)} custom-call(bf16[4,1152,256]{2,1,0:T(8,128)(2,1)} %get-tuple-element.172.refs_0_, bf16[4,1152,256]{2,1,0:T(8,128)(2,1)} %copy-done.15), custom_call_target="tpu_custom_call" | custom-call | tf_op jit(solution)/shard_map/fold_copies/pallas_call | solution.py:61
  332.0 31.1 %attend_back.1 = (bf16[1024,768]{1,0:T(8,128)(2,1)}, bf16[1024,768]{1,0:T(8,128)(2,1)}, bf16[1024,768]{1,0:T(8,128)(2,1)}) custom-call(bf16[1024,768]{1,0:T(8,128)(2,1)} %get-tuple-element.122.refs_0_, bf16[1024,768]{1,0:T(8,128)(2,1)} %get-tuple-element.123.refs_1_, bf16[1024,768]{1,0:T(8,128)(2,1)} %get-tuple-element.124.refs_2_, ...), custom_call_target="tpu_custom_call" | custom-call | flops 900000000 | bytes 220200 | tf_op jit(solution)/shard_map/attend_back/pallas_call | solution.py:61
  363.2 3.1 collective-permute-done.23
  368.3 14.7 %dense_grads.1 = (bf16[768,1536]{1,0:T(8,128)(2,1)}, bf16[768,1536]{1,0:T(8,128)(2,1)}) custom-call(s32[1]{0:T(128)} %bitcast.part_ref.refs_0_, bf16[1024,768]{1,0:T(8,128)(2,1)} %get-tuple-element.160.refs_1_, bf16[1024,768]{1,0:T(8,128)(2,1)} %get-tuple-element.125.refs_5_.refs_1_.refs_2_, bf16[1024,768]{1,0:T(8,128)(2,1)} %get-tuple-element.165.refs_3_.refs_1_, ...), custom_call_target="tpu_custom_call" | custom-call | flops 96636768 | bytes 283115 | tf_op jit(solution)/shard_map/dense_grads/pallas_call | solution.py:61
  383.0 4.6 reduce-scatter.5.cloned.1.call-done
  387.6 2.4 collective-permute-start.27
  390.0 2.4 collective-permute-done.26
  393.8 4.4 fold_parts.1
  398.2 6.1 %collective-permute-done.27 = bf16[1152,256]{1,0:T(8,128)(2,1)S(1)} collective-permute-done((bf16[1152,256]{1,0:T(8,128)(2,1)S(1)}, bf16[1152,256]{1,0:T(8,128)(2,1)S(1)}, u32[]{:S(2)}, u32[]{:S(2)}) %collective-permute-start.27) | collective-permute-done | bytes 589856 | tf_op jit(solution)/shard_map/ppermute | solution.py:1386
  409.2 7.8 %layer_out.1.refs_8_ = bf16[1024,768]{1,0:T(8,128)(2,1)} custom-call(f32[1024,768]{1,0:T(8,128)} %get-tuple-element.130.refs_1_.refs_0_, f32[1024,128]{1,0:T(8,128)} %get-tuple-element.131.refs_4_.refs_1_, s32[1024,2]{1,0:T(8,128)} %bitcast_select_fusion.refs_10_.refs_5_.refs_2_, s32[1024,2]{1,0:T(8,128)} %copy-done.2, ...), custom_call_target="tpu_custom_call" | custom-call | flops 48318384 | bytes 157286 | tf_op jit(solution)/shard_map/layer_out/pallas_call | solution.py:61
  417.0 10.6 %input_grad.1 = (bf16[1024,768]{1,0:T(8,128)(2,1)}, bf16[768,128]{1,0:T(8,128)(2,1)}) custom-call(s32[1]{0:T(128)} %bitcast.part_ref.refs_0_, bf16[1024,768]{1,0:T(8,128)(2,1)} %get-tuple-element.165.refs_3_.refs_1_, bf16[1024,768]{1,0:T(8,128)(2,1)} %get-tuple-element.166.refs_4_.refs_2_, bf16[1024,768]{1,0:T(8,128)(2,1)} %get-tuple-element.167.refs_5_.refs_3_, ...), custom_call_target="tpu_custom_call" | custom-call | flops 72477576 | bytes 220200 | tf_op jit(solution)/shard_map/input_grad/pallas_call | solution.py:61
  429.2 13.4 %unpack.2 = (f32[192,4,4096]{2,1,0:T(4,128)}, f32[512,4,768]{2,1,0:T(4,128)}) custom-call(s32[2]{0:T(128)} %pad_add_fusion.refs_0_, bf16[4,1152,256]{2,1,0:T(8,128)(2,1)} %copy-done.3, bf16[4,1152,256]{2,1,0:T(8,128)(2,1)} %copy-done.9, bf16[4,384,256]{2,1,0:T(8,128)(2,1)} %slice.44.refs_3_, bf16[4,384,256]{2,1,0:T(8,128)(2,1)} %slice.45.refs_4_), custom_call_target="tpu_custom_call" | custom-call | bytes 377487 | tf_op jit(solution)/shard_map/unpack/pallas_call | solution.py:61
  443.6 2.8 fold_quarters.1
  446.4 12.1 %collective-permute-start.32 = (bf16[64,1536]{1,0:T(8,128)(2,1)}, bf16[64,1536]{1,0:T(8,128)(2,1)S(1)}, u32[]{:S(2)}, u32[]{:S(2)}) collective-permute-start(bf16[64,1536]{1,0:T(8,128)(2,1)} %get-tuple-element.204), channel_id=1, source_target_pairs={{0,1},{1,2},{2,3},{3,0},{4,5},{5,6},{6,7},{7,4},{8,9},{9,10},{10,1... | collective-permute-start | bytes 589832 | tf_op jit(solution)/shard_map/ppermute | solution.py:1392
  458.5 2.4 collective-permute-start.34
  464.2 5.6 %collective-permute-done.33.refs_2_ = bf16[64,1536]{1,0:T(8,128)(2,1)S(1)} collective-permute-done((bf16[64,1536]{1,0:T(8,128)(2,1)}, bf16[64,1536]{1,0:T(8,128)(2,1)S(1)}, u32[]{:S(2)}, u32[]{:S(2)}) %collective-permute-start.33) | collective-permute-done | bytes 196640 | tf_op jit(solution)/shard_map/ppermute | solution.py:1392
  477.4 14.9 %collective-permute-done.35.refs_2_ = bf16[64,1536]{1,0:T(8,128)(2,1)S(1)} collective-permute-done((bf16[64,1536]{1,0:T(8,128)(2,1)}, bf16[64,1536]{1,0:T(8,128)(2,1)S(1)}, u32[]{:S(2)}, u32[]{:S(2)}) %collective-permute-start.35) | collective-permute-done | bytes 196640 | tf_op jit(solution)/shard_map/ppermute | solution.py:1386
  493.8 5.2 collective-permute-done.37.refs_4_
  504.5 3.2 collective-permute-done.38.refs_2_
  508.6 2.8 unpack_dense.1
  521.4 13.6 %unpack.3 = (f32[192,4,4096]{2,1,0:T(4,128)}, f32[512,4,768]{2,1,0:T(4,128)}) custom-call(s32[2]{0:T(128)} %pad_add_fusion.refs_0_, bf16[4,1152,256]{2,1,0:T(8,128)(2,1)} %copy-done.4, bf16[4,1152,256]{2,1,0:T(8,128)(2,1)} %collective-permute-done.42.refs_2_, bf16[4,384,256]{2,1,0:T(8,128)(2,1)} %slice.46.refs_3_, ...), custom_call_target="tpu_custom_call", output_to_operand_aliasing={{0}: (5, {}), {1}: (6, {})} | custom-call | bytes 377487 | tf_op jit(solution)/shard_map/unpack/pallas_call | solution.py:61
  (214 shorter events, 94.5 us)
Async XLA Ops:
  7.2 147.6 %all-gather.5.cloned.1.call-start = ((), (), s32[]{:S(2)}) async-start(), calls=%async_computation.4 | async-start | bytes 2949120 | tf_op jit(solution)/shard_map/all_gather | solution.py:1421
  32.1 122.8 %all-gather.7.cloned.1.call-start = ((), (), s32[]{:S(2)}) async-start(), calls=%async_computation.5 | async-start | bytes 2949120 | tf_op jit(solution)/shard_map/all_gather | solution.py:1421
  32.2 11.0 %collective-permute-start = (bf16[64,1536]{1,0:T(8,128)(2,1)S(1)}, bf16[64,1536]{1,0:T(8,128)(2,1)S(1)}, u32[]{:S(2)}, u32[]{:S(2)}) collective-permute-start(bf16[64,1536]{1,0:T(8,128)(2,1)S(1)} %copy-done.34), channel_id=1, source_target_pairs={{0,1},{1,2},{2,3},{3,0},{4,5},{5,6},{6,7},{7,4},{8,9},{9,10},{10,1... | collective-permute-start | bytes 589832 | tf_op jit(solution)/shard_map/ppermute | solution.py:1392
  35.3 24.0 %collective-permute-start.1 = (bf16[64,1536]{1,0:T(8,128)(2,1)S(1)}, bf16[64,1536]{1,0:T(8,128)(2,1)S(1)}, u32[]{:S(2)}, u32[]{:S(2)}) collective-permute-start(bf16[64,1536]{1,0:T(8,128)(2,1)S(1)} %copy-done.34), channel_id=1, source_target_pairs={{0,2},{1,3},{2,0},{3,1},{4,6},{5,7},{6,4},{7,5},{8,10},{9,11},{10,... | collective-permute-start | bytes 589832 | tf_op jit(solution)/shard_map/ppermute | solution.py:1392
  37.9 21.4 %collective-permute-start.2 = (bf16[64,1536]{1,0:T(8,128)(2,1)S(1)}, bf16[64,1536]{1,0:T(8,128)(2,1)S(1)}, u32[]{:S(2)}, u32[]{:S(2)}) collective-permute-start(bf16[64,1536]{1,0:T(8,128)(2,1)S(1)} %copy-done.34), channel_id=1, source_target_pairs={{0,3},{1,0},{2,1},{3,2},{4,7},{5,4},{6,5},{7,6},{8,11},{9,8},{10,9... | collective-permute-start | bytes 589832 | tf_op jit(solution)/shard_map/ppermute | solution.py:1392
  39.2 290.3 %reduce-scatter.3.cloned.1.call-start = ((), (), s32[]{:S(2)}) async-start(), calls=%async_computation.2 | async-start | bytes 2949120 | tf_op jit(solution)/shard_map/reduce_scatter | solution.py:1514
  41.0 26.5 %copy-start.47 = (s32[1,1024]{1,0:T(1,128)S(1)}, s32[1,1024]{1,0:T(1,128)}, u32[]{:S(2)}) copy-start(s32[1,1024]{1,0:T(1,128)} %param.21) | copy-start | bytes 12292
  62.1 13.4 %collective-permute-start.3 = (bf16[4,48,1152]{2,1,0:T(8,128)(2,1)}, bf16[4,48,1152]{2,1,0:T(8,128)(2,1)}, u32[]{:S(2)}, u32[]{:S(2)}) collective-permute-start(bf16[4,48,1152]{2,1,0:T(8,128)(2,1)} %get-tuple-element.119.refs_1_), channel_id=1, source_target_pairs={{0,8},{4,12},{8,0},{12,4},{16,24},{20,28},{24,16},{28,20},{1,9},{5... | collective-permute-start | bytes 1327112 | tf_op jit(solution)/shard_map/ppermute | solution.py:1386
  63.4 20.5 %collective-permute-start.4 = (bf16[4,48,1152]{2,1,0:T(8,128)(2,1)}, bf16[4,48,1152]{2,1,0:T(8,128)(2,1)}, u32[]{:S(2)}, u32[]{:S(2)}) collective-permute-start(bf16[4,48,1152]{2,1,0:T(8,128)(2,1)} %get-tuple-element.119.refs_1_), channel_id=1, source_target_pairs={{0,16},{4,20},{8,24},{12,28},{16,0},{20,4},{24,8},{28,12},{1,17},{... | collective-permute-start | bytes 1327112 | tf_op jit(solution)/shard_map/ppermute | solution.py:1386
  65.0 19.7 %collective-permute-start.5 = (bf16[4,48,1152]{2,1,0:T(8,128)(2,1)}, bf16[4,48,1152]{2,1,0:T(8,128)(2,1)}, u32[]{:S(2)}, u32[]{:S(2)}) collective-permute-start(bf16[4,48,1152]{2,1,0:T(8,128)(2,1)} %get-tuple-element.119.refs_1_), channel_id=1, source_target_pairs={{0,24},{4,28},{8,16},{12,20},{16,8},{20,12},{24,0},{28,4},{1,25},{... | collective-permute-start | bytes 1327112 | tf_op jit(solution)/shard_map/ppermute | solution.py:1386
  87.5 9.8 %collective-permute-start.6 = (bf16[768,1152]{1,0:T(8,128)(2,1)}, bf16[768,1152]{1,0:T(8,128)(2,1)S(1)}, u32[]{:S(2)}, u32[]{:S(2)}) collective-permute-start(bf16[768,1152]{1,0:T(8,128)(2,1)} %bitcast.46), channel_id=1, source_target_pairs={{0,4},{4,0},{8,12},{12,8},{16,20},{20,16},{24,28},{28,24},{1,5},{5... | collective-permute-start | bytes 5308424 | tf_op jit(solution)/shard_map/ppermute | solution.py:1389
  93.8 39.6 %collective-permute-start.7 = (bf16[480,768]{1,0:T(8,128)(2,1)}, bf16[480,768]{1,0:T(8,128)(2,1)S(1)}, u32[]{:S(2)}, u32[]{:S(2)}) collective-permute-start(bf16[480,768]{1,0:T(8,128)(2,1)} %get-tuple-element.127), channel_id=1, source_target_pairs={{0,8},{4,12},{8,0},{12,4},{16,24},{20,28},{24,16},{28,20},{1,9},{5... | collective-permute-start | bytes 2211848 | tf_op jit(solution)/shard_map/ppermute | solution.py:1386
  95.3 38.2 %collective-permute-start.8 = (bf16[480,768]{1,0:T(8,128)(2,1)}, bf16[480,768]{1,0:T(8,128)(2,1)S(1)}, u32[]{:S(2)}, u32[]{:S(2)}) collective-permute-start(bf16[480,768]{1,0:T(8,128)(2,1)} %get-tuple-element.128), channel_id=1, source_target_pairs={{0,16},{4,20},{8,24},{12,28},{16,0},{20,4},{24,8},{28,12},{1,17},{... | collective-permute-start | bytes 2211848 | tf_op jit(solution)/shard_map/ppermute | solution.py:1386
  96.1 37.4 %collective-permute-start.9 = (bf16[480,768]{1,0:T(8,128)(2,1)}, bf16[480,768]{1,0:T(8,128)(2,1)S(1)}, u32[]{:S(2)}, u32[]{:S(2)}) collective-permute-start(bf16[480,768]{1,0:T(8,128)(2,1)} %get-tuple-element.129), channel_id=1, source_target_pairs={{0,24},{4,28},{8,16},{12,20},{16,8},{20,12},{24,0},{28,4},{1,25},{... | collective-permute-start | bytes 2211848 | tf_op jit(solution)/shard_map/ppermute | solution.py:1386
  137.5 2.2 collective-permute-start.10
  154.8 6.8 %collective-permute-start.14 = (bf16[4,1152,256]{2,1,0:T(8,128)(2,1)}, bf16[4,1152,256]{2,1,0:T(8,128)(2,1)}, u32[]{:S(2)}, u32[]{:S(2)}) collective-permute-start(bf16[4,1152,256]{2,1,0:T(8,128)(2,1)} %bitcast.55), channel_id=1, source_target_pairs={{0,4},{4,0},{8,12},{12,8},{16,20},{20,16},{24,28},{28,24},{1,5},{5... | collective-permute-start | bytes 7077896 | tf_op jit(solution)/shard_map/ppermute | solution.py:1389
  154.9 8.0 %collective-permute-start.15 = (bf16[4,1152,256]{2,1,0:T(8,128)(2,1)}, bf16[4,1152,256]{2,1,0:T(8,128)(2,1)S(1)}, u32[]{:S(2)}, u32[]{:S(2)}) collective-permute-start(bf16[4,1152,256]{2,1,0:T(8,128)(2,1)} %bitcast.57), channel_id=1, source_target_pairs={{0,4},{4,0},{8,12},{12,8},{16,20},{20,16},{24,28},{28,24},{1,5},{5... | collective-permute-start | bytes 7077896 | tf_op jit(solution)/shard_map/ppermute | solution.py:1389
  155.3 16.9 %collective-permute-start.11 = (bf16[400,768]{1,0:T(8,128)(2,1)}, bf16[400,768]{1,0:T(8,128)(2,1)S(1)}, u32[]{:S(2)}, u32[]{:S(2)}) collective-permute-start(bf16[400,768]{1,0:T(8,128)(2,1)} %get-tuple-element.135), channel_id=1, source_target_pairs={{0,8},{4,12},{8,0},{12,4},{16,24},{20,28},{24,16},{28,20},{1,9},{5... | collective-permute-start | bytes 1843208 | tf_op jit(solution)/shard_map/ppermute | solution.py:1386
  156.7 27.5 %collective-permute-start.12 = (bf16[400,768]{1,0:T(8,128)(2,1)}, bf16[400,768]{1,0:T(8,128)(2,1)S(1)}, u32[]{:S(2)}, u32[]{:S(2)}) collective-permute-start(bf16[400,768]{1,0:T(8,128)(2,1)} %get-tuple-element.136), channel_id=1, source_target_pairs={{0,16},{4,20},{8,24},{12,28},{16,0},{20,4},{24,8},{28,12},{1,17},{... | collective-permute-start | bytes 1843208 | tf_op jit(solution)/shard_map/ppermute | solution.py:1386
  157.6 28.2 %collective-permute-start.13 = (bf16[400,768]{1,0:T(8,128)(2,1)}, bf16[400,768]{1,0:T(8,128)(2,1)S(1)}, u32[]{:S(2)}, u32[]{:S(2)}) collective-permute-start(bf16[400,768]{1,0:T(8,128)(2,1)} %get-tuple-element.137), channel_id=1, source_target_pairs={{0,24},{4,28},{8,16},{12,20},{16,8},{20,12},{24,0},{28,4},{1,25},{... | collective-permute-start | bytes 1843208 | tf_op jit(solution)/shard_map/ppermute | solution.py:1386
  218.6 4.8 collective-permute-start.19
  231.2 156.5 %reduce-scatter.5.cloned.1.call-start = ((), (), s32[]{:S(2)}) async-start(), calls=%async_computation.3 | async-start | bytes 2949120 | tf_op jit(solution)/shard_map/reduce_scatter | solution.py:1514
  267.6 50.6 %collective-permute-start.25 = (bf16[4,1152,256]{2,1,0:T(8,128)(2,1)}, bf16[4,1152,256]{2,1,0:T(8,128)(2,1)S(1)}, u32[]{:S(2)}, u32[]{:S(2)}) collective-permute-start(bf16[4,1152,256]{2,1,0:T(8,128)(2,1)} %get-tuple-element.171), channel_id=1, source_target_pairs={{0,4},{4,0},{8,12},{12,8},{16,20},{20,16},{24,28},{28,24},{1,5},{5... | collective-permute-start | bytes 7077896 | tf_op jit(solution)/shard_map/ppermute | solution.py:1389
  267.8 16.9 %collective-permute-start.16 = (bf16[400,768]{1,0:T(8,128)(2,1)}, bf16[400,768]{1,0:T(8,128)(2,1)S(1)}, u32[]{:S(2)}, u32[]{:S(2)}) collective-permute-start(bf16[400,768]{1,0:T(8,128)(2,1)} %get-tuple-element.150), channel_id=1, source_target_pairs={{0,8},{4,12},{8,0},{12,4},{16,24},{20,28},{24,16},{28,20},{1,9},{5... | collective-permute-start | bytes 1843208 | tf_op jit(solution)/shard_map/ppermute | solution.py:1386
  268.6 29.2 %collective-permute-start.17 = (bf16[400,768]{1,0:T(8,128)(2,1)}, bf16[400,768]{1,0:T(8,128)(2,1)S(1)}, u32[]{:S(2)}, u32[]{:S(2)}) collective-permute-start(bf16[400,768]{1,0:T(8,128)(2,1)} %get-tuple-element.151), channel_id=1, source_target_pairs={{0,16},{4,20},{8,24},{12,28},{16,0},{20,4},{24,8},{28,12},{1,17},{... | collective-permute-start | bytes 1843208 | tf_op jit(solution)/shard_map/ppermute | solution.py:1386
  270.9 27.5 %collective-permute-start.18 = (bf16[400,768]{1,0:T(8,128)(2,1)}, bf16[400,768]{1,0:T(8,128)(2,1)S(1)}, u32[]{:S(2)}, u32[]{:S(2)}) collective-permute-start(bf16[400,768]{1,0:T(8,128)(2,1)} %get-tuple-element.152), channel_id=1, source_target_pairs={{0,24},{4,28},{8,16},{12,20},{16,8},{20,12},{24,0},{28,4},{1,25},{... | collective-permute-start | bytes 1843208 | tf_op jit(solution)/shard_map/ppermute | solution.py:1386
  326.0 37.2 %collective-permute-start.20 = (bf16[384,768]{1,0:T(8,128)(2,1)}, bf16[384,768]{1,0:T(8,128)(2,1)S(1)}, u32[]{:S(2)}, u32[]{:S(2)}) collective-permute-start(bf16[384,768]{1,0:T(8,128)(2,1)} %get-tuple-element.157), channel_id=1, source_target_pairs={{0,8},{4,12},{8,0},{12,4},{16,24},{20,28},{24,16},{28,20},{1,9},{5... | collective-permute-start | bytes 1769480 | tf_op jit(solution)/shard_map/ppermute | solution.py:1386
  327.5 35.7 %collective-permute-start.21 = (bf16[384,768]{1,0:T(8,128)(2,1)}, bf16[384,768]{1,0:T(8,128)(2,1)S(1)}, u32[]{:S(2)}, u32[]{:S(2)}) collective-permute-start(bf16[384,768]{1,0:T(8,128)(2,1)} %get-tuple-element.158), channel_id=1, source_target_pairs={{0,16},{4,20},{8,24},{12,28},{16,0},{20,4},{24,8},{28,12},{1,17},{... | collective-permute-start | bytes 1769480 | tf_op jit(solution)/shard_map/ppermute | solution.py:1386
  328.6 34.7 %collective-permute-start.22 = (bf16[384,768]{1,0:T(8,128)(2,1)}, bf16[384,768]{1,0:T(8,128)(2,1)S(1)}, u32[]{:S(2)}, u32[]{:S(2)}) collective-permute-start(bf16[384,768]{1,0:T(8,128)(2,1)} %get-tuple-element.159), channel_id=1, source_target_pairs={{0,24},{4,28},{8,16},{12,20},{16,8},{20,12},{24,0},{28,4},{1,25},{... | collective-permute-start | bytes 1769480 | tf_op jit(solution)/shard_map/ppermute | solution.py:1386
  329.5 36.8 %collective-permute-start.23 = (bf16[1152,256]{1,0:T(8,128)(2,1)}, bf16[1152,256]{1,0:T(8,128)(2,1)S(1)}, u32[]{:S(2)}, u32[]{:S(2)}) collective-permute-start(bf16[1152,256]{1,0:T(8,128)(2,1)} %bitcast.64), channel_id=1, source_target_pairs={{0,8},{4,12},{8,0},{12,4},{16,24},{20,28},{24,16},{28,20},{1,9},{5... | collective-permute-start | bytes 1769480 | tf_op jit(solution)/shard_map/ppermute | solution.py:1386
  331.0 36.5 %collective-permute-start.24 = (bf16[1152,256]{1,0:T(8,128)(2,1)}, bf16[1152,256]{1,0:T(8,128)(2,1)S(1)}, u32[]{:S(2)}, u32[]{:S(2)}) collective-permute-start(bf16[1152,256]{1,0:T(8,128)(2,1)} %bitcast.65), channel_id=1, source_target_pairs={{0,16},{4,20},{8,24},{12,28},{16,0},{20,4},{24,8},{28,12},{1,17},{... | collective-permute-start | bytes 1769480 | tf_op jit(solution)/shard_map/ppermute | solution.py:1386
  387.6 4.7 collective-permute-start.26
  387.6 16.6 %collective-permute-start.27 = (bf16[1152,256]{1,0:T(8,128)(2,1)S(1)}, bf16[1152,256]{1,0:T(8,128)(2,1)S(1)}, u32[]{:S(2)}, u32[]{:S(2)}) collective-permute-start(bf16[1152,256]{1,0:T(8,128)(2,1)S(1)} %bitcast.66), channel_id=1, source_target_pairs={{0,24},{4,28},{8,16},{12,20},{16,8},{20,12},{24,0},{28,4},{1,25},{... | collective-permute-start | bytes 1769480 | tf_op jit(solution)/shard_map/ppermute | solution.py:1386
  404.6 22.9 %collective-permute-start.31 = (bf16[4,1152,256]{2,1,0:T(8,128)(2,1)S(1)}, bf16[4,1152,256]{2,1,0:T(8,128)(2,1)S(1)}, u32[]{:S(2)}, u32[]{:S(2)}) collective-permute-start(bf16[4,1152,256]{2,1,0:T(8,128)(2,1)S(1)} %pad_maximum_fusion.refs_1_), channel_id=1, source_target_pairs={{0,4},{4,0},{8,12},{12,8},{16,20},{20,16},{24,28},{28,24},{1,5},{5... | collective-permute-start | bytes 7077896 | tf_op jit(solution)/shard_map/ppermute | solution.py:1389
  404.7 37.9 %collective-permute-start.28 = (bf16[4,48,1536]{2,1,0:T(8,128)(2,1)}, bf16[4,48,1536]{2,1,0:T(8,128)(2,1)S(1)}, u32[]{:S(2)}, u32[]{:S(2)}) collective-permute-start(bf16[4,48,1536]{2,1,0:T(8,128)(2,1)} %get-tuple-element.182), channel_id=1, source_target_pairs={{0,8},{4,12},{8,0},{12,4},{16,24},{20,28},{24,16},{28,20},{1,9},{5... | collective-permute-start | bytes 1769480 | tf_op jit(solution)/shard_map/ppermute | solution.py:1386
  406.2 36.4 %collective-permute-start.29 = (bf16[4,48,1536]{2,1,0:T(8,128)(2,1)}, bf16[4,48,1536]{2,1,0:T(8,128)(2,1)S(1)}, u32[]{:S(2)}, u32[]{:S(2)}) collective-permute-start(bf16[4,48,1536]{2,1,0:T(8,128)(2,1)} %get-tuple-element.183), channel_id=1, source_target_pairs={{0,16},{4,20},{8,24},{12,28},{16,0},{20,4},{24,8},{28,12},{1,17},{... | collective-permute-start | bytes 1769480 | tf_op jit(solution)/shard_map/ppermute | solution.py:1386
  407.7 35.0 %collective-permute-start.30 = (bf16[4,48,1536]{2,1,0:T(8,128)(2,1)}, bf16[4,48,1536]{2,1,0:T(8,128)(2,1)}, u32[]{:S(2)}, u32[]{:S(2)}) collective-permute-start(bf16[4,48,1536]{2,1,0:T(8,128)(2,1)} %get-tuple-element.184), channel_id=1, source_target_pairs={{0,24},{4,28},{8,16},{12,20},{16,8},{20,12},{24,0},{28,4},{1,25},{... | collective-permute-start | bytes 1769480 | tf_op jit(solution)/shard_map/ppermute | solution.py:1386
  446.4 17.8 %collective-permute-start.32 = (bf16[64,1536]{1,0:T(8,128)(2,1)}, bf16[64,1536]{1,0:T(8,128)(2,1)S(1)}, u32[]{:S(2)}, u32[]{:S(2)}) collective-permute-start(bf16[64,1536]{1,0:T(8,128)(2,1)} %get-tuple-element.204), channel_id=1, source_target_pairs={{0,1},{1,2},{2,3},{3,0},{4,5},{5,6},{6,7},{7,4},{8,9},{9,10},{10,1... | collective-permute-start | bytes 589832 | tf_op jit(solution)/shard_map/ppermute | solution.py:1392
  458.5 11.3 %collective-permute-start.33 = (bf16[64,1536]{1,0:T(8,128)(2,1)}, bf16[64,1536]{1,0:T(8,128)(2,1)S(1)}, u32[]{:S(2)}, u32[]{:S(2)}) collective-permute-start(bf16[64,1536]{1,0:T(8,128)(2,1)} %get-tuple-element.205), channel_id=1, source_target_pairs={{0,2},{1,3},{2,0},{3,1},{4,6},{5,7},{6,4},{7,5},{8,10},{9,11},{10,... | collective-permute-start | bytes 589832 | tf_op jit(solution)/shard_map/ppermute | solution.py:1392
  458.5 12.7 %collective-permute-start.34 = (bf16[64,1536]{1,0:T(8,128)(2,1)}, bf16[64,1536]{1,0:T(8,128)(2,1)S(1)}, u32[]{:S(2)}, u32[]{:S(2)}) collective-permute-start(bf16[64,1536]{1,0:T(8,128)(2,1)} %get-tuple-element.206), channel_id=1, source_target_pairs={{0,3},{1,0},{2,1},{3,2},{4,7},{5,4},{6,5},{7,6},{8,11},{9,8},{10,9... | collective-permute-start | bytes 589832 | tf_op jit(solution)/shard_map/ppermute | solution.py:1392
  460.9 41.0 %collective-permute-start.39 = (bf16[1152,256]{1,0:T(8,128)(2,1)S(1)}, bf16[1152,256]{1,0:T(8,128)(2,1)S(1)}, u32[]{:S(2)}, u32[]{:S(2)}) collective-permute-start(bf16[1152,256]{1,0:T(8,128)(2,1)S(1)} %bitcast.61), channel_id=1, source_target_pairs={{0,8},{4,12},{8,0},{12,4},{16,24},{20,28},{24,16},{28,20},{1,9},{5... | collective-permute-start | bytes 1769480 | tf_op jit(solution)/shard_map/ppermute | solution.py:1386
  461.3 40.6 %collective-permute-start.40 = (bf16[1152,256]{1,0:T(8,128)(2,1)S(1)}, bf16[1152,256]{1,0:T(8,128)(2,1)S(1)}, u32[]{:S(2)}, u32[]{:S(2)}) collective-permute-start(bf16[1152,256]{1,0:T(8,128)(2,1)S(1)} %bitcast.62), channel_id=1, source_target_pairs={{0,16},{4,20},{8,24},{12,28},{16,0},{20,4},{24,8},{28,12},{1,17},{... | collective-permute-start | bytes 1769480 | tf_op jit(solution)/shard_map/ppermute | solution.py:1386
  473.9 28.0 %collective-permute-start.41 = (bf16[1152,256]{1,0:T(8,128)(2,1)S(1)}, bf16[1152,256]{1,0:T(8,128)(2,1)S(1)}, u32[]{:S(2)}, u32[]{:S(2)}) collective-permute-start(bf16[1152,256]{1,0:T(8,128)(2,1)S(1)} %bitcast.63), channel_id=1, source_target_pairs={{0,24},{4,28},{8,16},{12,20},{16,8},{20,12},{24,0},{28,4},{1,25},{... | collective-permute-start | bytes 1769480 | tf_op jit(solution)/shard_map/ppermute | solution.py:1386
  475.1 17.1 %collective-permute-start.35 = (bf16[64,1536]{1,0:T(8,128)(2,1)}, bf16[64,1536]{1,0:T(8,128)(2,1)S(1)}, u32[]{:S(2)}, u32[]{:S(2)}) collective-permute-start(bf16[64,1536]{1,0:T(8,128)(2,1)} %fold_shards.1.refs_1_), channel_id=1, source_target_pairs={{0,8},{4,12},{8,0},{12,4},{16,24},{20,28},{24,16},{28,20},{1,9},{5... | collective-permute-start | bytes 589832 | tf_op jit(solution)/shard_map/ppermute | solution.py:1386
  475.7 18.1 %collective-permute-start.36 = (bf16[64,1536]{1,0:T(8,128)(2,1)}, bf16[64,1536]{1,0:T(8,128)(2,1)S(1)}, u32[]{:S(2)}, u32[]{:S(2)}) collective-permute-start(bf16[64,1536]{1,0:T(8,128)(2,1)} %fold_shards.1.refs_1_), channel_id=1, source_target_pairs={{0,16},{4,20},{8,24},{12,28},{16,0},{20,4},{24,8},{28,12},{1,17},{... | collective-permute-start | bytes 589832 | tf_op jit(solution)/shard_map/ppermute | solution.py:1386
  492.3 6.8 %collective-permute-start.37 = (bf16[64,1536]{1,0:T(8,128)(2,1)}, bf16[64,1536]{1,0:T(8,128)(2,1)S(1)}, u32[]{:S(2)}, u32[]{:S(2)}) collective-permute-start(bf16[64,1536]{1,0:T(8,128)(2,1)} %fold_shards.1.refs_1_), channel_id=1, source_target_pairs={{0,24},{4,28},{8,16},{12,20},{16,8},{20,12},{24,0},{28,4},{1,25},{... | collective-permute-start | bytes 589832 | tf_op jit(solution)/shard_map/ppermute | solution.py:1386
  502.2 17.1 %collective-permute-start.42 = (bf16[4,1152,256]{2,1,0:T(8,128)(2,1)S(1)}, bf16[4,1152,256]{2,1,0:T(8,128)(2,1)}, u32[]{:S(2)}, u32[]{:S(2)}) collective-permute-start(bf16[4,1152,256]{2,1,0:T(8,128)(2,1)S(1)} %pad_maximum_fusion.1.refs_1_), channel_id=1, source_target_pairs={{0,4},{4,0},{8,12},{12,8},{16,20},{20,16},{24,28},{28,24},{1,5},{5... | collective-permute-start | bytes 7077896 | tf_op jit(solution)/shard_map/ppermute | solution.py:1389
  502.9 4.8 collective-permute-start.38
  (47 other events, 322.4 us)
Sparse Core Ops, SparseCore 0:
  32.3 60.9 all-gather.4
  95.4 49.9 all-gather.6
  231.3 60.9 reduce-scatter.2
  326.1 61.4 reduce-scatter.4

commit v2 on v1

--- a/solution.py
+++ b/solution.py
@@ -20,6 +20,7 @@
 VMEM_BYTES = 58 * 1024 * 1024
 EPS = 1e-06
 COST_SCALE = 0.02
+ATT = 100
 f32 = jnp.float32
 bf16 = jnp.bfloat16
 
@@ -217,7 +218,7 @@
         grid=(pairs,),
         scratch_shapes=[pltpu.VMEM((length // QB, REACH + QB, QB), f32)],
         compiler_params=params(),
-        cost_estimate=cost(20e9, 8 * length * D),
+        cost_estimate=cost(ATT * 20e9, ATT * 8 * length * D),
         name="attend",
     )
 
@@ -307,21 +308,24 @@
     )
 
 
-def cut_dense_kernel(quarter, widths, who_ref, qkv_ref, proj_ref, small_ref, out_ref, token_ref):
-    token_ref[0] = who_ref[0]
+def cut_dense_kernel(quarter, widths, who_ref, qkv_ref, proj_ref, *refs):
+    smalls, out_ref, mark_ref = refs[:-2], refs[-2], refs[-1]
+    mark_ref[...] = qkv_ref[:16, :LANES]
     row = pl.multiple_of(who_ref[0] * quarter, quarter)
     start = 0
     for ref, width in zip((qkv_ref, proj_ref), widths, strict=True):
         column = pl.multiple_of(who_ref[1] * width, LANES)
         out_ref[:quarter, start : start + width] = ref[pl.ds(row, quarter), pl.ds(column, width)]
         start += width
-    shard = small_ref.shape[1]
+    shard = qkv_ref.shape[0]
     out_ref[quarter:, :] = jnp.zeros((16, start), bf16)
-    out_ref[quarter:, :shard] = small_ref[:16, :]
-    out_ref[quarter:, 2 * LANES : 3 * LANES] = small_ref[16:, :LANES]
-
-
-def cut_dense(who, qkv, proj, small, copies):
+    rows = jnp.concatenate([ref[...].astype(f32) for ref in smalls[:-1]], axis=0)
+    out_ref[quarter:, :shard] = rows.astype(bf16)
+    prev = smalls[-1]
+    out_ref[quarter : quarter + prev.shape[0], 2 * LANES : 2 * LANES + NCH] = prev[...]
+
+
+def cut_dense(who, qkv, proj, smalls, copies):
     shard = qkv.shape[0]
     quarter = shard // EXPERTS
     widths = (qkv.shape[1] // copies, proj.shape[1] // copies)
@@ -329,12 +333,12 @@
     if quarter % 16 == 0 and all(w % LANES == 0 for w in widths):
         return launch(
             partial(cut_dense_kernel, quarter, widths),
-            [who, qkv, proj, small],
-            [SMEM, VM, VM, VM],
-            [VM, SMEM],
+            [who, qkv, proj, *smalls],
+            [SMEM] + [VM] * (2 + len(smalls)),
+            [VM, VM],
             [
                 jax.ShapeDtypeStruct((quarter + 16, total), bf16),
-                jax.ShapeDtypeStruct((1,), jnp.int32),
+                jax.ShapeDtypeStruct((16, LANES), bf16),
             ],
             name="cut_dense",
         )
@@ -343,16 +347,16 @@
         lax.dynamic_slice(w, (row, who[1] * width), (quarter, width))
         for w, width in zip((qkv, proj), widths, strict=True)
     ]
-    spare = total - 3 * LANES
+    prev = smalls[-1]
     below = jnp.concatenate(
         [
-            jnp.pad(small[:16], ((0, 0), (0, 2 * LANES - shard))),
-            jnp.pad(small[16:], ((0, 0), (0, 2 * LANES - shard)))[:, :LANES],
-            jnp.zeros((16, spare), bf16),
+            jnp.pad(jnp.concatenate(smalls[:-1]), ((0, 0), (0, 2 * LANES - shard))),
+            jnp.pad(prev, ((0, 16 - prev.shape[0]), (0, total - 2 * LANES - NCH))),
         ],
         axis=1,
     )
-    return jnp.concatenate([jnp.concatenate(cuts, axis=1), below]), who[:1]
+    piece = jnp.concatenate([jnp.concatenate(cuts, axis=1), below])
+    return piece, piece[:16, :LANES]
 
 
 def lay_shards_kernel(count, shard, quarter, width, zi_ref, *refs):
@@ -574,38 +578,60 @@
         return (part * self.chunks + chunk) * self.seg
 
 
-def pack_kernel(plan, part_ref, in_ref, out_ref, *packs):
-    part = part_ref[0]
+def pack_kernel(plan, who_ref, in_ref, out_ref, pack):
+    mine, part = who_ref[0], who_ref[1]
     seg, shard = plan.seg, plan.shard
-    for chunk in range(plan.chunks):
-        pack = packs[chunk]
-        for half in range(2):
-            for tile in range(plan.tiles):
-                row = (half * plan.tiles + tile) * shard
-                for span in range(plan.spans):
-                    at = pl.multiple_of(plan.column(half, tile, span, part, chunk), LANES)
-                    pack[row : row + shard, span * seg : (span + 1) * seg] = in_ref[
-                        :, pl.ds(at, seg)
+    step = pl.program_id(0)
+    half, z = step // plan.shards, step % plan.shards
+    row = pl.multiple_of((half * plan.tiles + z // plan.spans) * shard, shard)
+    column = pl.multiple_of(z % plan.spans * seg, seg)
+    for e in range(EXPERTS):
+
+        @pl.when(mine == e)
+        def _(e=e):
+            value = in_ref[:, e, :]
+            for chunk in range(plan.chunks):
+                piece = value[:, chunk * seg : (chunk + 1) * seg]
+                for p in range(1, plan.copies):
+                    at = (p * plan.chunks + chunk) * seg
+                    piece = jnp.where(part == p, value[:, at : at + seg], piece)
+                at = pl.multiple_of(chunk * plan.rows + row, 16)
+                pack[pl.ds(at, shard), pl.ds(column, seg)] = piece
+
+        @pl.when((mine == e) & (step == 0))
+        def _(e=e):
+            for chunk in range(plan.chunks):
+                start = chunk * plan.rows + 2 * plan.tiles * shard
+                at = pl.multiple_of(plan.down_row(part, chunk), seg)
+                value = out_ref[pl.ds(at, seg), e, :]
+                for down in range(plan.downs):
+                    pack[start + down * seg : start + (down + 1) * seg, :] = value[
+                        :, down * plan.wide : (down + 1) * plan.wide
                     ]
-        row = 2 * plan.tiles * shard
-        at = pl.multiple_of(plan.down_row(part, chunk), seg)
-        for down in range(plan.downs):
-            pack[row + down * seg : row + (down + 1) * seg, :] = out_ref[
-                pl.ds(at, seg), down * plan.wide : (down + 1) * plan.wide
-            ]
-
-
-def pack_pieces(plan, part, own_in, own_out):
+
+
+def pack_pieces(plan, who, expert_in, expert_out, after):
     if plan.seg % LANES == 0:
-        vmem = pl.BlockSpec(memory_space=pltpu.VMEM)
-        return pl.pallas_call(
+        per = plan.hidden // plan.shards
+        return launch(
             partial(pack_kernel, plan),
-            in_specs=[SMEM, vmem, vmem],
-            out_specs=[vmem] * plan.chunks,
-            out_shape=[jax.ShapeDtypeStruct((plan.rows, plan.wide), bf16)] * plan.chunks,
-            compiler_params=pltpu.CompilerParams(vmem_limit_bytes=VMEM_BYTES),
+            [who, expert_in, expert_out],
+            [
+                SMEM,
+                pl.BlockSpec((plan.shard, EXPERTS, per), lambda i: (0, 0, i)),
+                whole(expert_out.shape),
+            ],
+            whole((plan.chunks * plan.rows, plan.wide)),
+            jax.ShapeDtypeStruct((plan.chunks * plan.rows, plan.wide), bf16),
+            after,
+            grid=(2 * plan.shards,),
+            compiler_params=params(),
+            cost_estimate=cost(0, 0),
             name="pack",
-        )(part, own_in, own_out)
+        )
+    mine, part = who[0], who[1:]
+    own_in = lax.dynamic_index_in_dim(expert_in, mine, 1, keepdims=False)
+    own_out = lax.dynamic_index_in_dim(expert_out, mine, 1, keepdims=False)
     packs = []
     for chunk in range(plan.chunks):
         blocks = []
@@ -621,7 +647,7 @@
         rows = lax.dynamic_slice_in_dim(own_out, plan.down_row(part[0], chunk), plan.seg, 0)
         blocks += [rows[:, d * plan.wide : (d + 1) * plan.wide] for d in range(plan.downs)]
         packs.append(jnp.concatenate(blocks, axis=0))
-    return packs
+    return jnp.concatenate(packs, axis=0)
 
 
 def unpack_kernel(plan, begun, who_ref, *refs):
@@ -849,13 +875,17 @@
         copy.wait()
 
 
-def expert_call(plan, xs, ys, weights, carried, last):
-    first = carried is None
+def expert_call(plan, xs, ys, weights, chunk, carried):
+    first, last = chunk == 0, chunk == plan.chunks - 1
     rows = EXPERTS * CAP
-    vmem = pl.BlockSpec(memory_space=pltpu.VMEM)
     hbm = pl.BlockSpec(memory_space=pl.ANY)
     copies = plan.copies
-    in_specs = [vmem] * (2 * EXPERTS + copies)
+    block = pl.BlockSpec(
+        (plan.shards, plan.rows, plan.wide),
+        lambda i: (0, chunk, 0),
+        pipeline_mode=pl.Buffered(1),
+    )
+    in_specs = [whole(a.shape) for a in (*xs, *ys)] + [block] * copies
     operands = list(xs) + list(ys) + list(weights)
     if not first:
         in_specs += [hbm] * 2
@@ -863,7 +893,8 @@
     out_specs = [hbm] * copies
     out_shape = [jax.ShapeDtypeStruct((plan.shards, plan.rows, plan.wide), bf16)] * copies
     if last:
-        out_specs += [vmem] * (2 * EXPERTS)
+        out_specs += [whole((CAP + EXTRA, D))] * EXPERTS
+        out_specs += [whole((CAP, D))] * EXPERTS
         out_shape += [jax.ShapeDtypeStruct((CAP + EXTRA, D), bf16)] * EXPERTS
         out_shape += [jax.ShapeDtypeStruct((CAP, D), bf16)] * EXPERTS
     else:
@@ -890,7 +921,8 @@
             pltpu.VMEM((copies, plan.shards, plan.rows, plan.wide), bf16),
             pltpu.SemaphoreType.DMA((4 + copies,)),
         ],
-        compiler_params=pltpu.CompilerParams(vmem_limit_bytes=VMEM_BYTES),
+        grid=(1,),
+        compiler_params=params(),
         cost_estimate=cost(
             18 * rows * D * plan.width * copies, 12 * D * plan.width * copies + 12 * rows * D
         ),
@@ -1085,52 +1117,81 @@
     )
 
 
-def dense_kernel(copies, part_ref, h_ref, ctx_ref, dq_ref, dk_ref, dv_ref, branch_ref, *outs):
-    cut = 4 * D // copies
-    ht = h_ref[...].astype(f32).T.astype(bf16)
-    ct = ctx_ref[...].astype(f32).T.astype(bf16)
-    step = 384
-    for index, (left, right) in enumerate(
-        ((ht, dq_ref), (ht, dk_ref), (ht, dv_ref), (ct, branch_ref))
-    ):
-        for c in range(0, D, step):
-            made = mm(left, right[:, c : c + step]).astype(bf16)
-            at = index * D + c
-            done = 0
-            while done < step:
-                owner, column = (at + done) // cut, (at + done) % cut
-                size = min(step - done, cut - column)
-                for m in range(copies):
-
-                    @pl.when(part_ref[0] == (owner ^ m))
-                    def _(m=m, column=column, size=size, piece=made[:, done : done + size]):
-                        outs[m][:, column : column + size] = piece
-
-                done += size
-
-
-def dense_call(copies, part, h, ctx, dq, dk, dv, branch, after):
-    rows = h.shape[0]
-    return launch(
-        partial(dense_kernel, copies),
-        [part, h, ctx, dq, dk, dv, branch],
-        [SMEM] + [VM] * 6,
-        [VM] * copies,
-        [jax.ShapeDtypeStruct((D, 4 * D // copies), bf16)] * copies,
-        after,
+def turn_kernel(count, *refs):
+    for source, out in zip(refs[:count], refs[count:], strict=True):
+        out[...] = source[...].astype(f32).T.astype(bf16)
+
+
+def turn_call(arrays):
+    rows, columns = arrays[0].shape
+    return launch(
+        partial(turn_kernel, len(arrays)),
+        arrays,
+        [pl.BlockSpec((rows, 256), lambda i: (0, i))] * len(arrays),
+        [pl.BlockSpec((256, rows), lambda i: (i, 0))] * len(arrays),
+        [jax.ShapeDtypeStruct((columns, rows), bf16)] * len(arrays),
+        grid=(columns // 256,),
+        compiler_params=params(),
+        cost_estimate=cost(0, 0),
+        name="turn",
+    )
+
+
+def dense_kernel(copies, per, part_ref, ht_ref, ct_ref, *refs):
+    rights, outs = refs[:4], refs[4:]
+    step = pl.program_id(0)
+    source = ((step // per) ^ part_ref[0]) * per + step % per
+    for index, right in enumerate(rights):
+        left = ct_ref if index == 3 else ht_ref
+        for m in range(copies):
+
+            @pl.when((source // 2 == index) & (step // per == m))
+            def _(left=left, right=right, m=m):
+                outs[m][...] = mm(left[...], right[...]).astype(bf16)
+
+
+def dense_call(copies, part, ht, ct, dq, dk, dv, branch):
+    rows = ht.shape[1]
+    half = D // 2
+    per = 8 // copies
+
+    def right_block(index):
+        def block(i, part_ref):
+            source = ((i // per) ^ part_ref[0]) * per + i % per
+            return (0, jnp.clip(source - 2 * index, 0, 1))
+
+        return block
+
+    def out_block(m):
+        return lambda i, part_ref: (0, jnp.clip(i - m * per, 0, per - 1))
+
+    def fixed(shape):
+        return pl.BlockSpec(shape, lambda i, part_ref: (0, 0), pipeline_mode=pl.Buffered(1))
+
+    return pl.pallas_call(
+        partial(dense_kernel, copies, per),
+        grid_spec=pltpu.PrefetchScalarGridSpec(
+            num_scalar_prefetch=1,
+            grid=(8,),
+            in_specs=[fixed(ht.shape), fixed(ct.shape)]
+            + [pl.BlockSpec((rows, half), right_block(index)) for index in range(4)],
+            out_specs=[pl.BlockSpec((D, half), out_block(m)) for m in range(copies)],
+        ),
+        out_shape=[jax.ShapeDtypeStruct((D, 4 * D // copies), bf16)] * copies,
+        compiler_params=params(),
         cost_estimate=cost(8 * rows * D * D, 12 * rows * D + 8 * D * D),
         name="dense_grads",
-    )
+    )(part, ht, ct, dq, dk, dv, branch)
 
 
 def fold_parts_kernel(who_ref, *refs):
     pieces, outs = refs[:-EXPERTS], refs[-EXPERTS:]
     for k in range(EXPERTS):
         at = who_ref[0] ^ k
-        total = pieces[0][:, at].astype(f32)
+        total = pieces[0][0, at].astype(f32)
         for piece in pieces[1:]:
-            total = total + piece[:, at].astype(f32)
-        outs[k][...] = total.astype(bf16)
+            total = total + piece[0, at].astype(f32)
+        outs[k][0] = total.astype(bf16)
 
 
 def fold_parts(who, pieces, shards):
@@ -1141,9 +1202,11 @@
     return launch(
         fold_parts_kernel,
         operands,
-        [SMEM] + [VM] * len(pieces),
-        [VM] * EXPERTS,
+        [SMEM] + [pl.BlockSpec((1, EXPERTS, quarter, cut), lambda i: (i, 0, 0, 0))] * len(pieces),
+        [pl.BlockSpec((1, quarter, cut), lambda i: (i, 0, 0))] * EXPERTS,
         [jax.ShapeDtypeStruct((shards, quarter, cut), bf16)] * EXPERTS,
+        grid=(shards,),
+        compiler_params=params(),
         name="fold_parts",
     )
 
@@ -1202,19 +1265,10 @@
 
 
 def fold_copies(pieces):
-    shards, rows, wide = pieces[0].shape
-    block = pl.BlockSpec((1, rows // 2, wide), lambda i: (i // 2, i % 2, 0))
-    return launch(
-        fold_shards_kernel,
-        pieces,
-        [block] * len(pieces),
-        block,
-        jax.ShapeDtypeStruct(pieces[0].shape, bf16),
-        grid=(2 * shards,),
-        compiler_params=params(),
-        cost_estimate=cost(0, 0),
-        name="fold_copies",
-    )
+    total = pieces[0].astype(f32)
+    for piece in pieces[1:]:
+        total = total + piece.astype(f32)
+    return total.astype(bf16)
 
 
 def fold_shards_kernel(*refs):
@@ -1236,7 +1290,9 @@
 
 
 def unpack_dense_kernel(count, rows, part_ref, *refs):
-    pieces, (qkv_ref, proj_ref, small_ref) = refs[:count], refs[count:]
+    pieces = refs[:count]
+    qkv_ref, proj_ref, router_ref, mix_ref, cvec_ref, gain_a_ref, gain_f_ref, prev_ref = refs[count:-1]
+    small_ref = refs[-1]
     cut = pieces[0].shape[1]
     small = pieces[0][rows:, :].astype(f32)
     for piece in pieces[1:]:
@@ -1244,6 +1300,13 @@
     spare = small.shape[0]
     for c in range(cut // LANES):
         small_ref[c * spare : (c + 1) * spare, :] = small[:, c * LANES : (c + 1) * LANES]
+    turned = small_ref[...].T
+    router_ref[...] = turned[:NCH]
+    mix_ref[...] = turned[NCH:CVEC]
+    cvec_ref[...] = turned[CVEC:GAIN_A]
+    gain_a_ref[...] = turned[GAIN_A:GAIN_F]
+    gain_f_ref[...] = turned[GAIN_F : GAIN_F + 1]
+    prev_ref[...] = small_ref[: prev_ref.shape[0], 16 : 16 + NCH]
     for p in range(count):
         chosen = pieces[0][:rows, :].astype(f32)
         for m in range(1, count):
@@ -1257,17 +1320,17 @@
             proj_ref[:, at : at + cut - in_qkv] = chosen[:, in_qkv:]
 
 
-def unpack_dense(part, pieces, rows):
+def unpack_dense(part, pieces, rows, owned):
+    heights = (NCH, 4, 2, 1, 1)
     return launch(
         partial(unpack_dense_kernel, len(pieces), rows),
         [part, *pieces],
         [SMEM] + [VM] * len(pieces),
-        [VM] * 3,
-        [
-            jax.ShapeDtypeStruct((rows, 3 * D), f32),
-            jax.ShapeDtypeStruct((rows, D), f32),
-            jax.ShapeDtypeStruct((rows, LANES), f32),
-        ],
+        [VM] * 8,
+        [jax.ShapeDtypeStruct((rows, 3 * D), f32), jax.ShapeDtypeStruct((rows, D), f32)]
+        + [jax.ShapeDtypeStruct((height, rows), f32) for height in heights]
+        + [jax.ShapeDtypeStruct((owned, NCH), f32)],
+        scratch_shapes=[pltpu.VMEM((rows, LANES), f32)],
         name="unpack_dense",
     )
 
@@ -1402,27 +1465,9 @@
 
     width = 3 * D // copies
     owned = prev_mix.shape[0]
-    smalls = jnp.concatenate(
-        [
-            router.T,
-            const_mix.T,
-            const_vec.T,
-            gain_attn[None],
-            gain_ffn[None],
-            jnp.pad(prev_mix, ((0, 16 - owned), (0, shard - NCH))),
-        ]
-    )
-    piece, mine_late = cut_dense(who, qkv_weight, proj_weight, smalls, copies)
+    smalls = [router.T, const_mix.T, const_vec.T, gain_attn[None], gain_ffn[None], prev_mix]
+    piece, mark = cut_dense(who, qkv_weight, proj_weight, smalls, copies)
     spun = [piece] + [spin(piece, k) for k in range(1, shards)]
-
-    own_in = lax.dynamic_index_in_dim(expert_in, mine_late[0], 1, keepdims=False)
-    own_out = lax.dynamic_index_in_dim(expert_out, mine_late[0], 1, keepdims=False)
-    packs = pack_pieces(plan, part_s, own_in, own_out)
-    gathered = [lax.all_gather(p, "fsdp", axis=0, tiled=False) for p in packs]
-
-    def weights_after(chunk, done):
-        full = tie(gathered[chunk], done)
-        return [full] + [to_part(full, m) for m in range(1, copies)]
 
     docs = doc_ids.reshape(-1)
     drow = docs[None, :]
@@ -1449,8 +1494,11 @@
     places = jnp.sum(jnp.where(hit, (kinds[:, None] * CAP + rank)[None], 0), axis=1)
     places = jnp.where(chosen < EXPERTS, places, -1).T
 
+    tables = (cosine, sine, spot, dcol, vcol, places)
+    packed = pack_pieces(plan, who, expert_in, expert_out, (to_part(mark, 1),))
+    gathered = lax.all_gather(packed, "fsdp", axis=0, tiled=False)
     qkv_part, proj_part, small, prevs = lay_shards(
-        zi_s, spun, shard, quarter, width, (packs[0],)
+        zi_s, spun, shard, quarter, width, (packed,)
     )
     pmix = prevs[:, :owned].reshape(NCH, LANES)
 
@@ -1465,7 +1513,7 @@
         return [by_xor(pieces, part, 1)]
 
     qkv_half = lay_xor(
-        mine_s, exchanged([qkv_part] * EXPERTS), (cosine, sine, spot, dcol, vcol, places)
+        mine_s, exchanged([qkv_part] * EXPERTS), tables
     )
     qkv_pieces = over_parts(qkv_half)
     part_q = part_s if len(qkv_pieces) == copies else jnp.zeros_like(part_s)
@@ -1487,10 +1535,11 @@
     )
 
     xs = dispatch_call(mine_s, spot, h2, gates)
-    weights = [weights_after(0, ctx)] + [
-        weights_after(c, xs[0]) for c in range(1, plan.chunks)
-    ]
+    gathered = tie(gathered, xs[0])
+    weights = [gathered] + [to_part(gathered, m) for m in range(1, copies)]
+    h1_t, ctx_t = turn_call([tie(h1, xs[0]), ctx])
     xs = exchanged(xs)
+    weights[0] = tie(weights[0], h1_t)
     carried = None
     chunk_grads = []
     for chunk in range(plan.chunks):
@@ -1498,9 +1547,9 @@
             plan,
             xs,
             ys,
-            weights[chunk] if chunk else tie(weights[0], weights[1:]),
+            weights,
+            chunk,
             carried,
-            chunk == plan.chunks - 1,
         )
         chunk_grads.append(grads)
     dx = exchanged(carried[:EXPERTS])
@@ -1508,7 +1557,7 @@
     chunk_grads = [
         [grads[0]] + [to_part(grads[m], m) for m in range(1, copies)] for grads in chunk_grads
     ]
-    total = fold_copies(chunk_grads[0])
+    total = fold_copies(tie(chunk_grads[0], carried[0]))
 
     def over_shards(t):
         return lax.psum_scatter(t, "fsdp", scatter_dimension=0, tiled=False)
@@ -1535,12 +1584,15 @@
     spread = [[first] + [to_expert(first, k) for k in range(1, EXPERTS - 1)]]
     dq, dk, dv = attend_back_call(q, k, v, dctx, lse, dcol, drow, vcol, cosine, sine, ())
     dense = dense_call(
-        copies, part_s, h1, ctx, tie(dq, ret, spread[0]), dk, dv, branch, ()
+        copies, part_s, h1_t, ctx_t, tie(dq, ret, spread[0]), dk, dv, branch
     )
     spread[0].append(to_expert(tie(first, dq), EXPERTS - 1))
     dense = tie(list(dense), summed[1:])
+    for piece in summed[1:]:
+        piece = tie(piece, dense[0])
+        spread.append([piece] + [to_expert(piece, k) for k in range(1, EXPERTS - 1)])
     dense = [dense[0]] + [to_part(dense[m], m) for m in range(1, copies)]
-    quarters = tie(fold_parts(who, dense, shards), spread[0])
+    quarters = fold_parts(who, dense, shards)
 
     def over_copies(pieces):
         stacked = jnp.stack(pieces)
@@ -1564,29 +1616,31 @@
     if plan.seg % LANES == 0:
         begun = unpack_chunk(plan, who, 0, spread[0], begun)
     out = finish_call(res, one, places, routes, small, tie(ret, quarters), ())
-    bands = fold_quarters(zi_s, smalls, exchanged(quarters), (*begun, out))
-    tail = fold_shards([bands[0]] + [spin(bands[k], k) for k in range(1, shards)])
-    for piece in summed[1:]:
-        piece = tie(piece, bands)
-        late = [to_expert(tie(piece, tail), k) for k in range(EXPERTS - 1, EXPERTS)]
-        spread.append([piece] + [to_expert(piece, k) for k in range(1, EXPERTS - 1)] + late)
-    tail = lay_tail(mine_s, exchanged([tail] * EXPERTS), quarter, ())
-    spread[1:] = [over_copies(tie(pieces, tail)) for pieces in spread[1:]]
+    near = [pieces[1:] for pieces in spread[1:]]
+    bands = fold_quarters(zi_s, smalls, exchanged(quarters), (*begun, out, *near[0]))
+    for pieces in spread[1:]:
+        pieces.append(to_expert(tie(pieces[0], bands), EXPERTS - 1))
+    spun = [bands[0]] + [spin(bands[k], k) for k in range(1, shards)]
+    spread[1:] = [over_copies(tie(pieces, spun)) for pieces in spread[1:]]
+    tail = fold_shards(spun)
+    full_in, full_out = unpack_grads(plan, who, spread, begun)
+    tail = lay_tail(mine_s, exchanged([tail] * EXPERTS), quarter, (full_out,))
     tails = [tail] + [to_part(tail, m) for m in range(1, copies)]
-    qkv_grad, proj_grad, small_grad = unpack_dense(part_s, tails, shard)
-
-    full_in, full_out = unpack_grads(plan, who, spread, begun)
+    qkv_grad, proj_grad, router_t, mix_t, cvec_t, gain_a, gain_f, prev_out = unpack_dense(
+        part_s, tails, shard, owned
+    )
+
     return (
         out,
         input_grad,
         qkv_grad,
         proj_grad,
-        small_grad[:, GAIN_A],
-        small_grad[:, GAIN_F],
-        small_grad[:, :NCH],
-        small_grad[:, NCH : NCH + 4],
-        small_grad[:owned, 16 : 16 + NCH],
-        small_grad[:, CVEC : CVEC + 2],
+        gain_a[0],
+        gain_f[0],
+        router_t.T,
+        mix_t.T,
+        prev_out,
+        cvec_t.T,
         full_in,
         full_out,
     )

time: 552 us -> 474 us (0.86)
  waiting for transfers between devices: 139 us -> 94.9 us
  local copies, waits for them, and re-layouts: 51.2 us -> 24.9 us
  starting transfers between devices: 55.6 us -> 44.2 us
  other arithmetic: 6.56 us -> 14.8 us
    ppermute x27, waiting for transfers between devices: 93.8 us -> 76 us  [to_expert(): lax.ppermute(a, 'rep', [(i, i ^ k * copies) for i in range(replicas)])]
    pallas_call x23 -> x22, Pallas kernels: 201 us -> 188 us  [launch(): pl.pallas_call(run, in_specs=list(in_specs) + [pl.BlockSpec(memory_space=...]
    ppermute x6, waiting for transfers between devices: 24.8 us -> 12.1 us  [spin(): lax.ppermute(a, 'fsdp', [(i, (i + k) % shards) for i in range(shards)])]
    pallas_call x1, Pallas kernels: 2.87 us -> 13.7 us  [dense_call(): pl.pallas_call(partial(dense_kernel, copies, per), grid_spec=pltpu.Prefet...]
    ppermute x6, starting transfers between devices: 21.5 us -> 10.8 us  [spin(): lax.ppermute(a, 'fsdp', [(i, (i + k) % shards) for i in range(shards)])]
    unnamed x103 -> x98, local copies, waits for them, and re-layouts: 23.6 us -> 14.7 us
    ppermute x10, waiting for transfers between devices: 15.3 us -> 6.77 us  [to_part(): return lax.ppermute(a, 'rep', [(i, i ^ m) for i in range(replicas)])]
    dynamic_slice x2 -> x0, local copies, waits for them, and re-layouts: 8.14 us -> none  [the longest x1 6.52 us: body(): lax.dynamic_index_in_dim(expert_in, mine_late[0], 1, keepdims=False)]
  transfers between devices with their start and end apart: 47 -> 46, of which waited for: 26 -> 18; matrix products, arithmetic and copies ran while one was open for 4% -> 4% of each run, Pallas kernels for 39% -> 49%
where the time goes in v2:
time: 474 us; the launch traced here: 465 us
  Pallas kernels  271 us (57%)
  waiting for transfers between devices  94.9 us (20%)
  starting transfers between devices  44.2 us (9%)
  local copies, waits for them, and re-layouts  24.9 us (5%)
  other arithmetic  14.8 us (3%)
  between operations  14.8 us (3%)
    pallas_call x22, Pallas kernels, launch(): pl.pallas_call(run, in_specs=list(in_specs) + [pl.BlockSpec(memory_space=...  188 us
    ppermute x27, waiting for transfers between devices, to_expert(): lax.ppermute(a, 'rep', [(i, i ^ k * copies) for i in range(replicas)])  76 us
    pallas_call x2, Pallas kernels, expert_call(): pl.pallas_call(partial(expert_kernel, plan, first, last), in_specs=in_spe...  68.5 us
    ppermute x27, starting transfers between devices, to_expert(): lax.ppermute(a, 'rep', [(i, i ^ k * copies) for i in range(replicas)])  32.1 us
    unnamed x98, local copies, waits for them, and re-layouts  14.7 us
    pallas_call x1, Pallas kernels, dense_call(): pl.pallas_call(partial(dense_kernel, copies, per), grid_spec=pltpu.Prefet...  13.7 us
    ppermute x6, waiting for transfers between devices, spin(): lax.ppermute(a, 'fsdp', [(i, (i + k) % shards) for i in range(shards)])  12.1 us
    ppermute x6, starting transfers between devices, spin(): lax.ppermute(a, 'fsdp', [(i, (i + k) % shards) for i in range(shards)])  10.8 us
  transfers between devices with their start and end apart: 46, of which 18 were waited for; matrix products, arithmetic and copies ran while one was open for 4% of the time, Pallas kernels for 49%

profile of v2, /device:TPU:0, one launch (start us, length us, event | category | flops | bytes accessed | tf_op | source)
XLA Modules:
  0.0 465.0 jit_solution(5780503183426552122)
XLA Ops:
  10.3 2.0 cut_dense.1
  12.3 5.0 %collective-permute-start.2 = (bf16[64,1536]{1,0:T(8,128)(2,1)}, bf16[64,1536]{1,0:T(8,128)(2,1)S(1)}, u32[]{:S(2)}, u32[]{:S(2)}) collective-permute-start(bf16[64,1536]{1,0:T(8,128)(2,1)} %get-tuple-element.117.refs_1_), channel_id=1, source_target_pairs={{0,3},{1,0},{2,1},{3,2},{4,7},{5,4},{6,5},{7,6},{8,11},{9,8},{10,9... | collective-permute-start | bytes 589832 | tf_op jit(solution)/shard_map/ppermute | solution.py:1455
  20.4 1.9 fusion.9
  22.9 9.6 %pack.1.refs_5_ = bf16[2304,256]{1,0:T(8,128)(2,1)} custom-call(s32[2]{0:T(128)} %pad_add_fusion.refs_0_, bf16[192,4,4096]{2,1,0:T(4,128)(2,1)} %refs_1_.4, bf16[512,4,768]{2,1,0:T(4,128)(2,1)} %refs_2_.5, bf16[16,128]{1,0:T(8,128)(2,1)} %copy-done.42), custom_call_target="tpu_custom_call" | custom-call | tf_op jit(solution)/shard_map/pack/pallas_call | solution.py:62
  35.0 2.1 lay_shards.1
  37.1 2.4 collective-permute-start.6
  43.5 1.9 pad_maximum_fusion.2
  46.2 5.0 %collective-permute-done.6.refs_4_ = bf16[4,48,1152]{2,1,0:T(8,128)(2,1)S(1)} collective-permute-done((bf16[4,48,1152]{2,1,0:T(8,128)(2,1)}, bf16[4,48,1152]{2,1,0:T(8,128)(2,1)S(1)}, u32[]{:S(2)}, u32[]{:S(2)}) %collective-permute-start.6) | collective-permute-done | bytes 442400 | tf_op jit(solution)/shard_map/ppermute | solution.py:1449
  51.3 8.7 %collective-permute-done.5.refs_3_ = bf16[4,48,1152]{2,1,0:T(8,128)(2,1)} collective-permute-done((bf16[4,48,1152]{2,1,0:T(8,128)(2,1)}, bf16[4,48,1152]{2,1,0:T(8,128)(2,1)}, u32[]{:S(2)}, u32[]{:S(2)}) %collective-permute-start.5) | collective-permute-done | bytes 442400 | tf_op jit(solution)/shard_map/ppermute | solution.py:1449
  60.1 2.8 lay_xor.1.refs_4_
  63.7 5.6 %dispatch.2 = (bf16[480,768]{1,0:T(8,128)(2,1)}, bf16[480,768]{1,0:T(8,128)(2,1)}, bf16[480,768]{1,0:T(8,128)(2,1)}, bf16[480,768]{1,0:T(8,128)(2,1)}) custom-call(s32[1]{0:T(128)} %bitcast.2.refs_0_, s32[4,1024]{1,0:T(4,128)} %get-tuple-element.223.refs_7_.refs_1_, bf16[1024,768]{1,0:T(8,128)(2,1)} %refs_3_.2, bf16[96,768]{1,0:T(8,128)(2,1)} %bitcast.62, ...), custom_call_target="tpu_custom_call" | custom-call | flops 48318384 | bytes 78643 | tf_op jit(solution)/shard_map/dispatch/pallas_call | solution.py:62
  74.1 8.8 %qkv_rope.1 = (bf16[1024,768]{1,0:T(8,128)(2,1)}, bf16[1024,768]{1,0:T(8,128)(2,1)}, bf16[1024,768]{1,0:T(8,128)(2,1)}, bf16[1024,768]{1,0:T(8,128)(2,1)}) custom-call(s32[1]{0:T(128)} %bitcast.refs_0_.part_ref, bf16[1024,768]{1,0:T(8,128)(2,1)} %refs_4_.3, bf16[128,768]{1,0:T(8,128)(2,1)} %get-tuple-element.119.refs_2_.refs_3_.refs_8_.refs_4_.refs_6_, ...), custom_call_target="tpu_custom_call" | custom-call | flops 72477576 | bytes 228065 | tf_op jit(solution)/shard_map/qkv_rope/pallas_call | solution.py:62
  82.9 25.8 %attend.1 = (bf16[1024,768]{1,0:T(8,128)(2,1)}, f32[6,2,1024]{2,1,0:T(2,128)}) custom-call(bf16[1024,768]{1,0:T(8,128)(2,1)} %get-tuple-element.123.refs_0_, bf16[1024,768]{1,0:T(8,128)(2,1)} %get-tuple-element.124.refs_1_, bf16[1024,768]{1,0:T(8,128)(2,1)} %get-tuple-element.125.refs_2_, s32[1024,1]{1,0:T(8,128)} %copy.73.refs_8_.refs_3_.refs_5_, ...), custom_call_target="tpu_custom_call" | custom-call | flops 40000000000 | bytes 12582912 | tf_op jit(solution)/shard_map/attend/pallas_call | solution.py:62
  110.0 2.6 lay_riders.1
  115.7 8.2 %after_attention.1 = (f32[1024,768]{1,0:T(8,128)}, bf16[1024,768]{1,0:T(8,128)(2,1)}, f32[1024,128]{1,0:T(8,128)}, bf16[16,1024]{1,0:T(8,128)(2,1)}) custom-call(s32[1]{0:T(128)} %bitcast.refs_0_.part_ref, bf16[1024,768]{1,0:T(8,128)(2,1)} %get-tuple-element.126.refs_5_.refs_1_, bf16[1024,768]{1,0:T(8,128)(2,1)} %refs_4_.3, ...), custom_call_target="tpu_custom_call" | custom-call | flops 24159192 | bytes 157286 | tf_op jit(solution)/shard_map/after_attention/pallas_call | solution.py:62
  123.9 6.0 %dispatch.3 = (bf16[400,768]{1,0:T(8,128)(2,1)}, bf16[400,768]{1,0:T(8,128)(2,1)}, bf16[400,768]{1,0:T(8,128)(2,1)}, bf16[400,768]{1,0:T(8,128)(2,1)}) custom-call(s32[1]{0:T(128)} %bitcast.2.refs_0_, s32[4,1024]{1,0:T(4,128)} %get-tuple-element.223.refs_7_.refs_1_, bf16[1024,768]{1,0:T(8,128)(2,1)} %get-tuple-element.133.refs_2_, ...), custom_call_target="tpu_custom_call" | custom-call | flops 48318384 | bytes 78643 | tf_op jit(solution)/shard_map/dispatch/pallas_call | solution.py:62
  133.6 4.6 turn.1
  138.2 8.8 %collective-permute-done.12.refs_1_ = bf16[400,768]{1,0:T(8,128)(2,1)S(1)} collective-permute-done((bf16[400,768]{1,0:T(8,128)(2,1)}, bf16[400,768]{1,0:T(8,128)(2,1)S(1)}, u32[]{:S(2)}, u32[]{:S(2)}) %collective-permute-start.12) | collective-permute-done | bytes 614432 | tf_op jit(solution)/shard_map/ppermute | solution.py:1449
  147.0 13.8 %collective-permute-done.13.refs_2_ = bf16[400,768]{1,0:T(8,128)(2,1)S(1)} collective-permute-done((bf16[400,768]{1,0:T(8,128)(2,1)}, bf16[400,768]{1,0:T(8,128)(2,1)S(1)}, u32[]{:S(2)}, u32[]{:S(2)}) %collective-permute-start.13) | collective-permute-done | bytes 614432 | tf_op jit(solution)/shard_map/ppermute | solution.py:1449
  161.7 2.2 copy-done
  163.8 32.1 %experts.2 = (bf16[4,1152,256]{2,1,0:T(8,128)(2,1)}, bf16[4,1152,256]{2,1,0:T(8,128)(2,1)}, f32[1536,768]{1,0:T(8,128)}, f32[1536,768]{1,0:T(8,128)}) custom-call(bf16[400,768]{1,0:T(8,128)(2,1)} %get-tuple-element.135.refs_0_, bf16[400,768]{1,0:T(8,128)(2,1)} %copy-done.10, bf16[400,768]{1,0:T(8,128)(2,1)} %copy-done.11, ...), custom_call_target="tpu_custom_call" | custom-call | flops 434865440 | bytes 471859 | tf_op jit(solution)/shard_map/experts/pallas_call | solution.py:903
  196.1 36.4 %experts.3 = (bf16[4,1152,256]{2,1,0:T(8,128)(2,1)}, bf16[4,1152,256]{2,1,0:T(8,128)(2,1)}, bf16[400,768]{1,0:T(8,128)(2,1)}, bf16[400,768]{1,0:T(8,128)(2,1)}, ...) custom-call(bf16[400,768]{1,0:T(8,128)(2,1)} %get-tuple-element.135., ...), custom_call_target="tpu_custom_call" | custom-call | flops 434865440 | bytes 471859 | tf_op jit(solution)/shard_map/experts/pallas_call | solution.py:903
  232.5 2.0 add_convert_fusion.1.refs_15_
  239.0 13.2 %collective-permute-done.16.refs_10_ = bf16[400,768]{1,0:T(8,128)(2,1)S(1)} collective-permute-done((bf16[400,768]{1,0:T(8,128)(2,1)S(1)}, bf16[400,768]{1,0:T(8,128)(2,1)S(1)}, u32[]{:S(2)}, u32[]{:S(2)}) %collective-permute-start.16) | collective-permute-done | bytes 614432 | tf_op jit(solution)/shard_map/ppermute | solution.py:1449
  252.4 12.7 %collective-permute-done.18.refs_12_ = bf16[400,768]{1,0:T(8,128)(2,1)S(1)} collective-permute-done((bf16[400,768]{1,0:T(8,128)(2,1)S(1)}, bf16[400,768]{1,0:T(8,128)(2,1)S(1)}, u32[]{:S(2)}, u32[]{:S(2)}) %collective-permute-start.18) | collective-permute-done | bytes 614432 | tf_op jit(solution)/shard_map/ppermute | solution.py:1449
  265.9 19.1 %combine_back.1 = (f32[1024,768]{1,0:T(8,128)}, bf16[1024,768]{1,0:T(8,128)(2,1)}, bf16[1024,768]{1,0:T(8,128)(2,1)}, f32[128,768]{1,0:T(8,128)}, f32[1,768]{1,0...) custom-call(s32[2]{0:T(128)} %pad_add_fusion.refs_0_, f32[1024,768]{1,0:T(8,128)} %get-tuple-element.131.refs_1_.refs_0_, ...), custom_call_target="tpu_custom_call" | custom-call | flops 88583696 | bytes 314572 | tf_op jit(solution)/shard_map/combine_back/pallas_call | solution.py:62
  285.1 1.9 add_convert_fusion
  287.0 1.8 collective-permute-start.20
  293.1 31.2 %attend_back.1 = (bf16[1024,768]{1,0:T(8,128)(2,1)}, bf16[1024,768]{1,0:T(8,128)(2,1)}, bf16[1024,768]{1,0:T(8,128)(2,1)}) custom-call(bf16[1024,768]{1,0:T(8,128)(2,1)} %get-tuple-element.123.refs_0_, bf16[1024,768]{1,0:T(8,128)(2,1)} %get-tuple-element.124.refs_1_, bf16[1024,768]{1,0:T(8,128)(2,1)} %get-tuple-element.125.refs_2_, ...), custom_call_target="tpu_custom_call" | custom-call | flops 900000000 | bytes 220200 | tf_op jit(solution)/shard_map/attend_back/pallas_call | solution.py:62
  324.3 4.3 collective-permute-done.24
  328.6 13.7 %dense_grads.1 = (bf16[768,1536]{1,0:T(8,128)(2,1)}, bf16[768,1536]{1,0:T(8,128)(2,1)}) custom-call(s32[1]{0:T(128)} %bitcast.refs_0_.part_ref, bf16[768,1024]{1,0:T(8,128)(2,1)} %get-tuple-element.142.ht_ref, bf16[768,1024]{1,0:T(8,128)(2,1)} %get-tuple-element.163.ct_ref, bf16[1024,768]{1,0:T(8,128)(2,1)} %get-tuple-element.168.refs_0_.refs_1_, ...), custom_call_target="tpu_custom_call" | custom-call | flops 96636768 | bytes 283115 | tf_op jit(solution)/shard_map/dense_grads/pallas_call | solution.py:1171
  344.1 3.1 collective-permute-done.26
  348.6 4.4 fold_parts.1
  352.9 6.2 %collective-permute-done.30 = bf16[1152,256]{1,0:T(8,128)(2,1)S(1)} collective-permute-done((bf16[1152,256]{1,0:T(8,128)(2,1)S(1)}, bf16[1152,256]{1,0:T(8,128)(2,1)S(1)}, u32[]{:S(2)}, u32[]{:S(2)}) %collective-permute-start.30) | collective-permute-done | bytes 589856 | tf_op jit(solution)/shard_map/ppermute | solution.py:1449
  368.7 7.7 %layer_out.1.refs_8_ = bf16[1024,768]{1,0:T(8,128)(2,1)} custom-call(f32[1024,768]{1,0:T(8,128)} %get-tuple-element.131.refs_1_.refs_0_, f32[1024,128]{1,0:T(8,128)} %get-tuple-element.132.refs_4_.refs_1_, s32[1024,2]{1,0:T(8,128)} %bitcast_select_fusion.refs_10_.refs_5_.refs_2_, s32[1024,2]{1,0:T(8,128)} %copy-done.1, ...), custom_call_target="tpu_custom_call" | custom-call | flops 48318384 | bytes 157286 | tf_op jit(solution)/shard_map/layer_out/pallas_call | solution.py:62
  376.4 10.4 %input_grad.1 = (bf16[1024,768]{1,0:T(8,128)(2,1)}, bf16[768,128]{1,0:T(8,128)(2,1)}) custom-call(s32[1]{0:T(128)} %bitcast.refs_0_.part_ref, bf16[1024,768]{1,0:T(8,128)(2,1)} %get-tuple-element.168.refs_0_.refs_1_, bf16[1024,768]{1,0:T(8,128)(2,1)} %get-tuple-element.169.refs_1_.refs_2_, bf16[1024,768]{1,0:T(8,128)(2,1)} %get-tuple-element.170.refs_2_.refs_3_, ...), custom_call_target="tpu_custom_call" | custom-call | flops 72477576 | bytes 220200 | tf_op jit(solution)/shard_map/input_grad/pallas_call | solution.py:62
  387.8 13.4 %unpack.2 = (f32[192,4,4096]{2,1,0:T(4,128)}, f32[512,4,768]{2,1,0:T(4,128)}) custom-call(s32[2]{0:T(128)} %pad_add_fusion.refs_0_, bf16[4,1152,256]{2,1,0:T(8,128)(2,1)} %copy-done.2, bf16[4,1152,256]{2,1,0:T(8,128)(2,1)} %copy-done.8, bf16[4,384,256]{2,1,0:T(8,128)(2,1)} %slice.20.refs_3_, bf16[4,384,256]{2,1,0:T(8,128)(2,1)} %slice.21.refs_4_), custom_call_target="tpu_custom_call" | custom-call | bytes 377487 | tf_op jit(solution)/shard_map/unpack/pallas_call | solution.py:62
  401.3 3.0 collective-permute-done.29.refs_5_
  404.2 2.7 fold_quarters.1
  408.5 2.3 collective-permute-start.34
  413.2 5.2 %collective-permute-done.34.refs_1_ = bf16[64,1536]{1,0:T(8,128)(2,1)S(1)} collective-permute-done((bf16[64,1536]{1,0:T(8,128)(2,1)}, bf16[64,1536]{1,0:T(8,128)(2,1)S(1)}, u32[]{:S(2)}, u32[]{:S(2)}) %collective-permute-start.34) | collective-permute-done | bytes 196640 | tf_op jit(solution)/shard_map/ppermute | solution.py:1455
  418.4 6.4 %collective-permute-done.35.refs_2_ = bf16[64,1536]{1,0:T(8,128)(2,1)S(1)} collective-permute-done((bf16[64,1536]{1,0:T(8,128)(2,1)}, bf16[64,1536]{1,0:T(8,128)(2,1)S(1)}, u32[]{:S(2)}, u32[]{:S(2)}) %collective-permute-start.35) | collective-permute-done | bytes 196640 | tf_op jit(solution)/shard_map/ppermute | solution.py:1455
  424.9 1.9 pad_maximum_fusion.1.refs_1_
  426.9 2.8 fold_shards.1.refs_1_
  435.7 13.4 %unpack.3 = (f32[192,4,4096]{2,1,0:T(4,128)}, f32[512,4,768]{2,1,0:T(4,128)}) custom-call(s32[2]{0:T(128)} %pad_add_fusion.refs_0_, bf16[4,1152,256]{2,1,0:T(8,128)(2,1)} %copy-done.3, bf16[4,1152,256]{2,1,0:T(8,128)(2,1)} %copy-done.9, bf16[4,384,256]{2,1,0:T(8,128)(2,1)} %slice.22.refs_3_, ...), custom_call_target="tpu_custom_call", output_to_operand_aliasing={{0}: (5, {}), {1}: (6, {})} | custom-call | bytes 377487 | tf_op jit(solution)/shard_map/unpack/pallas_call | solution.py:62
  449.9 2.1 lay_tail.1.refs_1_
  452.0 2.3 collective-permute-done.42.refs_2_
  455.1 2.9 unpack_dense.1
  (199 shorter events, 63.7 us)
Async XLA Ops:
  7.2 122.8 %all-gather.3.cloned.1.call-start = ((), (), s32[]{:S(2)}) async-start(), calls=%async_computation.4 | async-start | bytes 5898240 | tf_op jit(solution)/shard_map/all_gather | solution.py:1499
  12.3 21.4 %collective-permute-start.2 = (bf16[64,1536]{1,0:T(8,128)(2,1)}, bf16[64,1536]{1,0:T(8,128)(2,1)S(1)}, u32[]{:S(2)}, u32[]{:S(2)}) collective-permute-start(bf16[64,1536]{1,0:T(8,128)(2,1)} %get-tuple-element.117.refs_1_), channel_id=1, source_target_pairs={{0,3},{1,0},{2,1},{3,2},{4,7},{5,4},{6,5},{7,6},{8,11},{9,8},{10,9... | collective-permute-start | bytes 589832 | tf_op jit(solution)/shard_map/ppermute | solution.py:1455
  17.3 16.9 %collective-permute-start.1 = (bf16[64,1536]{1,0:T(8,128)(2,1)}, bf16[64,1536]{1,0:T(8,128)(2,1)S(1)}, u32[]{:S(2)}, u32[]{:S(2)}) collective-permute-start(bf16[64,1536]{1,0:T(8,128)(2,1)} %get-tuple-element.117.refs_1_), channel_id=1, source_target_pairs={{0,2},{1,3},{2,0},{3,1},{4,6},{5,7},{6,4},{7,5},{8,10},{9,11},{10,... | collective-permute-start | bytes 589832 | tf_op jit(solution)/shard_map/ppermute | solution.py:1455
  17.3 16.9 %collective-permute-start = (bf16[64,1536]{1,0:T(8,128)(2,1)}, bf16[64,1536]{1,0:T(8,128)(2,1)S(1)}, u32[]{:S(2)}, u32[]{:S(2)}) collective-permute-start(bf16[64,1536]{1,0:T(8,128)(2,1)} %get-tuple-element.117.refs_1_), channel_id=1, source_target_pairs={{0,1},{1,2},{2,3},{3,0},{4,5},{5,6},{6,7},{7,4},{8,9},{9,10},{10,1... | collective-permute-start | bytes 589832 | tf_op jit(solution)/shard_map/ppermute | solution.py:1455
  18.3 4.0 collective-permute-start.3
  32.5 258.1 %reduce-scatter.3.cloned.1.call-start = ((), (), s32[]{:S(2)}) async-start(), calls=%async_computation.2 | async-start | bytes 2949120 | tf_op jit(solution)/shard_map/reduce_scatter | solution.py:1563
  37.1 14.2 %collective-permute-start.6 = (bf16[4,48,1152]{2,1,0:T(8,128)(2,1)}, bf16[4,48,1152]{2,1,0:T(8,128)(2,1)S(1)}, u32[]{:S(2)}, u32[]{:S(2)}) collective-permute-start(bf16[4,48,1152]{2,1,0:T(8,128)(2,1)} %get-tuple-element.120.refs_1_), channel_id=1, source_target_pairs={{0,24},{4,28},{8,16},{12,20},{16,8},{20,12},{24,0},{28,4},{1,25},{... | collective-permute-start | bytes 1327112 | tf_op jit(solution)/shard_map/ppermute | solution.py:1449
  39.6 20.4 %collective-permute-start.5 = (bf16[4,48,1152]{2,1,0:T(8,128)(2,1)}, bf16[4,48,1152]{2,1,0:T(8,128)(2,1)}, u32[]{:S(2)}, u32[]{:S(2)}) collective-permute-start(bf16[4,48,1152]{2,1,0:T(8,128)(2,1)} %get-tuple-element.120.refs_1_), channel_id=1, source_target_pairs={{0,16},{4,20},{8,24},{12,28},{16,0},{20,4},{24,8},{28,12},{1,17},{... | collective-permute-start | bytes 1327112 | tf_op jit(solution)/shard_map/ppermute | solution.py:1449
  40.1 20.0 %collective-permute-start.4 = (bf16[4,48,1152]{2,1,0:T(8,128)(2,1)}, bf16[4,48,1152]{2,1,0:T(8,128)(2,1)}, u32[]{:S(2)}, u32[]{:S(2)}) collective-permute-start(bf16[4,48,1152]{2,1,0:T(8,128)(2,1)} %get-tuple-element.120.refs_1_), channel_id=1, source_target_pairs={{0,8},{4,12},{8,0},{12,4},{16,24},{20,28},{24,16},{28,20},{1,9},{5... | collective-permute-start | bytes 1327112 | tf_op jit(solution)/shard_map/ppermute | solution.py:1449
  62.9 9.9 %collective-permute-start.7 = (bf16[768,1152]{1,0:T(8,128)(2,1)}, bf16[768,1152]{1,0:T(8,128)(2,1)S(1)}, u32[]{:S(2)}, u32[]{:S(2)}) collective-permute-start(bf16[768,1152]{1,0:T(8,128)(2,1)} %bitcast.42), channel_id=1, source_target_pairs={{0,4},{4,0},{8,12},{12,8},{16,20},{20,16},{24,28},{28,24},{1,5},{5... | collective-permute-start | bytes 5308424 | tf_op jit(solution)/shard_map/ppermute | solution.py:1452
  69.3 39.4 %collective-permute-start.8 = (bf16[480,768]{1,0:T(8,128)(2,1)}, bf16[480,768]{1,0:T(8,128)(2,1)S(1)}, u32[]{:S(2)}, u32[]{:S(2)}) collective-permute-start(bf16[480,768]{1,0:T(8,128)(2,1)} %get-tuple-element.128), channel_id=1, source_target_pairs={{0,8},{4,12},{8,0},{12,4},{16,24},{20,28},{24,16},{28,20},{1,9},{5... | collective-permute-start | bytes 2211848 | tf_op jit(solution)/shard_map/ppermute | solution.py:1449
  70.8 37.9 %collective-permute-start.9 = (bf16[480,768]{1,0:T(8,128)(2,1)}, bf16[480,768]{1,0:T(8,128)(2,1)S(1)}, u32[]{:S(2)}, u32[]{:S(2)}) collective-permute-start(bf16[480,768]{1,0:T(8,128)(2,1)} %get-tuple-element.129), channel_id=1, source_target_pairs={{0,16},{4,20},{8,24},{12,28},{16,0},{20,4},{24,8},{28,12},{1,17},{... | collective-permute-start | bytes 2211848 | tf_op jit(solution)/shard_map/ppermute | solution.py:1449
  71.5 37.2 %collective-permute-start.10 = (bf16[480,768]{1,0:T(8,128)(2,1)}, bf16[480,768]{1,0:T(8,128)(2,1)S(1)}, u32[]{:S(2)}, u32[]{:S(2)}) collective-permute-start(bf16[480,768]{1,0:T(8,128)(2,1)} %get-tuple-element.130), channel_id=1, source_target_pairs={{0,24},{4,28},{8,16},{12,20},{16,8},{20,12},{24,0},{28,4},{1,25},{... | collective-permute-start | bytes 2211848 | tf_op jit(solution)/shard_map/ppermute | solution.py:1449
  112.7 2.2 collective-permute-start.11
  129.9 30.9 %collective-permute-start.15 = (bf16[4,2304,256]{2,1,0:T(8,128)(2,1)}, bf16[4,2304,256]{2,1,0:T(8,128)(2,1)S(1)}, u32[]{:S(2)}, u32[]{:S(2)}) collective-permute-start(bf16[4,2304,256]{2,1,0:T(8,128)(2,1)} %bitcast.45), channel_id=1, source_target_pairs={{0,4},{4,0},{8,12},{12,8},{16,20},{20,16},{24,28},{28,24},{1,5},{5... | collective-permute-start | bytes 14155784 | tf_op jit(solution)/shard_map/ppermute | solution.py:1452
  130.1 16.9 %collective-permute-start.12 = (bf16[400,768]{1,0:T(8,128)(2,1)}, bf16[400,768]{1,0:T(8,128)(2,1)S(1)}, u32[]{:S(2)}, u32[]{:S(2)}) collective-permute-start(bf16[400,768]{1,0:T(8,128)(2,1)} %get-tuple-element.136), channel_id=1, source_target_pairs={{0,8},{4,12},{8,0},{12,4},{16,24},{20,28},{24,16},{28,20},{1,9},{5... | collective-permute-start | bytes 1843208 | tf_op jit(solution)/shard_map/ppermute | solution.py:1449
  131.6 29.2 %collective-permute-start.13 = (bf16[400,768]{1,0:T(8,128)(2,1)}, bf16[400,768]{1,0:T(8,128)(2,1)S(1)}, u32[]{:S(2)}, u32[]{:S(2)}) collective-permute-start(bf16[400,768]{1,0:T(8,128)(2,1)} %get-tuple-element.137), channel_id=1, source_target_pairs={{0,16},{4,20},{8,24},{12,28},{16,0},{20,4},{24,8},{28,12},{1,17},{... | collective-permute-start | bytes 1843208 | tf_op jit(solution)/shard_map/ppermute | solution.py:1449
  132.3 28.5 %collective-permute-start.14 = (bf16[400,768]{1,0:T(8,128)(2,1)}, bf16[400,768]{1,0:T(8,128)(2,1)}, u32[]{:S(2)}, u32[]{:S(2)}) collective-permute-start(bf16[400,768]{1,0:T(8,128)(2,1)} %get-tuple-element.138), channel_id=1, source_target_pairs={{0,24},{4,28},{8,16},{12,20},{16,8},{20,12},{24,0},{28,4},{1,25},{... | collective-permute-start | bytes 1843208 | tf_op jit(solution)/shard_map/ppermute | solution.py:1449
  196.0 36.5 %collective-permute-start.19 = (bf16[4,1152,256]{2,1,0:T(8,128)(2,1)}, bf16[4,1152,256]{2,1,0:T(8,128)(2,1)S(1)}, u32[]{:S(2)}, u32[]{:S(2)}) collective-permute-start(bf16[4,1152,256]{2,1,0:T(8,128)(2,1)} %get-tuple-element.155), channel_id=1, source_target_pairs={{0,4},{4,0},{8,12},{12,8},{16,20},{20,16},{24,28},{28,24},{1,5},{5... | collective-permute-start | bytes 7077896 | tf_op jit(solution)/shard_map/ppermute | solution.py:1452
  196.0 36.4 %copy-start.14 = (bf16[4,1152,256]{2,1,0:T(8,128)(2,1)S(1)}, bf16[4,1152,256]{2,1,0:T(8,128)(2,1)}, u32[]{:S(2)}) copy-start(bf16[4,1152,256]{2,1,0:T(8,128)(2,1)} %get-tuple-element.156) | copy-start | bytes 7077892
  234.5 107.9 %reduce-scatter.5.cloned.1.call-start = ((), (), s32[]{:S(2)}) async-start(), calls=%async_computation.3 | async-start | bytes 2949120 | tf_op jit(solution)/shard_map/reduce_scatter | solution.py:1563
  234.5 50.5 %collective-permute-start.25 = (bf16[4,1152,256]{2,1,0:T(8,128)(2,1)}, bf16[4,1152,256]{2,1,0:T(8,128)(2,1)S(1)}, u32[]{:S(2)}, u32[]{:S(2)}) collective-permute-start(bf16[4,1152,256]{2,1,0:T(8,128)(2,1)} %get-tuple-element.174), channel_id=1, source_target_pairs={{0,4},{4,0},{8,12},{12,8},{16,20},{20,16},{24,28},{28,24},{1,5},{5... | collective-permute-start | bytes 7077896 | tf_op jit(solution)/shard_map/ppermute | solution.py:1452
  235.5 16.7 %collective-permute-start.16 = (bf16[400,768]{1,0:T(8,128)(2,1)S(1)}, bf16[400,768]{1,0:T(8,128)(2,1)S(1)}, u32[]{:S(2)}, u32[]{:S(2)}) collective-permute-start(bf16[400,768]{1,0:T(8,128)(2,1)S(1)} %copy-done.46), channel_id=1, source_target_pairs={{0,8},{4,12},{8,0},{12,4},{16,24},{20,28},{24,16},{28,20},{1,9},{5... | collective-permute-start | bytes 1843208 | tf_op jit(solution)/shard_map/ppermute | solution.py:1449
  235.7 16.7 %collective-permute-start.17 = (bf16[400,768]{1,0:T(8,128)(2,1)S(1)}, bf16[400,768]{1,0:T(8,128)(2,1)S(1)}, u32[]{:S(2)}, u32[]{:S(2)}) collective-permute-start(bf16[400,768]{1,0:T(8,128)(2,1)S(1)} %copy-done.45), channel_id=1, source_target_pairs={{0,16},{4,20},{8,24},{12,28},{16,0},{20,4},{24,8},{28,12},{1,17},{... | collective-permute-start | bytes 1843208 | tf_op jit(solution)/shard_map/ppermute | solution.py:1449
  237.5 27.6 %collective-permute-start.18 = (bf16[400,768]{1,0:T(8,128)(2,1)S(1)}, bf16[400,768]{1,0:T(8,128)(2,1)S(1)}, u32[]{:S(2)}, u32[]{:S(2)}) collective-permute-start(bf16[400,768]{1,0:T(8,128)(2,1)S(1)} %copy-done.44), channel_id=1, source_target_pairs={{0,24},{4,28},{8,16},{12,20},{16,8},{20,12},{24,0},{28,4},{1,25},{... | collective-permute-start | bytes 1843208 | tf_op jit(solution)/shard_map/ppermute | solution.py:1449
  287.0 37.2 %collective-permute-start.20 = (bf16[384,768]{1,0:T(8,128)(2,1)}, bf16[384,768]{1,0:T(8,128)(2,1)S(1)}, u32[]{:S(2)}, u32[]{:S(2)}) collective-permute-start(bf16[384,768]{1,0:T(8,128)(2,1)} %get-tuple-element.160), channel_id=1, source_target_pairs={{0,8},{4,12},{8,0},{12,4},{16,24},{20,28},{24,16},{28,20},{1,9},{5... | collective-permute-start | bytes 1769480 | tf_op jit(solution)/shard_map/ppermute | solution.py:1449
  288.9 35.4 %collective-permute-start.21 = (bf16[384,768]{1,0:T(8,128)(2,1)}, bf16[384,768]{1,0:T(8,128)(2,1)S(1)}, u32[]{:S(2)}, u32[]{:S(2)}) collective-permute-start(bf16[384,768]{1,0:T(8,128)(2,1)} %get-tuple-element.161), channel_id=1, source_target_pairs={{0,16},{4,20},{8,24},{12,28},{16,0},{20,4},{24,8},{28,12},{1,17},{... | collective-permute-start | bytes 1769480 | tf_op jit(solution)/shard_map/ppermute | solution.py:1449
  289.6 34.7 %collective-permute-start.22 = (bf16[384,768]{1,0:T(8,128)(2,1)S(1)}, bf16[384,768]{1,0:T(8,128)(2,1)S(1)}, u32[]{:S(2)}, u32[]{:S(2)}) collective-permute-start(bf16[384,768]{1,0:T(8,128)(2,1)S(1)} %copy-done.47), channel_id=1, source_target_pairs={{0,24},{4,28},{8,16},{12,20},{16,8},{20,12},{24,0},{28,4},{1,25},{... | collective-permute-start | bytes 1769480 | tf_op jit(solution)/shard_map/ppermute | solution.py:1449
  290.6 38.0 %collective-permute-start.24 = (bf16[1152,256]{1,0:T(8,128)(2,1)}, bf16[1152,256]{1,0:T(8,128)(2,1)S(1)}, u32[]{:S(2)}, u32[]{:S(2)}) collective-permute-start(bf16[1152,256]{1,0:T(8,128)(2,1)} %bitcast.55), channel_id=1, source_target_pairs={{0,16},{4,20},{8,24},{12,28},{16,0},{20,4},{24,8},{28,12},{1,17},{... | collective-permute-start | bytes 1769480 | tf_op jit(solution)/shard_map/ppermute | solution.py:1449
  292.3 36.3 %collective-permute-start.23 = (bf16[1152,256]{1,0:T(8,128)(2,1)}, bf16[1152,256]{1,0:T(8,128)(2,1)S(1)}, u32[]{:S(2)}, u32[]{:S(2)}) collective-permute-start(bf16[1152,256]{1,0:T(8,128)(2,1)} %bitcast.56), channel_id=1, source_target_pairs={{0,8},{4,12},{8,0},{12,4},{16,24},{20,28},{24,16},{28,20},{1,9},{5... | collective-permute-start | bytes 1769480 | tf_op jit(solution)/shard_map/ppermute | solution.py:1449
  342.4 4.8 %collective-permute-start.26 = (bf16[768,1536]{1,0:T(8,128)(2,1)}, bf16[768,1536]{1,0:T(8,128)(2,1)S(1)}, u32[]{:S(2)}, u32[]{:S(2)}) collective-permute-start(bf16[768,1536]{1,0:T(8,128)(2,1)} %get-tuple-element.178), channel_id=1, source_target_pairs={{0,4},{4,0},{8,12},{12,8},{16,20},{20,16},{24,28},{28,24},{1,5},{5... | collective-permute-start | bytes 7077896 | tf_op jit(solution)/shard_map/ppermute | solution.py:1452
  342.5 16.6 %collective-permute-start.30 = (bf16[1152,256]{1,0:T(8,128)(2,1)S(1)}, bf16[1152,256]{1,0:T(8,128)(2,1)S(1)}, u32[]{:S(2)}, u32[]{:S(2)}) collective-permute-start(bf16[1152,256]{1,0:T(8,128)(2,1)S(1)} %bitcast.57), channel_id=1, source_target_pairs={{0,24},{4,28},{8,16},{12,20},{16,8},{20,12},{24,0},{28,4},{1,25},{... | collective-permute-start | bytes 1769480 | tf_op jit(solution)/shard_map/ppermute | solution.py:1449
  361.6 4.6 collective-permute-start.31
  361.7 39.5 %collective-permute-start.33 = (bf16[1152,256]{1,0:T(8,128)(2,1)}, bf16[1152,256]{1,0:T(8,128)(2,1)S(1)}, u32[]{:S(2)}, u32[]{:S(2)}) collective-permute-start(bf16[1152,256]{1,0:T(8,128)(2,1)} %bitcast.19), channel_id=1, source_target_pairs={{0,16},{4,20},{8,24},{12,28},{16,0},{20,4},{24,8},{28,12},{1,17},{... | collective-permute-start | bytes 1769480 | tf_op jit(solution)/shard_map/ppermute | solution.py:1449
  362.3 38.9 %collective-permute-start.32 = (bf16[1152,256]{1,0:T(8,128)(2,1)}, bf16[1152,256]{1,0:T(8,128)(2,1)S(1)}, u32[]{:S(2)}, u32[]{:S(2)}) collective-permute-start(bf16[1152,256]{1,0:T(8,128)(2,1)} %bitcast.19), channel_id=1, source_target_pairs={{0,8},{4,12},{8,0},{12,4},{16,24},{20,28},{24,16},{28,20},{1,9},{5... | collective-permute-start | bytes 1769480 | tf_op jit(solution)/shard_map/ppermute | solution.py:1449
  363.9 37.4 %collective-permute-start.27 = (bf16[4,48,1536]{2,1,0:T(8,128)(2,1)}, bf16[4,48,1536]{2,1,0:T(8,128)(2,1)}, u32[]{:S(2)}, u32[]{:S(2)}) collective-permute-start(bf16[4,48,1536]{2,1,0:T(8,128)(2,1)} %get-tuple-element.180), channel_id=1, source_target_pairs={{0,8},{4,12},{8,0},{12,4},{16,24},{20,28},{24,16},{28,20},{1,9},{5... | collective-permute-start | bytes 1769480 | tf_op jit(solution)/shard_map/ppermute | solution.py:1449
  364.4 36.9 %collective-permute-start.28 = (bf16[4,48,1536]{2,1,0:T(8,128)(2,1)}, bf16[4,48,1536]{2,1,0:T(8,128)(2,1)}, u32[]{:S(2)}, u32[]{:S(2)}) collective-permute-start(bf16[4,48,1536]{2,1,0:T(8,128)(2,1)} %get-tuple-element.181), channel_id=1, source_target_pairs={{0,16},{4,20},{8,24},{12,28},{16,0},{20,4},{24,8},{28,12},{1,17},{... | collective-permute-start | bytes 1769480 | tf_op jit(solution)/shard_map/ppermute | solution.py:1449
  366.2 20.6 %copy-start.8 = (bf16[4,1152,256]{2,1,0:T(8,128)(2,1)}, bf16[4,1152,256]{2,1,0:T(8,128)(2,1)S(1)}, u32[]{:S(2)}) copy-start(bf16[4,1152,256]{2,1,0:T(8,128)(2,1)S(1)} %collective-permute-done.31.refs_2_) | copy-start | bytes 7077892
  366.2 38.0 %collective-permute-start.29 = (bf16[4,48,1536]{2,1,0:T(8,128)(2,1)}, bf16[4,48,1536]{2,1,0:T(8,128)(2,1)}, u32[]{:S(2)}, u32[]{:S(2)}) collective-permute-start(bf16[4,48,1536]{2,1,0:T(8,128)(2,1)} %get-tuple-element.182), channel_id=1, source_target_pairs={{0,24},{4,28},{8,16},{12,20},{16,8},{20,12},{24,0},{28,4},{1,25},{... | collective-permute-start | bytes 1769480 | tf_op jit(solution)/shard_map/ppermute | solution.py:1449
  407.0 17.9 %collective-permute-start.40 = (bf16[1152,256]{1,0:T(8,128)(2,1)}, bf16[1152,256]{1,0:T(8,128)(2,1)S(1)}, u32[]{:S(2)}, u32[]{:S(2)}) collective-permute-start(bf16[1152,256]{1,0:T(8,128)(2,1)} %bitcast.19), channel_id=1, source_target_pairs={{0,24},{4,28},{8,16},{12,20},{16,8},{20,12},{24,0},{28,4},{1,25},{... | collective-permute-start | bytes 1769480 | tf_op jit(solution)/shard_map/ppermute | solution.py:1449
  408.5 9.9 %collective-permute-start.34 = (bf16[64,1536]{1,0:T(8,128)(2,1)}, bf16[64,1536]{1,0:T(8,128)(2,1)S(1)}, u32[]{:S(2)}, u32[]{:S(2)}) collective-permute-start(bf16[64,1536]{1,0:T(8,128)(2,1)} %get-tuple-element.204), channel_id=1, source_target_pairs={{0,1},{1,2},{2,3},{3,0},{4,5},{5,6},{6,7},{7,4},{8,9},{9,10},{10,1... | collective-permute-start | bytes 589832 | tf_op jit(solution)/shard_map/ppermute | solution.py:1455
  410.8 14.0 %collective-permute-start.35 = (bf16[64,1536]{1,0:T(8,128)(2,1)}, bf16[64,1536]{1,0:T(8,128)(2,1)S(1)}, u32[]{:S(2)}, u32[]{:S(2)}) collective-permute-start(bf16[64,1536]{1,0:T(8,128)(2,1)} %get-tuple-element.205), channel_id=1, source_target_pairs={{0,2},{1,3},{2,0},{3,1},{4,6},{5,7},{6,4},{7,5},{8,10},{9,11},{10,... | collective-permute-start | bytes 589832 | tf_op jit(solution)/shard_map/ppermute | solution.py:1455
  411.8 13.1 %collective-permute-start.36 = (bf16[64,1536]{1,0:T(8,128)(2,1)}, bf16[64,1536]{1,0:T(8,128)(2,1)S(1)}, u32[]{:S(2)}, u32[]{:S(2)}) collective-permute-start(bf16[64,1536]{1,0:T(8,128)(2,1)} %get-tuple-element.206), channel_id=1, source_target_pairs={{0,3},{1,0},{2,1},{3,2},{4,7},{5,4},{6,5},{7,6},{8,11},{9,8},{10,9... | collective-permute-start | bytes 589832 | tf_op jit(solution)/shard_map/ppermute | solution.py:1455
  426.8 7.3 %collective-permute-start.41 = (bf16[4,1152,256]{2,1,0:T(8,128)(2,1)S(1)}, bf16[4,1152,256]{2,1,0:T(8,128)(2,1)S(1)}, u32[]{:S(2)}, u32[]{:S(2)}) collective-permute-start(bf16[4,1152,256]{2,1,0:T(8,128)(2,1)S(1)} %pad_maximum_fusion.1.refs_1_), channel_id=1, source_target_pairs={{0,4},{4,0},{8,12},{12,8},{16,20},{20,16},{24,28},{28,24},{1,5},{5... | collective-permute-start | bytes 7077896 | tf_op jit(solution)/shard_map/ppermute | solution.py:1452
  429.6 19.4 %collective-permute-start.39 = (bf16[64,1536]{1,0:T(8,128)(2,1)}, bf16[64,1536]{1,0:T(8,128)(2,1)S(1)}, u32[]{:S(2)}, u32[]{:S(2)}) collective-permute-start(bf16[64,1536]{1,0:T(8,128)(2,1)} %fold_shards.1.refs_1_), channel_id=1, source_target_pairs={{0,24},{4,28},{8,16},{12,20},{16,8},{20,12},{24,0},{28,4},{1,25},{... | collective-permute-start | bytes 589832 | tf_op jit(solution)/shard_map/ppermute | solution.py:1449
  431.0 18.0 %collective-permute-start.38 = (bf16[64,1536]{1,0:T(8,128)(2,1)}, bf16[64,1536]{1,0:T(8,128)(2,1)S(1)}, u32[]{:S(2)}, u32[]{:S(2)}) collective-permute-start(bf16[64,1536]{1,0:T(8,128)(2,1)} %fold_shards.1.refs_1_), channel_id=1, source_target_pairs={{0,16},{4,20},{8,24},{12,28},{16,0},{20,4},{24,8},{28,12},{1,17},{... | collective-permute-start | bytes 589832 | tf_op jit(solution)/shard_map/ppermute | solution.py:1449
  431.6 17.5 %collective-permute-start.37 = (bf16[64,1536]{1,0:T(8,128)(2,1)}, bf16[64,1536]{1,0:T(8,128)(2,1)S(1)}, u32[]{:S(2)}, u32[]{:S(2)}) collective-permute-start(bf16[64,1536]{1,0:T(8,128)(2,1)} %fold_shards.1.refs_1_), channel_id=1, source_target_pairs={{0,8},{4,12},{8,0},{12,4},{16,24},{20,28},{24,16},{28,20},{1,9},{5... | collective-permute-start | bytes 589832 | tf_op jit(solution)/shard_map/ppermute | solution.py:1449
  452.0 2.3 collective-permute-start.42
  (46 other events, 244.4 us)
Sparse Core Ops, SparseCore 0:
  32.6 90.0 all-gather.2
  234.6 47.6 reduce-scatter.2
  287.2 47.9 reduce-scatter.4

commit v3 on v2

--- a/solution.py
+++ b/solution.py
@@ -21,6 +21,7 @@
 EPS = 1e-06
 COST_SCALE = 0.02
 ATT = 100
+BACK = 400
 f32 = jnp.float32
 bf16 = jnp.bfloat16
 
@@ -154,69 +155,118 @@
     )
 
 
-def fill_bias(bias_ref, dcol_ref, drow_ref, vcol_ref, length):
+PAD_LANE = 6
+
+
+def fill_masks(query_mask, key_mask, key_mask_own, table, dcol_ref, vcol_ref):
+    length = dcol_ref.shape[0]
+    lane = lax.broadcasted_iota(jnp.int32, (length, LANES), 1) % HDIM
+    docs = dcol_ref[...]
+    query_mask[...] = jnp.where((lane == docs) | (lane == PAD_LANE), 1.0, 0.0).astype(bf16)
+    other = jnp.where((lane < PAD_LANE) & (lane != docs), -1e30, 0.0)
+    key_mask_own[...] = other.astype(bf16)
+    padded = (lane == PAD_LANE) & (vcol_ref[...] == 0)
+    key_mask[...] = jnp.where(padded, -1e30, other).astype(bf16)
+    key = lax.broadcasted_iota(jnp.int32, (QB, QB), 0)
+    query = lax.broadcasted_iota(jnp.int32, (QB, QB), 1)
     for i in range(length // QB):
-        start = i * QB
-        low = max(0, start - REACH)
-        size = start + QB - low
-        key = low + lax.broadcasted_iota(jnp.int32, (size, QB), 0)
-        query = start + lax.broadcasted_iota(jnp.int32, (size, QB), 1)
-        same = dcol_ref[low : low + size, :] == drow_ref[:, start : start + QB]
-        usable = (vcol_ref[low : low + size, :] > 0) | (key == query)
-        allowed = same & (key <= query) & usable
-        bias_ref[i, :size, :] = jnp.where(allowed, 0.0, -1e30)
-
-
-def lane_head(shape, head):
-    lane = lax.broadcasted_iota(jnp.int32, shape, 1)
-    return (lane // HDIM) == head
-
-
-def attend_kernel(q_ref, k_ref, v_ref, dcol_ref, drow_ref, vcol_ref, ctx_ref, lse_ref, bias_ref):
+        usable = (vcol_ref[i * QB : (i + 1) * QB, :] > 0) | (key == query)
+        table[i] = jnp.where((key <= query) & usable, 0.0, -1e30)
+
+
+def mask_scratch(length):
+    return [pltpu.VMEM((length, LANES), bf16)] * 3 + [pltpu.VMEM((length // QB, QB, QB), f32)]
+
+
+def per_head(inside, outside):
+    lane = lax.broadcasted_iota(jnp.int32, inside.shape, 1)
+    return [jnp.where(lane // HDIM == head, inside, outside) for head in range(2)]
+
+
+def key_blocks(i):
+    start = i * QB
+    return [start] + list(range(max(0, start - REACH), start, QB))
+
+
+def attend_kernel(
+    q_ref, k_ref, v_ref, dcol_ref, vcol_ref, ctx_ref, lse_ref, q_mask, k_mask, k_own, table
+):
     length = q_ref.shape[0]
 
     @pl.when(pl.program_id(0) == 0)
     def _():
-        fill_bias(bias_ref, dcol_ref, drow_ref, vcol_ref, length)
+        fill_masks(q_mask, k_mask, k_own, table, dcol_ref, vcol_ref)
 
     values_t = v_ref[...].astype(f32).T.astype(bf16)
-    for i in range(length // QB):
+    queries = per_head(q_ref[...], q_mask[...])
+    keys = per_head(k_ref[...], k_mask[...])
+    own_keys = per_head(k_ref[...], k_own[...])
+
+    def scores_of(i, head):
         start = i * QB
-        low = max(0, start - REACH)
-        size = start + QB - low
-        keys = k_ref[low : low + size, :]
-        query = q_ref[start : start + QB, :]
-        parts = []
-        for head in range(2):
-            masked = jnp.where(lane_head(query.shape, head), query, jnp.zeros_like(query))
-            scores = mm_nt(keys, masked) + bias_ref[i, :size, :]
-            largest = jnp.max(scores, axis=0, keepdims=True)
-            raised = jnp.exp(scores - largest)
-            total = jnp.sum(raised, axis=0, keepdims=True)
-            part = mm(
-                values_t[head * HDIM : (head + 1) * HDIM, low : low + size], raised.astype(bf16)
+        query = queries[head][start : start + QB]
+        scores = [mm_nt(own_keys[head][start : start + QB], query) + table[i]]
+        for at in key_blocks(i)[1:]:
+            scores.append(mm_nt(keys[head][at : at + QB], query))
+        return scores
+
+    def weights_of(i, head, scores):
+        largest = scores[0]
+        for block in scores[1:]:
+            largest = jnp.maximum(largest, block)
+        largest = jnp.max(largest, axis=0, keepdims=True)
+        raised = [jnp.exp(block - largest) for block in scores]
+        total = raised[0]
+        for block in raised[1:]:
+            total = total + block
+        total = jnp.sum(total, axis=0, keepdims=True)
+        lse_ref[0, head : head + 1, i * QB : (i + 1) * QB] = largest + jnp.log(total)
+        return [block.astype(bf16) for block in raised], total
+
+    def context_of(i, head, raised, total):
+        context = 0.0
+        for at, block in zip(key_blocks(i), raised, strict=True):
+            context = context + mm(
+                values_t[head * HDIM : (head + 1) * HDIM, at : at + QB], block
             )
-            parts.append(part * (1.0 / total))
-            lse_ref[0, head : head + 1, start : start + QB] = largest + jnp.log(total)
-        ctx_ref[start : start + QB, :] = jnp.concatenate(parts, axis=0).T.astype(bf16)
-
-
-def attend_call(q, k, v, dcol, drow, vcol, after):
+        return context * (1.0 / total)
+
+    units = [(i, head) for i in range(length // QB) for head in range(2)]
+    ahead = scores_of(*units[0])
+    behind, contexts = None, []
+    for index in range(len(units) + 1):
+        scores = ahead
+        if index + 1 < len(units):
+            ahead = scores_of(*units[index + 1])
+        made = None
+        if index < len(units):
+            made = (*units[index], *weights_of(*units[index], scores))
+        if behind is not None:
+            contexts.append(context_of(*behind))
+            if len(contexts) == 2:
+                i = behind[0]
+                ctx_ref[i * QB : (i + 1) * QB, :] = (
+                    jnp.concatenate(contexts, axis=0).T.astype(bf16)
+                )
+                contexts = []
+        behind = made
+
+
+def attend_call(q, k, v, dcol, vcol):
     length = q.shape[0]
     pairs = HEADS // 2
     column = pl.BlockSpec((length, LANES), lambda p: (0, p))
     return launch(
         attend_kernel,
-        [q, k, v, dcol, drow, vcol],
-        [column, column, column, whole(dcol.shape), whole(drow.shape), whole(vcol.shape)],
+        [q, k, v, dcol, vcol],
+        [column, column, column, whole(dcol.shape), whole(vcol.shape)],
         [column, pl.BlockSpec((1, 2, length), lambda p: (p, 0, 0))],
         [
             jax.ShapeDtypeStruct((length, D), bf16),
             jax.ShapeDtypeStruct((pairs, 2, length), f32),
         ],
-        after,
         grid=(pairs,),
-        scratch_shapes=[pltpu.VMEM((length // QB, REACH + QB, QB), f32)],
+        scratch_shapes=mask_scratch(length),
         compiler_params=params(),
         cost_estimate=cost(ATT * 20e9, ATT * 8 * length * D),
         name="attend",
@@ -230,14 +280,16 @@
     g_ref,
     lse_ref,
     dcol_ref,
-    drow_ref,
     vcol_ref,
     cos_ref,
     sin_ref,
     dq_ref,
     dk_ref,
     dv_ref,
-    bias_ref,
+    q_mask,
+    k_mask,
+    k_own,
+    table,
     gk_ref,
     gv_ref,
     gq_ref,
@@ -246,34 +298,71 @@
 
     @pl.when(pl.program_id(0) == 0)
     def _():
-        fill_bias(bias_ref, dcol_ref, drow_ref, vcol_ref, length)
-
-    gk_ref[...] = jnp.zeros_like(gk_ref)
-    gv_ref[...] = jnp.zeros_like(gv_ref)
+        fill_masks(q_mask, k_mask, k_own, table, dcol_ref, vcol_ref)
+
     keys_t = k_ref[...].astype(f32).T.astype(bf16)
-    for i in range(length // QB):
+    zero = jnp.zeros(q_ref.shape, bf16)
+    queries = per_head(q_ref[...], q_mask[...])
+    bare = per_head(q_ref[...], zero)
+    grads = per_head(g_ref[...], zero)
+    keys = per_head(k_ref[...], k_mask[...])
+    own_keys = per_head(k_ref[...], k_own[...])
+    begun = set()
+
+    def products_of(i, head):
         start = i * QB
-        low = max(0, start - REACH)
-        size = start + QB - low
-        span = slice(low, low + size)
-        keys = k_ref[span, :]
-        values = v_ref[span, :]
-        query = q_ref[start : start + QB, :]
-        grads = g_ref[start : start + QB, :]
-        for head in range(2):
-            own = lane_head(query.shape, head)
-            query_h = jnp.where(own, query, jnp.zeros_like(query))
-            grads_h = jnp.where(own, grads, jnp.zeros_like(grads))
-            scores = mm_nt(keys, query_h) + bias_ref[i, :size, :]
-            probs = jnp.exp(scores - lse_ref[0, head : head + 1, start : start + QB])
-            grad_probs = mm_nt(values, grads_h)
-            inner = jnp.sum(probs * grad_probs, axis=0, keepdims=True)
-            grad_scores = (probs * (grad_probs - inner)).astype(bf16)
-            gv_ref[span, :] += mm(probs.astype(bf16), grads_h)
-            gk_ref[span, :] += mm(grad_scores, query_h)
-            gq_ref[head * HDIM : (head + 1) * HDIM, start : start + QB] = mm(
-                keys_t[head * HDIM : (head + 1) * HDIM, span], grad_scores
-            )
+        query = queries[head][start : start + QB]
+        grad = grads[head][start : start + QB]
+        scores, grad_probs = [], []
+        for at in key_blocks(i):
+            if at == start:
+                scores.append(mm_nt(own_keys[head][at : at + QB], query) + table[i])
+            else:
+                scores.append(mm_nt(keys[head][at : at + QB], query))
+            grad_probs.append(mm_nt(v_ref[at : at + QB, :], grad))
+        return scores, grad_probs
+
+    def softmax_back(i, head, scores, grad_probs):
+        lse = lse_ref[0, head : head + 1, i * QB : (i + 1) * QB]
+        probs = [jnp.exp(block - lse) for block in scores]
+        inner = probs[0] * grad_probs[0]
+        for p, d in zip(probs[1:], grad_probs[1:], strict=True):
+            inner = inner + p * d
+        inner = jnp.sum(inner, axis=0, keepdims=True)
+        grad_scores = [
+            (p * (d - inner)).astype(bf16) for p, d in zip(probs, grad_probs, strict=True)
+        ]
+        return [p.astype(bf16) for p in probs], grad_scores
+
+    def spread_back(i, head, probs, grad_scores):
+        start = i * QB
+        grad_q = 0.0
+        for at, p, s in zip(key_blocks(i), probs, grad_scores, strict=True):
+            grad_v = mm(p, grads[head][start : start + QB])
+            grad_k = mm(s, bare[head][start : start + QB])
+            if at in begun:
+                gv_ref[at : at + QB, :] += grad_v
+                gk_ref[at : at + QB, :] += grad_k
+            else:
+                begun.add(at)
+                gv_ref[at : at + QB, :] = grad_v
+                gk_ref[at : at + QB, :] = grad_k
+            grad_q = grad_q + mm(keys_t[head * HDIM : (head + 1) * HDIM, at : at + QB], s)
+        gq_ref[head * HDIM : (head + 1) * HDIM, start : start + QB] = grad_q
+
+    units = [(i, head) for i in range(length // QB) for head in range(2)]
+    ahead = products_of(*units[0])
+    behind = None
+    for index in range(len(units) + 1):
+        products = ahead
+        if index + 1 < len(units):
+            ahead = products_of(*units[index + 1])
+        made = None
+        if index < len(units):
+            made = (*units[index], *softmax_back(*units[index], *products))
+        if behind is not None:
+            spread_back(*behind)
+        behind = made
     cosine, sine = cos_ref[...], sin_ref[...]
     grad_q = gq_ref[...].T * HDIM**-0.5
     grad_k = gk_ref[...]
@@ -282,22 +371,21 @@
     dv_ref[...] = gv_ref[...].astype(bf16)
 
 
-def attend_back_call(q, k, v, g, lse, dcol, drow, vcol, cosine, sine, after):
+def attend_back_call(q, k, v, g, lse, dcol, vcol, cosine, sine):
     length = q.shape[0]
     pairs = HEADS // 2
     column = pl.BlockSpec((length, LANES), lambda p: (0, p))
     return launch(
         attend_back_kernel,
-        [q, k, v, g, lse, dcol, drow, vcol, cosine, sine],
+        [q, k, v, g, lse, dcol, vcol, cosine, sine],
         [column] * 4
         + [pl.BlockSpec((1, 2, length), lambda p: (p, 0, 0))]
-        + [whole(a.shape) for a in (dcol, drow, vcol, cosine, sine)],
+        + [whole(a.shape) for a in (dcol, vcol, cosine, sine)],
         [column] * 3,
         [jax.ShapeDtypeStruct((length, D), bf16)] * 3,
-        after,
         grid=(pairs,),
-        scratch_shapes=[
-            pltpu.VMEM((length // QB, REACH + QB, QB), f32),
+        scratch_shapes=mask_scratch(length)
+        + [
             pltpu.VMEM((length, LANES), f32),
             pltpu.VMEM((length, LANES), f32),
             pltpu.VMEM((LANES, length), f32),
@@ -414,29 +502,6 @@
     )
 
 
-def lay_riders_kernel(shape, own_ref, *refs):
-    pieces, out = refs[:-1], refs[-1]
-    shards, quarter, width = shape
-    per = D // width
-    for k, piece in enumerate(pieces):
-        for z in range(shards):
-            row, column = z // per * quarter, z % per * width
-            out[z, own_ref[0] ^ k] = piece[CAP + row : CAP + row + quarter, column : column + width]
-
-
-def lay_riders(own, blocks, shape, after):
-    shards, quarter, width = shape
-    return launch(
-        partial(lay_riders_kernel, shape),
-        [own, *blocks],
-        [SMEM] + [VM] * len(blocks),
-        VM,
-        jax.ShapeDtypeStruct((shards, len(blocks), quarter, width), bf16),
-        after,
-        name="lay_riders",
-    )
-
-
 def lanes_of(shape):
     return lax.broadcasted_iota(jnp.int32, shape, 1)
 
@@ -511,13 +576,12 @@
 
 
 EXTRA = 16
+COEF, INVERSE = 16, 17
 
 
 def dispatch_kernel(gated, mine_ref, spot_ref, v_ref, *refs):
     if gated:
         gate_ref, refs = refs[0], refs[1:]
-    else:
-        rider, refs = refs[0], refs[1:]
     rows = v_ref.shape[0]
     slot = lax.broadcasted_iota(jnp.int32, (CAP, rows), 0)
     for k in range(EXPERTS):
@@ -534,13 +598,11 @@
             ).astype(bf16)
             refs[k][CAP:, :CAP] = tail
             refs[k][CAP:, CAP:] = jnp.zeros((EXTRA, D - CAP), bf16)
-        else:
-            refs[k][CAP:, :] = rider[...]
-
-
-def dispatch_call(mine, spot, values, gates=None, rider=None, after=()):
-    size = CAP + (EXTRA if rider is None else rider.shape[0])
-    operands = [mine, spot, values] + [rider if gates is None else gates]
+
+
+def dispatch_call(mine, spot, values, gates=None, after=()):
+    size = CAP + (0 if gates is None else EXTRA)
+    operands = [mine, spot, values] + ([] if gates is None else [gates])
     rows = values.shape[0]
     return launch(
         partial(dispatch_kernel, gates is not None),
@@ -572,10 +634,10 @@
     def column(self, half, tile, span, part, chunk):
         z = tile * self.spans + span
         base = half * self.hidden + z * (self.hidden // self.shards)
-        return base + (part * self.chunks + chunk) * self.seg
+        return base + (chunk * self.copies + part) * self.seg
 
     def down_row(self, part, chunk):
-        return (part * self.chunks + chunk) * self.seg
+        return (chunk * self.copies + part) * self.seg
 
 
 def pack_kernel(plan, who_ref, in_ref, out_ref, pack):
@@ -591,9 +653,10 @@
         def _(e=e):
             value = in_ref[:, e, :]
             for chunk in range(plan.chunks):
-                piece = value[:, chunk * seg : (chunk + 1) * seg]
+                at = chunk * plan.copies * seg
+                piece = value[:, at : at + seg]
                 for p in range(1, plan.copies):
-                    at = (p * plan.chunks + chunk) * seg
+                    at = (chunk * plan.copies + p) * seg
                     piece = jnp.where(part == p, value[:, at : at + seg], piece)
                 at = pl.multiple_of(chunk * plan.rows + row, 16)
                 pack[pl.ds(at, shard), pl.ds(column, seg)] = piece
@@ -656,29 +719,32 @@
     in_out, down_out = refs[2 * copies + 2 * begun :]
     mine, part = who_ref[0], who_ref[1]
     step = pl.program_id(0)
-    p = step % copies
-    z = (step // copies) % plan.shards
+    z = step % plan.shards
+
+    def of_replica(arrays, p, index):
+        chosen = arrays[0][index].astype(f32)
+        for m in range(1, copies):
+            chosen = jnp.where(part == (p ^ m), arrays[m][index].astype(f32), chosen)
+        return chosen
+
     for j in range(EXPERTS):
-        chosen = ins[0][j ^ mine].astype(f32)
-        for m in range(1, copies):
-            chosen = jnp.where(part == (p ^ m), ins[m][j ^ mine].astype(f32), chosen)
-        piece = chosen[:, :seg]
-        for span in range(1, plan.spans):
-            here = z % plan.spans == span
-            piece = jnp.where(here, chosen[:, span * seg : (span + 1) * seg], piece)
-        in_out[:, j, :] = piece
-
-    @pl.when(step < copies)
+        for p in range(copies):
+            chosen = of_replica(ins, p, j ^ mine)
+            piece = chosen[:, :seg]
+            for span in range(1, plan.spans):
+                here = z % plan.spans == span
+                piece = jnp.where(here, chosen[:, span * seg : (span + 1) * seg], piece)
+            in_out[:, j, p * seg : (p + 1) * seg] = piece
+
+    @pl.when(step == 0)
     def _():
         for j in range(EXPERTS):
-            for down in range(plan.downs):
-                rows = slice(down * seg, (down + 1) * seg)
-                chosen = downs[0][j ^ mine, rows, :].astype(f32)
-                for m in range(1, copies):
-                    chosen = jnp.where(
-                        part == (p ^ m), downs[m][j ^ mine, rows, :].astype(f32), chosen
-                    )
-                down_out[:, j, down * plan.wide : (down + 1) * plan.wide] = chosen
+            for p in range(copies):
+                chosen = of_replica(downs, p, j ^ mine)
+                for down in range(plan.downs):
+                    down_out[
+                        p * seg : (p + 1) * seg, j, down * plan.wide : (down + 1) * plan.wide
+                    ] = chosen[down * seg : (down + 1) * seg]
 
 
 def unpack_chunk(plan, who, chunk, sums, begun):
@@ -686,32 +752,34 @@
     per = plan.hidden // shards
     start = 2 * plan.tiles * plan.shard
     down_rows = plan.downs * plan.seg
+    both = copies * plan.seg
 
     def in_block(i):
-        half, z = i // (shards * copies), (i // copies) % shards
-        return (0, half * plan.tiles + z // plan.spans, 0)
-
-    def down_block(i):
-        return (jnp.minimum(i, copies - 1) * plan.chunks + chunk, 0, 0)
-
+        return (0, i // shards * plan.tiles + i % shards // plan.spans, 0)
+
+    down_in = pl.BlockSpec(
+        (EXPERTS, down_rows, plan.wide),
+        lambda i: (0, start // down_rows, 0),
+        pipeline_mode=pl.Buffered(1),
+    )
     hbm = pl.BlockSpec(memory_space=pl.ANY)
-    operands = [who, *sums, *[s[:, start:, :] for s in sums], *begun]
+    operands = [who, *sums, *sums, *begun]
     return launch(
         partial(unpack_kernel, plan, len(begun) // 2),
         operands,
         [SMEM]
         + [pl.BlockSpec((EXPERTS, plan.shard, plan.wide), in_block)] * copies
-        + [whole((EXPERTS, down_rows, plan.wide))] * copies
+        + [down_in] * copies
         + [hbm] * len(begun),
         [
-            pl.BlockSpec((plan.shard, EXPERTS, plan.seg), lambda i: (0, 0, i * plan.chunks + chunk)),
-            pl.BlockSpec((plan.seg, EXPERTS, D), down_block),
+            pl.BlockSpec((plan.shard, EXPERTS, both), lambda i: (0, 0, i * plan.chunks + chunk)),
+            pl.BlockSpec((both, EXPERTS, D), lambda i: (chunk, 0, 0)),
         ],
         [
             jax.ShapeDtypeStruct((plan.shard, EXPERTS, 2 * plan.hidden), f32),
             jax.ShapeDtypeStruct((per, EXPERTS, D), f32),
         ],
-        grid=(2 * shards * copies,),
+        grid=(2 * shards,),
         input_output_aliases={len(operands) - 2 + i: i for i in range(len(begun))},
         compiler_params=params(),
         cost_estimate=cost(0, 12 * plan.shard * plan.hidden * EXPERTS),
@@ -729,8 +797,8 @@
     for j in range(EXPERTS):
         columns = {}
         rows = []
-        for p in range(plan.copies):
-            for chunk in range(plan.chunks):
+        for chunk in range(plan.chunks):
+            for p in range(plan.copies):
                 stacked = jnp.stack(sums[chunk])
                 piece = lax.dynamic_index_in_dim(stacked, part ^ p, 0, keepdims=False)
                 piece = lax.dynamic_index_in_dim(piece, mine ^ j, 0, keepdims=False)
@@ -756,6 +824,25 @@
     return jnp.stack(ins, axis=1).astype(f32), jnp.stack(outs, axis=1).astype(f32)
 
 
+def weight_grads(plan, part, xt, ds, act, grad_gate, grad_up, grads):
+    shard, seg, wide, tiles = plan.shard, plan.seg, plan.wide, plan.tiles
+    for half, source in ((0, grad_gate), (1, grad_up)):
+        for tile in range(tiles):
+            made = mm(xt[...], source[part, :, tile * wide : (tile + 1) * wide]).astype(bf16)
+            row = (half * tiles + tile) * shard
+            for z in range(plan.shards):
+                grads[part, z, row : row + shard, :] = made[z * shard : (z + 1) * shard, :]
+    for tile in range(tiles):
+        made = mm_tn(act[part, :, tile * wide : (tile + 1) * wide], ds[...]).astype(bf16)
+        for span in range(plan.spans):
+            z = tile * plan.spans + span
+            for down in range(plan.downs):
+                row = 2 * tiles * shard + down * seg
+                grads[part, z, row : row + seg, :] = made[
+                    span * seg : (span + 1) * seg, down * wide : (down + 1) * wide
+                ]
+
+
 def expert_kernel(plan, first, last, *refs):
     refs = list(refs)
 
@@ -767,112 +854,138 @@
     copies = plan.copies
     x_refs, y_refs = take(EXPERTS), take(EXPERTS)
     w_refs = take(copies)
-    carry_in = [] if first else take(2)
-    grad_outs = take(copies)
+    if first:
+        carry_in = []
+    else:
+        carry_in = take(2)
+        (ds,) = take(1)
     if last:
-        dx_outs, ret_outs = take(EXPERTS), take(EXPERTS)
-        carry_out = []
+        dx_outs, ret_outs, saved = take(EXPERTS), take(EXPERTS), take(3)
     else:
-        carry_out = take(2)
-    xs, ds, xt, gcol, ret_acc, dx_acc, wg, wu, wo, act_s, dg_s, du_s, grads, sems = refs
-    rows = EXPERTS * CAP
+        grad_outs, carry_out, saved = take(copies), take(2), take(2)
+    xs, gcol, ret_acc, dx_acc, act_s, dg_s, du_s = take(7)
+    waiting = [take(3), take(3)]
+    if last:
+        y_held, sems = refs
+    else:
+        ds, xt, grads, sems = refs
     shard, seg, wide, tiles = plan.shard, plan.seg, plan.wide, plan.tiles
-
-    carries = [
-        pltpu.make_async_copy(src, dst, sems.at[i])
-        for i, (src, dst) in enumerate(zip(carry_in, (ret_acc, dx_acc)))
-    ]
-    for copy in carries:
-        copy.start()
+    started = []
+
+    def copy(src, dst):
+        made = pltpu.make_async_copy(src, dst, sems.at[len(started)])
+        started.append(made)
+        made.start()
+        return made
+
+    carries = [copy(src, dst) for src, dst in zip(carry_in, (ret_acc, dx_acc))]
+    if last:
+        held = [
+            copy(y_refs[k].at[pl.ds(0, CAP)], y_held.at[pl.ds(k * CAP, CAP)])
+            for k in range(EXPERTS)
+        ]
     for k in range(EXPERTS):
         span = slice(k * CAP, (k + 1) * CAP)
         x = x_refs[k][:CAP, :]
         xs[span, :] = x
-        xt[:, span] = x.astype(f32).T.astype(bf16)
         extra = x_refs[k][CAP:, :CAP].astype(f32)
         gate = (extra[0:1] + extra[1:2]).T
         gcol[span, :] = jnp.broadcast_to(gate, (CAP, LANES))
-        ds[span, :] = (y_refs[k][:CAP, :].astype(f32) * gate).astype(bf16)
+        if not last:
+            xt[:, span] = x.astype(f32).T.astype(bf16)
+            ds[span, :] = (y_refs[k][:CAP, :].astype(f32) * gate).astype(bf16)
+    sends = []
+    if not last:
+        sends = [copy(src, dst) for src, dst in zip((xt, ds), saved, strict=True)]
     if first:
         ret_acc[...] = jnp.zeros_like(ret_acc)
         dx_acc[...] = jnp.zeros_like(dx_acc)
-    for copy in carries:
-        copy.wait()
-
-    sends = []
-    for m in range(copies):
-        w = w_refs[m]
-        for z in range(plan.shards):
-            for tile in range(tiles):
-                for half, target in ((0, wg), (1, wu)):
-                    row = (half * tiles + tile) * shard
-                    target[z * shard : (z + 1) * shard, tile * wide : (tile + 1) * wide] = w[
-                        z, row : row + shard, :
-                    ]
-            for down in range(plan.downs):
-                row = 2 * tiles * shard + down * seg
-                wo[z * seg : (z + 1) * seg, down * wide : (down + 1) * wide] = w[
-                    z, row : row + seg, :
+
+    def columns(part, half, tile):
+        row = (half * tiles + tile) * shard
+        return w_refs[part][:, row : row + shard, :].reshape(D, wide)
+
+    def down_columns(part, down):
+        row = 2 * tiles * shard + down * seg
+        return w_refs[part][:, row : row + seg, :].reshape(plan.width, wide)
+
+    def products(part, b, held):
+        span = slice(b * CAP, (b + 1) * CAP)
+        x, d = xs[span, :], ds[span, :]
+        for tile in range(tiles):
+            at = slice(tile * wide, (tile + 1) * wide)
+            held[0][:, at] = mm(x, columns(part, 0, tile))
+            held[1][:, at] = mm(x, columns(part, 1, tile))
+        grad = 0.0
+        for down in range(plan.downs):
+            grad = grad + mm_nt(
+                d[:, down * wide : (down + 1) * wide], down_columns(part, down)
+            )
+        held[2][...] = grad
+
+    def gating(part, b, held):
+        span = slice(b * CAP, (b + 1) * CAP)
+        gate, up, grad_act = held[0][...], held[1][...], held[2][...]
+        sig = 1.0 / (1.0 + jnp.exp(-gate))
+        silu = gate * sig
+        act_s[part, span, :] = (silu * up).astype(bf16)
+        du_s[part, span, :] = (grad_act * silu).astype(bf16)
+        dg_s[part, span, :] = (grad_act * up * (sig + silu * (1.0 - sig))).astype(bf16)
+
+    def back(part, b):
+        span = slice(b * CAP, (b + 1) * CAP)
+        act = act_s[part, span, :]
+        for down in range(plan.downs):
+            ret_acc[span, down * wide : (down + 1) * wide] += mm(act, down_columns(part, down))
+        total = 0.0
+        for tile in range(tiles):
+            at = slice(tile * wide, (tile + 1) * wide)
+            total = total + mm_nt(dg_s[part, span, at], columns(part, 0, tile))
+            total = total + mm_nt(du_s[part, span, at], columns(part, 1, tile))
+        dx_acc[span, :] += total
+
+    for part in range(copies):
+        products(part, 0, waiting[0])
+        for b in range(EXPERTS):
+            if b + 1 < EXPERTS:
+                products(part, b + 1, waiting[(b + 1) % 2])
+            gating(part, b, waiting[b % 2])
+            if b > 0:
+                if part == 0 and b == 1:
+                    for made in carries:
+                        made.wait()
+                back(part, b - 1)
+        back(part, EXPERTS - 1)
+        if last:
+            sends += [
+                copy(src.at[part], dst.at[part])
+                for src, dst in zip((act_s, dg_s, du_s), saved, strict=True)
+            ]
+        else:
+            if part == copies - 1:
+                sends += [
+                    copy(src, dst) for src, dst in zip((ret_acc, dx_acc), carry_out, strict=True)
                 ]
-
-        def block(b, _):
-            span = pl.ds(pl.multiple_of(b * CAP, CAP), CAP)
-            x, d = xs[span, :], ds[span, :]
-            gate = mm(x, wg[...])
-            up = mm(x, wu[...])
-            grad_act = mm_nt(d, wo[...])
-            sig = 1.0 / (1.0 + jnp.exp(-gate))
-            silu = gate * sig
-            act = (silu * up).astype(bf16)
-            grad_up = (grad_act * silu).astype(bf16)
-            grad_gate = (grad_act * up * (sig + silu * (1.0 - sig))).astype(bf16)
-            act_s[span, :] = act
-            du_s[span, :] = grad_up
-            dg_s[span, :] = grad_gate
-            ret_acc[span, :] += mm(act, wo[...])
-            dx_acc[span, :] += mm_nt(grad_gate, wg[...]) + mm_nt(grad_up, wu[...])
-            return 0
-
-        lax.fori_loop(0, EXPERTS, block, 0)
-        if m == copies - 1 and not last:
-            for i, (src, dst) in enumerate(zip((ret_acc, dx_acc), carry_out, strict=True)):
-                copy = pltpu.make_async_copy(src, dst, sems.at[2 + i])
-                copy.start()
-                sends.append(copy)
-        if m == copies - 1 and last:
-            for k in range(EXPERTS):
-                span = slice(k * CAP, (k + 1) * CAP)
-                ret = ret_acc[span, :]
-                dgate = jnp.sum(ret * y_refs[k][:CAP, :].astype(f32), axis=-1, keepdims=True)
-                dgate = jnp.broadcast_to(dgate, (CAP, LANES)).T[:1]
-                ret_outs[k][...] = (ret * gcol[span, :1]).astype(bf16)
-                dx_outs[k][:CAP, :] = dx_acc[span, :].astype(bf16)
-                high = dgate.astype(bf16).astype(f32)
-                tail = jnp.concatenate(
-                    [high, dgate - high, jnp.zeros((EXTRA - 2, CAP), f32)], axis=0
-                ).astype(bf16)
-                dx_outs[k][CAP:, :CAP] = tail
-                dx_outs[k][CAP:, CAP:] = jnp.zeros((EXTRA, D - CAP), bf16)
-        for half, source in ((0, dg_s), (1, du_s)):
-            for tile in range(tiles):
-                made = mm(xt[...], source[:, tile * wide : (tile + 1) * wide]).astype(bf16)
-                row = (half * tiles + tile) * shard
-                for z in range(plan.shards):
-                    grads[m, z, row : row + shard, :] = made[z * shard : (z + 1) * shard, :]
-        for tile in range(tiles):
-            made = mm_tn(act_s[:, tile * wide : (tile + 1) * wide], ds[...]).astype(bf16)
-            for span in range(plan.spans):
-                z = tile * plan.spans + span
-                for down in range(plan.downs):
-                    row = 2 * tiles * shard + down * seg
-                    grads[m, z, row : row + seg, :] = made[
-                        span * seg : (span + 1) * seg, down * wide : (down + 1) * wide
-                    ]
-        copy = pltpu.make_async_copy(grads.at[m], grad_outs[m], sems.at[4 + m])
-        copy.start()
-        sends.append(copy)
-    for copy in sends:
-        copy.wait()
+            weight_grads(plan, part, xt, ds, act_s, dg_s, du_s, grads)
+            sends.append(copy(grads.at[part], grad_outs[part]))
+    if last:
+        for made in held:
+            made.wait()
+        for k in range(EXPERTS):
+            span = slice(k * CAP, (k + 1) * CAP)
+            ret = ret_acc[span, :]
+            dgate = jnp.sum(ret * y_held[span, :].astype(f32), axis=-1, keepdims=True)
+            dgate = jnp.broadcast_to(dgate, (CAP, LANES)).T[:1]
+            ret_outs[k][...] = (ret * gcol[span, :1]).astype(bf16)
+            dx_outs[k][:CAP, :] = dx_acc[span, :].astype(bf16)
+            high = dgate.astype(bf16).astype(f32)
+            tail = jnp.concatenate(
+                [high, dgate - high, jnp.zeros((EXTRA - 2, CAP), f32)], axis=0
+            ).astype(bf16)
+            dx_outs[k][CAP:, :CAP] = tail
+            dx_outs[k][CAP:, CAP:] = jnp.zeros((EXTRA, D - CAP), bf16)
+    for made in sends:
+        made.wait()
 
 
 def expert_call(plan, xs, ys, weights, chunk, carried):
@@ -885,50 +998,88 @@
         lambda i: (0, chunk, 0),
         pipeline_mode=pl.Buffered(1),
     )
-    in_specs = [whole(a.shape) for a in (*xs, *ys)] + [block] * copies
+    in_specs = [whole(a.shape) for a in xs]
+    in_specs += [hbm if last else whole(a.shape) for a in ys] + [block] * copies
     operands = list(xs) + list(ys) + list(weights)
     if not first:
-        in_specs += [hbm] * 2
+        in_specs += [hbm] * 2 + [whole((rows, D))]
         operands += list(carried)
-    out_specs = [hbm] * copies
-    out_shape = [jax.ShapeDtypeStruct((plan.shards, plan.rows, plan.wide), bf16)] * copies
+    held = jax.ShapeDtypeStruct((copies, rows, plan.width), bf16)
     if last:
-        out_specs += [whole((CAP + EXTRA, D))] * EXPERTS
-        out_specs += [whole((CAP, D))] * EXPERTS
-        out_shape += [jax.ShapeDtypeStruct((CAP + EXTRA, D), bf16)] * EXPERTS
+        out_specs = [whole((CAP + EXTRA, D))] * EXPERTS + [whole((CAP, D))] * EXPERTS
+        out_shape = [jax.ShapeDtypeStruct((CAP + EXTRA, D), bf16)] * EXPERTS
         out_shape += [jax.ShapeDtypeStruct((CAP, D), bf16)] * EXPERTS
+        out_specs += [hbm] * 3
+        out_shape += [held] * 3
     else:
-        out_specs += [hbm] * 2
+        out_specs = [hbm] * (copies + 4)
+        out_shape = [jax.ShapeDtypeStruct((plan.shards, plan.rows, plan.wide), bf16)] * copies
         out_shape += [jax.ShapeDtypeStruct((rows, D), f32)] * 2
-    made = pl.pallas_call(
+        out_shape += [
+            jax.ShapeDtypeStruct((D, rows), bf16),
+            jax.ShapeDtypeStruct((rows, D), bf16),
+        ]
+    scratch = [
+        pltpu.VMEM((rows, D), bf16),
+        pltpu.VMEM((rows, LANES), f32),
+        pltpu.VMEM((rows, D), f32),
+        pltpu.VMEM((rows, D), f32),
+    ]
+    scratch += [pltpu.VMEM((copies, rows, plan.width), bf16)] * 3
+    scratch += [pltpu.VMEM((CAP, plan.width), f32)] * 6
+    if last:
+        scratch.append(pltpu.VMEM((rows, D), bf16))
+    else:
+        scratch += [
+            pltpu.VMEM((rows, D), bf16),
+            pltpu.VMEM((D, rows), bf16),
+            pltpu.VMEM((copies, plan.shards, plan.rows, plan.wide), bf16),
+        ]
+    scratch.append(pltpu.SemaphoreType.DMA((6 + 3 * copies,)))
+    return pl.pallas_call(
         partial(expert_kernel, plan, first, last),
+        grid=(1,),
         in_specs=in_specs,
         out_specs=out_specs,
         out_shape=out_shape,
-        scratch_shapes=[
-            pltpu.VMEM((rows, D), bf16),
-            pltpu.VMEM((rows, D), bf16),
-            pltpu.VMEM((D, rows), bf16),
-            pltpu.VMEM((rows, LANES), f32),
-            pltpu.VMEM((rows, D), f32),
-            pltpu.VMEM((rows, D), f32),
-            pltpu.VMEM((D, plan.width), bf16),
-            pltpu.VMEM((D, plan.width), bf16),
-            pltpu.VMEM((plan.width, D), bf16),
-            pltpu.VMEM((rows, plan.width), bf16),
-            pltpu.VMEM((rows, plan.width), bf16),
-            pltpu.VMEM((rows, plan.width), bf16),
-            pltpu.VMEM((copies, plan.shards, plan.rows, plan.wide), bf16),
-            pltpu.SemaphoreType.DMA((4 + copies,)),
-        ],
-        grid=(1,),
+        scratch_shapes=scratch,
         compiler_params=params(),
         cost_estimate=cost(
             18 * rows * D * plan.width * copies, 12 * D * plan.width * copies + 12 * rows * D
         ),
         name="experts",
     )(*operands)
-    return made[:copies], made[copies:]
+
+
+def expert_grads_kernel(plan, act, grad_gate, grad_up, xt, ds, *refs):
+    outs, (grads, sems) = refs[: plan.copies], refs[plan.copies :]
+    sends = []
+    for part in range(plan.copies):
+        weight_grads(plan, part, xt, ds, act, grad_gate, grad_up, grads)
+        sends.append(pltpu.make_async_copy(grads.at[part], outs[part], sems.at[part]))
+        sends[-1].start()
+    for made in sends:
+        made.wait()
+
+
+def expert_grads(plan, held):
+    copies = plan.copies
+    packed = (plan.shards, plan.rows, plan.wide)
+    return launch(
+        partial(expert_grads_kernel, plan),
+        list(held),
+        [whole(a.shape) for a in held],
+        [pl.BlockSpec(memory_space=pl.ANY)] * copies,
+        [jax.ShapeDtypeStruct(packed, bf16)] * copies,
+        grid=(1,),
+        scratch_shapes=[
+            pltpu.VMEM((copies, *packed), bf16),
+            pltpu.SemaphoreType.DMA((copies,)),
+        ],
+        compiler_params=params(),
+        cost_estimate=cost(0, 0),
+        name="expert_grads",
+    )
 
 
 def spots_of(place_ref, rows):
@@ -942,6 +1093,67 @@
     a1 = one[:, NCH + 2 * m + 1 : NCH + 2 * m + 2]
     gate = chosen[:, EXPERTS + 2 + m : EXPERTS + 3 + m]
     return gate, a0, a1
+
+
+def side_kernel(
+    res_ref, dy_ref, one_ref, place_ref, choice_ref, small_ref, two_ref, spots_ref, cvec_out
+):
+    @pl.when(pl.program_id(0) == 0)
+    def _():
+        cvec_out[...] = jnp.zeros_like(cvec_out)
+
+    res = res_ref[...]
+    one = one_ref[...]
+    lane = lanes_of(one.shape)
+    named = selected(choice_ref, lane)
+    chosen = jnp.where(named, one, 0.0)
+    is_mix = (lane >= NCH) & (lane < NCH + 4)
+    spots_ref[...] = spots_of(place_ref, res.shape[0])
+    inverse = lax.rsqrt(jnp.mean(res * res, axis=-1, keepdims=True) + EPS)
+    dy = dy_ref[...]
+    spread = res * inverse * row_of(small_ref, GAIN_F)
+    hd = jnp.sum(spread * dy.astype(f32), axis=-1, keepdims=True)
+    cd = mm_nt(dy, small_ref[...])
+    coef = chosen[:, EXPERTS + 1 : EXPERTS + 2]
+    grads = jnp.where(lane == EXPERTS + 1, hd, 0.0)
+    made = jnp.zeros_like(one)
+    for m in range(2):
+        gate, a0, a1 = constant_gates(one, chosen, m)
+        dot = cd[:, CVEC + m : CVEC + m + 1]
+        coef = coef + gate * a0
+        grads = jnp.where(lane == EXPERTS + 2 + m, a0 * hd + a1 * dot, grads)
+        grads = jnp.where(lane == NCH + 2 * m, gate * hd, grads)
+        grads = jnp.where(lane == NCH + 2 * m + 1, gate * dot, grads)
+        made = jnp.where(lane == m, gate * a1, made)
+    two = jnp.where(is_mix | named, grads, 0.0)
+    two = jnp.where(lane == COEF, coef, two)
+    two_ref[...] = jnp.where(lane == INVERSE, inverse, two)
+    high = made.astype(bf16)
+    rest = (made - high.astype(f32)).astype(bf16)
+    cvec_out[...] += mm_tn(high, dy) + mm_tn(rest, dy)
+
+
+def side_call(res, dy, one, places, choices, small):
+    rows = res.shape[0]
+    block = 256
+    return launch(
+        side_kernel,
+        [res, dy, one, places, choices, small],
+        [rows_of(block, D)] * 2
+        + [rows_of(block, LANES)]
+        + [rows_of(block, 2)] * 2
+        + [whole(small.shape)],
+        [rows_of(block, LANES), rows_of(block, EXPERTS * CAP), whole((LANES, D))],
+        [
+            jax.ShapeDtypeStruct((rows, LANES), f32),
+            jax.ShapeDtypeStruct((rows, EXPERTS * CAP), bf16),
+            jax.ShapeDtypeStruct((LANES, D), f32),
+        ],
+        grid=(rows // block,),
+        compiler_params=params(),
+        cost_estimate=cost(0, 0),
+        name="side",
+    )
 
 
 def back_kernel(
@@ -951,8 +1163,8 @@
     h_ref,
     dy_ref,
     one_ref,
-    place_ref,
-    choice_ref,
+    two_ref,
+    spots_ref,
     prev_ref,
     wsmall_ref,
     *refs,
@@ -966,7 +1178,6 @@
         dsmall_ref,
         gain_out,
         prev_out,
-        cvec_out,
         w_ref,
         dg_ref,
     ) = refs
@@ -975,7 +1186,6 @@
     def _():
         gain_out[...] = jnp.zeros_like(gain_out)
         prev_out[...] = jnp.zeros_like(prev_out)
-        cvec_out[...] = jnp.zeros_like(cvec_out)
         dsmall_ref[...] = jnp.zeros_like(dsmall_ref)
         lay_columns(w_ref, pieces, who_ref[1])
         lane = lanes_of((CAP, LANES))
@@ -990,36 +1200,20 @@
     rows = res.shape[0]
     one = one_ref[...]
     lane = lanes_of(one.shape)
-    chosen = jnp.where(selected(choice_ref, lane), one, 0.0)
     choice = lane < NCH
     is_mix = (lane >= NCH) & (lane < NCH + 4)
-    spots = spots_of(place_ref, rows)
+    two = two_ref[...]
+    spots = spots_ref[...]
     moved = jnp.zeros(res.shape, f32)
     for k in range(EXPERTS):
         moved = moved + mm(spots[:, k * CAP : (k + 1) * CAP], dx_refs[k][:CAP, :])
     from_experts = mm(spots, dg_ref[...])
     from_experts = from_experts + pltpu.roll(from_experts, LANES - 16, 1)
-
-    inverse = lax.rsqrt(jnp.mean(res * res, axis=-1, keepdims=True) + EPS)
+    coef, inverse = two[:, COEF : COEF + 1], two[:, INVERSE : INVERSE + 1]
     dy = dy_ref[...]
     dyf = dy.astype(f32)
     gain = row_of(wsmall_ref, GAIN_F)
-    spread = res * inverse * gain
-    hd = jnp.sum(spread * dyf, axis=-1, keepdims=True)
-    cd = mm_nt(dy, wsmall_ref[...])
-    coef = chosen[:, EXPERTS + 1 : EXPERTS + 2]
-    grads = jnp.where(lane < EXPERTS, from_experts, 0.0)
-    grads = jnp.where(lane == EXPERTS + 1, hd, grads)
-    made = jnp.zeros_like(one)
-    for m in range(2):
-        gate, a0, a1 = constant_gates(one, chosen, m)
-        dot = cd[:, CVEC + m : CVEC + m + 1]
-        coef = coef + gate * a0
-        grads = jnp.where(lane == EXPERTS + 2 + m, a0 * hd + a1 * dot, grads)
-        grads = jnp.where(lane == NCH + 2 * m, gate * hd, grads)
-        grads = jnp.where(lane == NCH + 2 * m + 1, gate * dot, grads)
-        made = jnp.where(lane == m, gate * a1, made)
-    grads = jnp.where(is_mix | selected(choice_ref, lane), grads, 0.0)
+    grads = jnp.where(lane < EXPERTS, from_experts, jnp.where(lane < NCH + 4, two, 0.0))
     weighted = one * grads
     mean_choice = jnp.sum(jnp.where(choice, weighted, 0.0), axis=-1, keepdims=True)
     d_logits = jnp.where(choice, one * (grads - mean_choice), 0.0)
@@ -1040,45 +1234,40 @@
     rest = (d_logits - high.astype(f32)).astype(bf16)
     prev = prev_ref[...]
     prev_out[...] += mm(prev, high) + mm(prev, rest)
-    high = made.astype(bf16)
-    rest = (made - high.astype(f32)).astype(bf16)
-    cvec_out[...] += mm_tn(high, dy) + mm_tn(rest, dy)
-
-
-def back_call(who, res, h, dy, one, places, choices, prev, small, dx, pieces, after):
+
+
+def back_call(who, res, h, dy, one, two, spots, prev, small, dx, pieces, after):
     rows = res.shape[0]
     block = 256
-    tall = jax.ShapeDtypeStruct((LANES, D), f32)
     return launch(
         partial(back_kernel, len(pieces)),
-        [who, res, h, dy, one, places, choices, prev, small, *dx, *pieces],
+        [who, res, h, dy, one, two, spots, prev, small, *dx, *pieces],
         [SMEM]
         + [rows_of(block, D)] * 3
-        + [rows_of(block, LANES)]
-        + [rows_of(block, 2)] * 2
+        + [rows_of(block, LANES)] * 2
+        + [rows_of(block, EXPERTS * CAP)]
         + [pl.BlockSpec((NCH, block), lambda i: (0, i))]
         + [whole(a.shape) for a in (small, *dx, *pieces)],
         [rows_of(block, D)] * 3
-        + [whole((LANES, D)), whole((1, D)), whole((NCH, LANES)), whole((LANES, D))],
+        + [whole((LANES, D)), whole((1, D)), whole((NCH, LANES))],
         [
             jax.ShapeDtypeStruct((rows, D), f32),
             jax.ShapeDtypeStruct((rows, D), bf16),
             jax.ShapeDtypeStruct((rows, D), bf16),
-            tall,
+            jax.ShapeDtypeStruct((LANES, D), f32),
             jax.ShapeDtypeStruct((1, D), f32),
             jax.ShapeDtypeStruct((NCH, LANES), f32),
-            tall,
         ],
         after,
         grid=(rows // block,),
         scratch_shapes=[pltpu.VMEM((D, D), bf16), pltpu.VMEM((EXPERTS * CAP, LANES), bf16)],
         compiler_params=params(),
-        cost_estimate=cost(2 * rows * D * (D + 2048), 20 * rows * D),
+        cost_estimate=cost(BACK * 2 * rows * D * (D + 2048), BACK * 20 * rows * D),
         name="combine_back",
     )
 
 
-def finish_kernel(res_ref, one_ref, place_ref, choice_ref, small_ref, *refs):
+def finish_kernel(res_ref, one_ref, spots_ref, choice_ref, small_ref, *refs):
     ret_refs, out_ref = refs[:EXPERTS], refs[EXPERTS]
     res = res_ref[...]
     one = one_ref[...]
@@ -1092,20 +1281,20 @@
         coef = coef + gate * a0
         total = total + (gate * a1) * row_of(small_ref, CVEC + m)
     total = total + (coef * inverse) * res * row_of(small_ref, GAIN_F)
-    spots = spots_of(place_ref, res.shape[0])
+    spots = spots_ref[...]
     for k in range(EXPERTS):
         total = total + mm(spots[:, k * CAP : (k + 1) * CAP], ret_refs[k][...])
     out_ref[...] = total.astype(bf16)
 
 
-def finish_call(res, one, places, choices, small, ret, after):
+def finish_call(res, one, spots, choices, small, ret, after):
     rows = res.shape[0]
     block = 256
     return launch(
         finish_kernel,
-        [res, one, places, choices, small, *ret],
+        [res, one, spots, choices, small, *ret],
         [rows_of(block, D), rows_of(block, LANES)]
-        + [rows_of(block, 2)] * 2
+        + [rows_of(block, EXPERTS * CAP), rows_of(block, 2)]
         + [whole(a.shape) for a in (small, *ret)],
         rows_of(block, D),
         jax.ShapeDtypeStruct((rows, D), bf16),
@@ -1137,78 +1326,87 @@
     )
 
 
-def dense_kernel(copies, per, part_ref, ht_ref, ct_ref, *refs):
-    rights, outs = refs[:4], refs[4:]
+def dense_kernel(copies, each, own, part_ref, mine_ref, ht_ref, ct_ref, *refs):
+    rights, refs = refs[:4], refs[4:]
     step = pl.program_id(0)
-    source = ((step // per) ^ part_ref[0]) * per + step % per
+    if own:
+        got, outs, total_ref = refs[: copies - 1], refs[copies - 1 : -1], refs[-1]
+    else:
+        outs = refs
+    per = pl.num_programs(0) if own else pl.num_programs(0) // (copies - 1)
+    source = (part_ref[0] if own else (step // per + 1) ^ part_ref[0]) * per + step % per
     for index, right in enumerate(rights):
         left = ct_ref if index == 3 else ht_ref
-        for m in range(copies):
-
-            @pl.when((source // 2 == index) & (step // per == m))
-            def _(left=left, right=right, m=m):
-                outs[m][...] = mm(left[...], right[...]).astype(bf16)
-
-
-def dense_call(copies, part, ht, ct, dq, dk, dv, branch):
+
+        @pl.when(source // each == index)
+        def _(left=left, right=right):
+            made = mm(left[...], right[...])
+            if own:
+                for ref in got:
+                    made = made + ref[...].astype(f32)
+                total_ref[...] = made.astype(bf16).reshape(total_ref.shape)
+            else:
+                for m, out in enumerate(outs):
+                    if len(outs) == 1:
+                        out[...] = made.astype(bf16)
+                    else:
+
+                        @pl.when(step // per == m)
+                        def _(out=out):
+                            out[...] = made.astype(bf16)
+
+    if own:
+        for k, out in enumerate(outs):
+            out[...] = total_ref[:, mine_ref[0] ^ k]
+
+
+def dense_call(copies, shards, part, mine, ht, ct, rights, got=None):
     rows = ht.shape[1]
-    half = D // 2
-    per = 8 // copies
+    cut = 4 * D // copies
+    step = D // 2 if cut % D == 0 else cut
+    per = cut // step
+    each = D // step
+    quarter = D // (shards * EXPERTS)
+    own = got is not None
 
     def right_block(index):
-        def block(i, part_ref):
-            source = ((i // per) ^ part_ref[0]) * per + i % per
-            return (0, jnp.clip(source - 2 * index, 0, 1))
+        def block(i, part_ref, mine_ref):
+            replica = part_ref[0] if own else (i // per + 1) ^ part_ref[0]
+            return (0, jnp.clip(replica * per + i % per - each * index, 0, each - 1))
 
         return block
 
-    def out_block(m):
-        return lambda i, part_ref: (0, jnp.clip(i - m * per, 0, per - 1))
+    def other_block(m):
+        return lambda i, *_: (0, jnp.clip(i - m * per, 0, per - 1))
 
     def fixed(shape):
-        return pl.BlockSpec(shape, lambda i, part_ref: (0, 0), pipeline_mode=pl.Buffered(1))
-
+        return pl.BlockSpec(shape, lambda i, *_: (0, 0), pipeline_mode=pl.Buffered(1))
+
+    in_specs = [fixed(ht.shape), fixed(ct.shape)]
+    in_specs += [pl.BlockSpec((rows, step), right_block(index)) for index in range(4)]
+    if own:
+        in_specs += [pl.BlockSpec((D, step), lambda i, *_: (0, i))] * (copies - 1)
+        out_specs = [pl.BlockSpec((shards, quarter, step), lambda i, *_: (0, 0, i))] * EXPERTS
+        out_shape = [jax.ShapeDtypeStruct((shards, quarter, cut), bf16)] * EXPERTS
+        scratch = [pltpu.VMEM((shards, EXPERTS, quarter, step), bf16)]
+    else:
+        out_specs = [pl.BlockSpec((D, step), other_block(m)) for m in range(copies - 1)]
+        out_shape = [jax.ShapeDtypeStruct((D, cut), bf16)] * (copies - 1)
+        scratch = []
     return pl.pallas_call(
-        partial(dense_kernel, copies, per),
+        partial(dense_kernel, copies, each, own),
         grid_spec=pltpu.PrefetchScalarGridSpec(
-            num_scalar_prefetch=1,
-            grid=(8,),
-            in_specs=[fixed(ht.shape), fixed(ct.shape)]
-            + [pl.BlockSpec((rows, half), right_block(index)) for index in range(4)],
-            out_specs=[pl.BlockSpec((D, half), out_block(m)) for m in range(copies)],
+            num_scalar_prefetch=2,
+            grid=(per if own else per * (copies - 1),),
+            in_specs=in_specs,
+            out_specs=out_specs,
+            scratch_shapes=scratch,
         ),
-        out_shape=[jax.ShapeDtypeStruct((D, 4 * D // copies), bf16)] * copies,
+        out_shape=out_shape,
         compiler_params=params(),
         cost_estimate=cost(8 * rows * D * D, 12 * rows * D + 8 * D * D),
-        name="dense_grads",
-    )(part, ht, ct, dq, dk, dv, branch)
-
-
-def fold_parts_kernel(who_ref, *refs):
-    pieces, outs = refs[:-EXPERTS], refs[-EXPERTS:]
-    for k in range(EXPERTS):
-        at = who_ref[0] ^ k
-        total = pieces[0][0, at].astype(f32)
-        for piece in pieces[1:]:
-            total = total + piece[0, at].astype(f32)
-        outs[k][0] = total.astype(bf16)
-
-
-def fold_parts(who, pieces, shards):
-    cut = pieces[0].shape[1]
-    quarter = D // (shards * EXPERTS)
-    shape = (shards, EXPERTS, quarter, cut)
-    operands = [who] + [a.reshape(shape) for a in pieces]
-    return launch(
-        fold_parts_kernel,
-        operands,
-        [SMEM] + [pl.BlockSpec((1, EXPERTS, quarter, cut), lambda i: (i, 0, 0, 0))] * len(pieces),
-        [pl.BlockSpec((1, quarter, cut), lambda i: (i, 0, 0))] * EXPERTS,
-        [jax.ShapeDtypeStruct((shards, quarter, cut), bf16)] * EXPERTS,
-        grid=(shards,),
-        compiler_params=params(),
-        name="fold_parts",
-    )
+        name="dense_own" if own else "dense_others",
+    )(part, mine, ht, ct, *rights, *(got or ()))
 
 
 def fold_quarters_kernel(count, zi_ref, small_ref, *refs):
@@ -1465,7 +1663,7 @@
 
     width = 3 * D // copies
     owned = prev_mix.shape[0]
-    smalls = [router.T, const_mix.T, const_vec.T, gain_attn[None], gain_ffn[None], prev_mix]
+    smalls = [router.T, const_mix.T, const_vec.T, jnp.stack([gain_attn, gain_ffn]), prev_mix]
     piece, mark = cut_dense(who, qkv_weight, proj_weight, smalls, copies)
     spun = [piece] + [spin(piece, k) for k in range(1, shards)]
 
@@ -1517,60 +1715,56 @@
     )
     qkv_pieces = over_parts(qkv_half)
     part_q = part_s if len(qkv_pieces) == copies else jnp.zeros_like(part_s)
-    per = D // proj_part.shape[2]
-    rider = proj_part.reshape(-1, per, quarter, D // per).transpose(0, 2, 1, 3)
-    rider = rider.reshape(-1, D)
-    rider = jnp.pad(rider, ((0, -rider.shape[0] % 16), (0, 0)))
-    ys = dispatch_call(mine_s, spot, out_grad, rider=rider, after=(qkv_half,))
+    ys = dispatch_call(mine_s, spot, out_grad, after=(qkv_half,))
+    proj_half = lay_xor(mine_s, exchanged([tie(proj_part, qkv_half)] * EXPERTS))
 
     prev = prev_logits.T
     h1, q, k, v = qkv_call(part_q, tokens, small, cosine, sine, qkv_pieces, (ys[0],))
-    ys = exchanged(ys)
-    ctx, lse = attend_call(q, k, v, dcol, drow, vcol, ())
-    proj_half = lay_riders(mine_s, ys, proj_part.shape, (ctx,))
+    q, proj_half = tie((q, proj_half), h1)
+    q = tie(q, proj_half)
     proj_pieces = over_parts(proj_half)
     part_p = part_s if len(proj_pieces) == copies else jnp.zeros_like(part_s)
+    ys = exchanged(tie(ys, h1))
+    ctx, lse = attend_call(q, k, v, dcol, vcol)
     res, h2, one, gates = after_call(
         part_p, ctx, tokens, small, prev, pmix, routes, proj_pieces
     )
 
-    xs = dispatch_call(mine_s, spot, h2, gates)
+    xs = dispatch_call(mine_s, spot, tie(h2, ys), gates)
     gathered = tie(gathered, xs[0])
     weights = [gathered] + [to_part(gathered, m) for m in range(1, copies)]
     h1_t, ctx_t = turn_call([tie(h1, xs[0]), ctx])
+    two, spots, cvec_grad = side_call(tie(res, xs[0]), out_grad, one, places, routes, small)
     xs = exchanged(xs)
-    weights[0] = tie(weights[0], h1_t)
-    carried = None
+    weights[0] = tie(weights[0], (h1_t, two))
+    carried, turned = None, None
     chunk_grads = []
     for chunk in range(plan.chunks):
-        grads, carried = expert_call(
-            plan,
-            xs,
-            ys,
-            weights,
-            chunk,
-            carried,
-        )
-        chunk_grads.append(grads)
-    dx = exchanged(carried[:EXPERTS])
+        made = expert_call(plan, xs, ys, weights, chunk, carried)
+        if chunk < plan.chunks - 1:
+            chunk_grads.append(made[:copies])
+            carried = [*made[copies : copies + 2], made[copies + 3]]
+            turned = made[copies + 2]
+    dx, returned = exchanged(made[:EXPERTS]), made[EXPERTS : 2 * EXPERTS]
+    chunk_grads.append(expert_grads(plan, [*made[2 * EXPERTS :], turned, carried[2]]))
 
     chunk_grads = [
         [grads[0]] + [to_part(grads[m], m) for m in range(1, copies)] for grads in chunk_grads
     ]
-    total = fold_copies(tie(chunk_grads[0], carried[0]))
+    total = fold_copies(tie(chunk_grads[0], returned[0]))
 
     def over_shards(t):
         return lax.psum_scatter(t, "fsdp", scatter_dimension=0, tiled=False)
 
     who_p = jnp.concatenate([mine_s, part_p])
-    dres, branch, dctx, dsmall, gain_f_grad, prev_grad, cvec_grad = back_call(
+    dres, branch, dctx, dsmall, gain_f_grad, prev_grad = back_call(
         who_p,
         res,
         h2,
         out_grad,
         one,
-        places,
-        routes,
+        two,
+        spots,
         prev,
         small,
         dx,
@@ -1579,21 +1773,17 @@
     )
     summed = [over_shards(total)]
     summed += [over_shards(fold_copies(tie(grads, branch))) for grads in chunk_grads[1:]]
-    ret = exchanged(tie(carried[EXPERTS:], branch))
+    ret = exchanged(tie(returned, dx))
     first = tie(summed[0], branch)
     spread = [[first] + [to_expert(first, k) for k in range(1, EXPERTS - 1)]]
-    dq, dk, dv = attend_back_call(q, k, v, dctx, lse, dcol, drow, vcol, cosine, sine, ())
-    dense = dense_call(
-        copies, part_s, h1_t, ctx_t, tie(dq, ret, spread[0]), dk, dv, branch
-    )
-    spread[0].append(to_expert(tie(first, dq), EXPERTS - 1))
-    dense = tie(list(dense), summed[1:])
-    for piece in summed[1:]:
-        piece = tie(piece, dense[0])
-        spread.append([piece] + [to_expert(piece, k) for k in range(1, EXPERTS - 1)])
-    dense = [dense[0]] + [to_part(dense[m], m) for m in range(1, copies)]
-    quarters = fold_parts(who, dense, shards)
-
+    dq, dk, dv = attend_back_call(q, k, v, dctx, lse, dcol, vcol, cosine, sine)
+    rights = [tie(dq, ret, spread[0]), dk, dv, branch]
+    others = dense_call(copies, shards, part_s, mine_s, h1_t, ctx_t, rights)
+    spread[0].append(to_expert(tie(first, others[0]), EXPERTS - 1))
+    out = finish_call(res, one, spots, routes, small, tie(ret, others), ())
+    got = [to_part(others[m - 1], m) for m in range(1, copies)]
+    got = tie(got, (out, summed[1:]))
+    quarters = dense_call(copies, shards, part_s, mine_s, h1_t, ctx_t, rights, got)
     def over_copies(pieces):
         stacked = jnp.stack(pieces)
         return [stacked] + [to_part(stacked, m) for m in range(1, copies)]
@@ -1612,12 +1802,13 @@
         qkv_pieces,
         (),
     )
+    for piece in summed[1:]:
+        piece = tie(piece, smalls)
+        spread.append([piece] + [to_expert(piece, k) for k in range(1, EXPERTS - 1)])
     begun = ()
     if plan.seg % LANES == 0:
         begun = unpack_chunk(plan, who, 0, spread[0], begun)
-    out = finish_call(res, one, places, routes, small, tie(ret, quarters), ())
-    near = [pieces[1:] for pieces in spread[1:]]
-    bands = fold_quarters(zi_s, smalls, exchanged(quarters), (*begun, out, *near[0]))
+    bands = fold_quarters(zi_s, smalls, exchanged(quarters), tuple(begun))
     for pieces in spread[1:]:
         pieces.append(to_expert(tie(pieces[0], bands), EXPERTS - 1))
     spun = [bands[0]] + [spin(bands[k], k) for k in range(1, shards)]

time: 474 us -> 434 us (0.916)
  waiting for transfers between devices: 94.9 us -> 74.8 us
  Pallas kernels: 271 us -> 256 us
    pallas_call x3 -> x4, Pallas kernels: 82.2 us -> 69.9 us  [the longest x2 52.6 us: expert_call(): pl.pallas_call(partial(expert_kernel, plan, first, last), grid=(1,), in_s...]
    ppermute x6, waiting for transfers between devices: 12.1 us -> 3.88 us  [spin(): lax.ppermute(a, 'fsdp', [(i, (i + k) % shards) for i in range(shards)])]
    ppermute x27 -> x30, waiting for transfers between devices: 76 us -> 68.6 us  [to_expert(): lax.ppermute(a, 'rep', [(i, i ^ k * copies) for i in range(replicas)])]
    ppermute x27 -> x30, starting transfers between devices: 32.1 us -> 34.4 us  [to_expert(): lax.ppermute(a, 'rep', [(i, i ^ k * copies) for i in range(replicas)])]
    pallas_call x22 -> x23, Pallas kernels: 188 us -> 186 us  [launch(): pl.pallas_call(run, in_specs=list(in_specs) + [pl.BlockSpec(memory_space=...]
    unnamed x98 -> x101, local copies, waits for them, and re-layouts: 14.7 us -> 15.3 us
  transfers between devices with their start and end apart: 46 -> 49, of which waited for: 18 -> 13; matrix products, arithmetic and copies ran while one was open for 4% -> 3% of each run, Pallas kernels for 49% -> 52%
where the time goes in v3:
time: 434 us; the launch traced here: 428 us
  Pallas kernels  256 us (59%)
  waiting for transfers between devices  74.8 us (17%)
  starting transfers between devices  47.4 us (11%)
  local copies, waits for them, and re-layouts  20.5 us (5%)
  between operations  14.6 us (3%)
  other arithmetic  13.5 us (3%)
    pallas_call x23, Pallas kernels, launch(): pl.pallas_call(run, in_specs=list(in_specs) + [pl.BlockSpec(memory_space=...  186 us
    ppermute x30, waiting for transfers between devices, to_expert(): lax.ppermute(a, 'rep', [(i, i ^ k * copies) for i in range(replicas)])  68.6 us
    pallas_call x2, Pallas kernels, expert_call(): pl.pallas_call(partial(expert_kernel, plan, first, last), grid=(1,), in_s...  52.6 us
    ppermute x30, starting transfers between devices, to_expert(): lax.ppermute(a, 'rep', [(i, i ^ k * copies) for i in range(replicas)])  34.4 us
    pallas_call x2, Pallas kernels, dense_call(): pl.pallas_call(partial(dense_kernel, copies, each, own), grid_spec=pltpu....  17.3 us
    unnamed x101, local copies, waits for them, and re-layouts  15.3 us
    ppermute x6, starting transfers between devices, spin(): lax.ppermute(a, 'fsdp', [(i, (i + k) % shards) for i in range(shards)])  12.1 us
  transfers between devices with their start and end apart: 49, of which 13 were waited for; matrix products, arithmetic and copies ran while one was open for 3% of the time, Pallas kernels for 52%

profile of v3, /device:TPU:0, one launch (start us, length us, event | category | flops | bytes accessed | tf_op | source)
XLA Modules:
  0.0 427.7 jit_solution(888978426275811005)
XLA Ops:
  9.7 2.0 cut_dense.1
  11.7 5.0 %collective-permute-start.2 = (bf16[64,1536]{1,0:T(8,128)(2,1)}, bf16[64,1536]{1,0:T(8,128)(2,1)S(1)}, u32[]{:S(2)}, u32[]{:S(2)}) collective-permute-start(bf16[64,1536]{1,0:T(8,128)(2,1)} %get-tuple-element.131.refs_1_), channel_id=1, source_target_pairs={{0,3},{1,0},{2,1},{3,2},{4,7},{5,4},{6,5},{7,6},{8,11},{9,8},{10,9... | collective-permute-start | bytes 589832 | tf_op jit(solution)/shard_map/ppermute | solution.py:1653
  20.5 9.6 %pack.1.refs_5_ = bf16[2304,256]{1,0:T(8,128)(2,1)} custom-call(s32[2]{0:T(128)} %pad_add_fusion.refs_0_, bf16[192,4,4096]{2,1,0:T(4,128)(2,1)} %refs_1_.5, bf16[512,4,768]{2,1,0:T(4,128)(2,1)} %refs_2_.5, bf16[16,128]{1,0:T(8,128)(2,1)} %copy-done.38), custom_call_target="tpu_custom_call" | custom-call | tf_op jit(solution)/shard_map/pack/pallas_call | solution.py:63
  31.3 1.9 fusion.9
  34.4 2.1 lay_shards.1
  36.5 2.4 collective-permute-start.6
  42.9 1.9 pad_maximum_fusion.2
  45.7 5.1 %collective-permute-done.6.refs_4_ = bf16[4,48,1152]{2,1,0:T(8,128)(2,1)S(1)} collective-permute-done((bf16[4,48,1152]{2,1,0:T(8,128)(2,1)}, bf16[4,48,1152]{2,1,0:T(8,128)(2,1)S(1)}, u32[]{:S(2)}, u32[]{:S(2)}) %collective-permute-start.6) | collective-permute-done | bytes 442400 | tf_op jit(solution)/shard_map/ppermute | solution.py:1647
  50.7 8.8 %collective-permute-done.5.refs_3_ = bf16[4,48,1152]{2,1,0:T(8,128)(2,1)} collective-permute-done((bf16[4,48,1152]{2,1,0:T(8,128)(2,1)}, bf16[4,48,1152]{2,1,0:T(8,128)(2,1)}, u32[]{:S(2)}, u32[]{:S(2)}) %collective-permute-start.5) | collective-permute-done | bytes 442400 | tf_op jit(solution)/shard_map/ppermute | solution.py:1647
  59.6 2.8 lay_xor.2.refs_3_
  62.4 1.7 collective-permute-start.10
  67.2 4.9 %dispatch.2 = (bf16[384,768]{1,0:T(8,128)(2,1)}, bf16[384,768]{1,0:T(8,128)(2,1)}, bf16[384,768]{1,0:T(8,128)(2,1)}, bf16[384,768]{1,0:T(8,128)(2,1)}) custom-call(s32[1]{0:T(128)} %bitcast.2.refs_0_.mine_ref, s32[4,1024]{1,0:T(4,128)} %get-tuple-element.251.refs_7_.refs_1_, bf16[1024,768]{1,0:T(8,128)(2,1)} %refs_3_.2, bf16[4,4,48,1152]{3,2,1,0:T(8,128)(2,1)} %lay_xor.2.refs_3_), custom_call_target="tpu_custom_call" | custom-call | flops 48318384 | bytes 78643 | tf_op jit(solution)/shard_map/dispatch/pallas_call | solution.py:63
  74.0 2.0 lay_xor.3
  77.3 9.5 %qkv_rope.1 = (bf16[1024,768]{1,0:T(8,128)(2,1)}, bf16[1024,768]{1,0:T(8,128)(2,1)}, bf16[1024,768]{1,0:T(8,128)(2,1)}, bf16[1024,768]{1,0:T(8,128)(2,1)}) custom-call(s32[1]{0:T(128)} %bitcast.refs_0_.part_ref, bf16[1024,768]{1,0:T(8,128)(2,1)} %refs_4_.2, bf16[128,768]{1,0:T(8,128)(2,1)} %get-tuple-element.133.refs_2_.refs_3_.refs_5_.refs_8_.refs_4_.refs_6_, ...), custom_call_target="tpu_custom_call" | custom-call | flops 72477576 | bytes 228065 | tf_op jit(solution)/shard_map/qkv_rope/pallas_call | solution.py:63
  90.4 15.5 %attend.1 = (bf16[1024,768]{1,0:T(8,128)(2,1)}, f32[6,2,1024]{2,1,0:T(2,128)}) custom-call(bf16[1024,768]{1,0:T(8,128)(2,1)} %get-tuple-element.142.refs_0_, bf16[1024,768]{1,0:T(8,128)(2,1)} %get-tuple-element.143.refs_1_, bf16[1024,768]{1,0:T(8,128)(2,1)} %get-tuple-element.144.refs_2_, s32[1024,1]{1,0:T(8,128)} %copy.70.refs_8_.refs_3_.refs_5_, ...), custom_call_target="tpu_custom_call" | custom-call | flops 40000000000 | bytes 12582912 | tf_op jit(solution)/shard_map/attend/pallas_call | solution.py:63
  106.7 8.2 %after_attention.1 = (f32[1024,768]{1,0:T(8,128)}, bf16[1024,768]{1,0:T(8,128)(2,1)}, f32[1024,128]{1,0:T(8,128)}, bf16[16,1024]{1,0:T(8,128)(2,1)}) custom-call(s32[1]{0:T(128)} %bitcast.refs_0_.part_ref, bf16[1024,768]{1,0:T(8,128)(2,1)} %get-tuple-element.145.refs_1_, bf16[1024,768]{1,0:T(8,128)(2,1)} %refs_4_.2, ...), custom_call_target="tpu_custom_call" | custom-call | flops 24159192 | bytes 157286 | tf_op jit(solution)/shard_map/after_attention/pallas_call | solution.py:63
  116.2 6.1 %dispatch.3 = (bf16[400,768]{1,0:T(8,128)(2,1)}, bf16[400,768]{1,0:T(8,128)(2,1)}, bf16[400,768]{1,0:T(8,128)(2,1)}, bf16[400,768]{1,0:T(8,128)(2,1)}) custom-call(s32[1]{0:T(128)} %bitcast.2.refs_0_.mine_ref, s32[4,1024]{1,0:T(4,128)} %get-tuple-element.251.refs_7_.refs_1_, bf16[1024,768]{1,0:T(8,128)(2,1)} %get-tuple-element.157.refs_2_, ...), custom_call_target="tpu_custom_call" | custom-call | flops 48318384 | bytes 78643 | tf_op jit(solution)/shard_map/dispatch/pallas_call | solution.py:63
  125.8 4.5 %turn.1 = (bf16[768,1024]{1,0:T(8,128)(2,1)}, bf16[768,1024]{1,0:T(8,128)(2,1)}) custom-call(bf16[1024,768]{1,0:T(8,128)(2,1)} %get-tuple-element.166.refs_0_, bf16[1024,768]{1,0:T(8,128)(2,1)} %get-tuple-element.145.refs_1_), custom_call_target="tpu_custom_call" | custom-call | tf_op jit(solution)/shard_map/turn/pallas_call | solution.py:63
  130.4 10.1 %side.1 = (f32[1024,128]{1,0:T(8,128)}, bf16[1024,1536]{1,0:T(8,128)(2,1)}, f32[128,768]{1,0:T(8,128)}) custom-call(f32[1024,768]{1,0:T(8,128)} %get-tuple-element.160.refs_0_.refs_1_, bf16[1024,768]{1,0:T(8,128)(2,1)} %refs_3_.2, f32[1024,128]{1,0:T(8,128)} %get-tuple-element.148.refs_2_.refs_4_.refs_1_, s32[1024,2]{1,0:T(8,128)} %bitcast_select_fusion.refs_10_.refs_3_, ...), custom_call_target="tpu_custom_call" | custom-call | tf_op jit(solution)/shard_map/side/pallas_call | solution.py:63
  140.5 11.8 %collective-permute-done.17.refs_3_ = bf16[400,768]{1,0:T(8,128)(2,1)} collective-permute-done((bf16[400,768]{1,0:T(8,128)(2,1)}, bf16[400,768]{1,0:T(8,128)(2,1)}, u32[]{:S(2)}, u32[]{:S(2)}) %collective-permute-start.17) | collective-permute-done | bytes 614432 | tf_op jit(solution)/shard_map/ppermute | solution.py:1647
  152.3 2.2 copy-done.2
  154.5 28.4 %experts.2 = (bf16[4,1152,256]{2,1,0:T(8,128)(2,1)}, bf16[4,1152,256]{2,1,0:T(8,128)(2,1)}, f32[1536,768]{1,0:T(8,128)}, f32[1536,768]{1,0:T(8,128)}, bf16[768,1...) custom-call(bf16[400,768]{1,0:T(8,128)(2,1)} %get-tuple-element.159.refs_0_, bf16[400,768]{1,0:T(8,128)(2,1)} %copy-done.7, ...), custom_call_target="tpu_custom_call" | custom-call | flops 434865440 | bytes 471859 | tf_op jit(solution)/shard_map/experts/pallas_call | solution.py:1039
  183.0 24.2 %experts.3 = (bf16[400,768]{1,0:T(8,128)(2,1)}, bf16[400,768]{1,0:T(8,128)(2,1)}, bf16[400,768]{1,0:T(8,128)(2,1)}, bf16[400,768]{1,0:T(8,128)(2,1)}, bf16[384,7...) custom-call(bf16[400,768]{1,0:T(8,128)(2,1)} %get-tuple-element.159., ...), custom_call_target="tpu_custom_call" | custom-call | flops 434865440 | bytes 471859 | tf_op jit(solution)/shard_map/experts/pallas_call | solution.py:1039
  207.2 2.0 add_convert_fusion.1.refs_15_
  210.3 2.2 collective-permute-start.19
  214.1 14.5 %expert_grads.1 = (bf16[4,1152,256]{2,1,0:T(8,128)(2,1)}, bf16[4,1152,256]{2,1,0:T(8,128)(2,1)}) custom-call(bf16[2,1536,512]{2,1,0:T(8,128)(2,1)} %get-tuple-element.203.refs_0_, bf16[2,1536,512]{2,1,0:T(8,128)(2,1)} %get-tuple-element.204.refs_1_, bf16[2,1536,512]{2,1,0:T(8,128)(2,1)} %get-tuple-element.205.refs_2_, ...), custom_call_target="tpu_custom_call" | custom-call | tf_op jit(solution)/shard_map/expert_grads/pallas_call | solution.py:63
  228.7 12.9 %collective-permute-done.20.refs_11_ = bf16[400,768]{1,0:T(8,128)(2,1)S(1)} collective-permute-done((bf16[400,768]{1,0:T(8,128)(2,1)S(1)}, bf16[400,768]{1,0:T(8,128)(2,1)S(1)}, u32[]{:S(2)}, u32[]{:S(2)}) %collective-permute-start.20) | collective-permute-done | bytes 614432 | tf_op jit(solution)/shard_map/ppermute | solution.py:1647
  242.4 16.9 %combine_back.1 = (f32[1024,768]{1,0:T(8,128)}, bf16[1024,768]{1,0:T(8,128)(2,1)}, bf16[1024,768]{1,0:T(8,128)(2,1)}, f32[128,768]{1,0:T(8,128)}, f32[1,768]{1,0:T(1,128)}, /*index=5*/f32[8,128]{1,0:T(8,128)}) custom-call(s32[2]{0:T(128)} %pad_add_fusion.refs_0_, f32[1024,768]{1,0:T(8,128)} %get-tuple-element.160.refs_0_.refs_1_, ...), custom_call_target="tpu_custom_call" | custom-call | flops 35433480192 | bytes 125829120 | tf_op jit(solution)/shard_map/combine_back/pallas_call | solution.py:63
  259.3 1.9 add_convert_fusion
  266.9 25.9 %attend_back.1 = (bf16[1024,768]{1,0:T(8,128)(2,1)}, bf16[1024,768]{1,0:T(8,128)(2,1)}, bf16[1024,768]{1,0:T(8,128)(2,1)}) custom-call(bf16[1024,768]{1,0:T(8,128)(2,1)} %get-tuple-element.142.refs_0_, bf16[1024,768]{1,0:T(8,128)(2,1)} %get-tuple-element.143.refs_1_, bf16[1024,768]{1,0:T(8,128)(2,1)} %get-tuple-element.144.refs_2_, ...), custom_call_target="tpu_custom_call" | custom-call | flops 900000000 | bytes 220200 | tf_op jit(solution)/shard_map/attend_back/pallas_call | solution.py:63
  292.8 8.8 %collective-permute-done.27 = bf16[1152,256]{1,0:T(8,128)(2,1)S(1)} collective-permute-done((bf16[1152,256]{1,0:T(8,128)(2,1)}, bf16[1152,256]{1,0:T(8,128)(2,1)S(1)}, u32[]{:S(2)}, u32[]{:S(2)}) %collective-permute-start.27) | collective-permute-done | bytes 589856 | tf_op jit(solution)/shard_map/ppermute | solution.py:1647
  301.6 8.4 %dense_others.1 = bf16[768,1536]{1,0:T(8,128)(2,1)} custom-call(s32[1]{0:T(128)} %bitcast.refs_0_.part_ref, s32[1]{0:T(128)} %bitcast.2.refs_0_.mine_ref, bf16[768,1024]{1,0:T(8,128)(2,1)} %get-tuple-element.167.ht_ref, bf16[768,1024]{1,0:T(8,128)(2,1)} %get-tuple-element.185.ct_ref, bf16[1024,768]{1,0:T(8,128)(2,1)} %get-tuple-element.195.refs_0_.refs_1_, ...), custom_call_target="tpu_custom_call" | custom-call | flops 96636768 | bytes 283115 | tf_op jit(solution)/shard_map/dense_others/pallas_call | solution.py:1396
  310.0 1.6 collective-permute-start.33
  311.6 7.8 %layer_out.1 = bf16[1024,768]{1,0:T(8,128)(2,1)} custom-call(f32[1024,768]{1,0:T(8,128)} %get-tuple-element.160.refs_0_.refs_1_, f32[1024,128]{1,0:T(8,128)} %get-tuple-element.148.refs_2_.refs_4_.refs_1_, bf16[1024,1536]{1,0:T(8,128)(2,1)} %get-tuple-element.161.refs_6_.refs_2_, s32[1024,2]{1,0:T(8,128)} %copy-done.3, ...), custom_call_target="tpu_custom_call" | custom-call | flops 48318384 | bytes 157286 | tf_op jit(solution)/shard_map/layer_out/pallas_call | solution.py:63
  320.8 8.9 %dense_own.1 = (bf16[4,48,1536]{2,1,0:T(8,128)(2,1)}, bf16[4,48,1536]{2,1,0:T(8,128)(2,1)}, bf16[4,48,1536]{2,1,0:T(8,128)(2,1)}, bf16[4,48,1536]{2,1,0:T(8,128)(2,1)}) custom-call(s32[1]{0:T(128)} %bitcast.refs_0_.part_ref, s32[1]{0:T(128)} %bitcast.2.refs_0_.mine_ref, bf16[768,1024]{1,0:T(8,128)(2,1)} %get-tuple-element.167.ht_ref, ...), custom_call_target="tpu_custom_call" | custom-call | flops 96636768 | bytes 283115 | tf_op jit(solution)/shard_map/dense_own/pallas_call | solution.py:1396
  334.8 10.5 %input_grad.1 = (bf16[1024,768]{1,0:T(8,128)(2,1)}, bf16[768,128]{1,0:T(8,128)(2,1)}) custom-call(s32[1]{0:T(128)} %bitcast.refs_0_.part_ref, bf16[1024,768]{1,0:T(8,128)(2,1)} %get-tuple-element.195.refs_0_.refs_1_, bf16[1024,768]{1,0:T(8,128)(2,1)} %get-tuple-element.196.refs_1_.refs_2_, bf16[1024,768]{1,0:T(8,128)(2,1)} %get-tuple-element.197.refs_2_.refs_3_, ...), custom_call_target="tpu_custom_call" | custom-call | flops 72477576 | bytes 220200 | tf_op jit(solution)/shard_map/input_grad/pallas_call | solution.py:63
  347.5 11.5 %unpack.2 = (f32[192,4,4096]{2,1,0:T(4,128)}, f32[512,4,768]{2,1,0:T(4,128)}) custom-call(s32[2]{0:T(128)} %pad_add_fusion.refs_0_, bf16[4,1152,256]{2,1,0:T(8,128)(2,1)} %copy-done, bf16[4,1152,256]{2,1,0:T(8,128)(2,1)} %copy-done.4, bf16[4,1152,256]{2,1,0:T(8,128)(2,1)} %copy-done, bf16[4,1152,256]{2,1,0:T(8,128)(2,1)} %copy-done.4), custom_call_target="tpu_custom_call" | custom-call | bytes 377487 | tf_op jit(solution)/shard_map/unpack/pallas_call | solution.py:63
  359.0 1.8 collective-permute-done.31.refs_4_
  360.8 2.7 fold_quarters.1
  364.8 2.4 collective-permute-start.35
  368.2 17.4 %collective-permute-done.42 = bf16[1152,256]{1,0:T(8,128)(2,1)S(1)} collective-permute-done((bf16[1152,256]{1,0:T(8,128)(2,1)S(1)}, bf16[1152,256]{1,0:T(8,128)(2,1)S(1)}, u32[]{:S(2)}, u32[]{:S(2)}) %collective-permute-start.42) | collective-permute-done | bytes 589856 | tf_op jit(solution)/shard_map/ppermute | solution.py:1647
  385.5 2.7 collective-permute-start.37
  388.3 3.5 collective-permute-done.37.refs_3_
  392.9 2.8 fold_shards.1.refs_1_
  400.5 11.5 %unpack.3 = (f32[192,4,4096]{2,1,0:T(4,128)}, f32[512,4,768]{2,1,0:T(4,128)}) custom-call(s32[2]{0:T(128)} %pad_add_fusion.refs_0_, bf16[4,1152,256]{2,1,0:T(8,128)(2,1)} %copy-done.1, bf16[4,1152,256]{2,1,0:T(8,128)(2,1)} %copy-done.5, bf16[4,1152,256]{2,1,0:T(8,128)(2,1)} %copy-done.1, ...), custom_call_target="tpu_custom_call", output_to_operand_aliasing={{0}: (5, {}), {1}: (6, {})} | custom-call | bytes 377487 | tf_op jit(solution)/shard_map/unpack/pallas_call | solution.py:63
  412.9 2.1 lay_tail.1.refs_1_
  415.0 2.3 collective-permute-done.45.refs_2_
  418.1 2.9 unpack_dense.1
  (206 shorter events, 56.9 us)
Async XLA Ops:
  7.2 115.1 %all-gather.3.cloned.1.call-start = ((), (), s32[]{:S(2)}) async-start(), calls=%async_computation.4 | async-start | bytes 5898240 | tf_op jit(solution)/shard_map/all_gather | solution.py:1697
  11.7 21.5 %collective-permute-start.2 = (bf16[64,1536]{1,0:T(8,128)(2,1)}, bf16[64,1536]{1,0:T(8,128)(2,1)S(1)}, u32[]{:S(2)}, u32[]{:S(2)}) collective-permute-start(bf16[64,1536]{1,0:T(8,128)(2,1)} %get-tuple-element.131.refs_1_), channel_id=1, source_target_pairs={{0,3},{1,0},{2,1},{3,2},{4,7},{5,4},{6,5},{7,6},{8,11},{9,8},{10,9... | collective-permute-start | bytes 589832 | tf_op jit(solution)/shard_map/ppermute | solution.py:1653
  16.8 16.9 %collective-permute-start.1 = (bf16[64,1536]{1,0:T(8,128)(2,1)}, bf16[64,1536]{1,0:T(8,128)(2,1)S(1)}, u32[]{:S(2)}, u32[]{:S(2)}) collective-permute-start(bf16[64,1536]{1,0:T(8,128)(2,1)} %get-tuple-element.131.refs_1_), channel_id=1, source_target_pairs={{0,2},{1,3},{2,0},{3,1},{4,6},{5,7},{6,4},{7,5},{8,10},{9,11},{10,... | collective-permute-start | bytes 589832 | tf_op jit(solution)/shard_map/ppermute | solution.py:1653
  16.8 16.9 %collective-permute-start = (bf16[64,1536]{1,0:T(8,128)(2,1)}, bf16[64,1536]{1,0:T(8,128)(2,1)S(1)}, u32[]{:S(2)}, u32[]{:S(2)}) collective-permute-start(bf16[64,1536]{1,0:T(8,128)(2,1)} %get-tuple-element.131.refs_1_), channel_id=1, source_target_pairs={{0,1},{1,2},{2,3},{3,0},{4,5},{5,6},{6,7},{7,4},{8,9},{9,10},{10,1... | collective-permute-start | bytes 589832 | tf_op jit(solution)/shard_map/ppermute | solution.py:1653
  30.1 234.8 %reduce-scatter.3.cloned.1.call-start = ((), (), s32[]{:S(2)}) async-start(), calls=%async_computation.2 | async-start | bytes 2949120 | tf_op jit(solution)/shard_map/reduce_scatter | solution.py:1757
  36.5 14.2 %collective-permute-start.6 = (bf16[4,48,1152]{2,1,0:T(8,128)(2,1)}, bf16[4,48,1152]{2,1,0:T(8,128)(2,1)S(1)}, u32[]{:S(2)}, u32[]{:S(2)}) collective-permute-start(bf16[4,48,1152]{2,1,0:T(8,128)(2,1)} %get-tuple-element.134.refs_1_), channel_id=1, source_target_pairs={{0,24},{4,28},{8,16},{12,20},{16,8},{20,12},{24,0},{28,4},{1,25},{... | collective-permute-start | bytes 1327112 | tf_op jit(solution)/shard_map/ppermute | solution.py:1647
  39.0 20.5 %collective-permute-start.5 = (bf16[4,48,1152]{2,1,0:T(8,128)(2,1)}, bf16[4,48,1152]{2,1,0:T(8,128)(2,1)}, u32[]{:S(2)}, u32[]{:S(2)}) collective-permute-start(bf16[4,48,1152]{2,1,0:T(8,128)(2,1)} %get-tuple-element.134.refs_1_), channel_id=1, source_target_pairs={{0,16},{4,20},{8,24},{12,28},{16,0},{20,4},{24,8},{28,12},{1,17},{... | collective-permute-start | bytes 1327112 | tf_op jit(solution)/shard_map/ppermute | solution.py:1647
  39.5 20.1 %collective-permute-start.4 = (bf16[4,48,1152]{2,1,0:T(8,128)(2,1)}, bf16[4,48,1152]{2,1,0:T(8,128)(2,1)}, u32[]{:S(2)}, u32[]{:S(2)}) collective-permute-start(bf16[4,48,1152]{2,1,0:T(8,128)(2,1)} %get-tuple-element.134.refs_1_), channel_id=1, source_target_pairs={{0,8},{4,12},{8,0},{12,4},{16,24},{20,28},{24,16},{28,20},{1,9},{5... | collective-permute-start | bytes 1327112 | tf_op jit(solution)/shard_map/ppermute | solution.py:1647
  62.4 13.7 %collective-permute-start.7 = (bf16[768,1152]{1,0:T(8,128)(2,1)}, bf16[768,1152]{1,0:T(8,128)(2,1)S(1)}, u32[]{:S(2)}, u32[]{:S(2)}) collective-permute-start(bf16[768,1152]{1,0:T(8,128)(2,1)} %bitcast.35), channel_id=1, source_target_pairs={{0,4},{4,0},{8,12},{12,8},{16,20},{20,16},{24,28},{28,24},{1,5},{5... | collective-permute-start | bytes 5308424 | tf_op jit(solution)/shard_map/ppermute | solution.py:1650
  62.4 9.6 %collective-permute-start.10 = (bf16[4,48,384]{2,1,0:T(8,128)(2,1)S(1)}, bf16[4,48,384]{2,1,0:T(8,128)(2,1)S(1)}, u32[]{:S(2)}, u32[]{:S(2)}) collective-permute-start(bf16[4,48,384]{2,1,0:T(8,128)(2,1)S(1)} %copy-done.32), channel_id=1, source_target_pairs={{0,24},{4,28},{8,16},{12,20},{16,8},{20,12},{24,0},{28,4},{1,25},{... | collective-permute-start | bytes 442376 | tf_op jit(solution)/shard_map/ppermute | solution.py:1647
  64.0 8.7 %collective-permute-start.9 = (bf16[4,48,384]{2,1,0:T(8,128)(2,1)S(1)}, bf16[4,48,384]{2,1,0:T(8,128)(2,1)S(1)}, u32[]{:S(2)}, u32[]{:S(2)}) collective-permute-start(bf16[4,48,384]{2,1,0:T(8,128)(2,1)S(1)} %copy-done.32), channel_id=1, source_target_pairs={{0,16},{4,20},{8,24},{12,28},{16,0},{20,4},{24,8},{28,12},{1,17},{... | collective-permute-start | bytes 442376 | tf_op jit(solution)/shard_map/ppermute | solution.py:1647
  65.4 7.4 %collective-permute-start.8 = (bf16[4,48,384]{2,1,0:T(8,128)(2,1)S(1)}, bf16[4,48,384]{2,1,0:T(8,128)(2,1)S(1)}, u32[]{:S(2)}, u32[]{:S(2)}) collective-permute-start(bf16[4,48,384]{2,1,0:T(8,128)(2,1)S(1)} %copy-done.32), channel_id=1, source_target_pairs={{0,8},{4,12},{8,0},{12,4},{16,24},{20,28},{24,16},{28,20},{1,9},{5... | collective-permute-start | bytes 442376 | tf_op jit(solution)/shard_map/ppermute | solution.py:1647
  86.8 28.1 %collective-permute-start.12 = (bf16[384,768]{1,0:T(8,128)(2,1)S(1)}, bf16[384,768]{1,0:T(8,128)(2,1)}, u32[]{:S(2)}, u32[]{:S(2)}) collective-permute-start(bf16[384,768]{1,0:T(8,128)(2,1)S(1)} %copy-done.49), channel_id=1, source_target_pairs={{0,8},{4,12},{8,0},{12,4},{16,24},{20,28},{24,16},{28,20},{1,9},{5... | collective-permute-start | bytes 1769480 | tf_op jit(solution)/shard_map/ppermute | solution.py:1647
  88.4 27.8 %collective-permute-start.13 = (bf16[384,768]{1,0:T(8,128)(2,1)S(1)}, bf16[384,768]{1,0:T(8,128)(2,1)}, u32[]{:S(2)}, u32[]{:S(2)}) collective-permute-start(bf16[384,768]{1,0:T(8,128)(2,1)S(1)} %copy-done.48), channel_id=1, source_target_pairs={{0,16},{4,20},{8,24},{12,28},{16,0},{20,4},{24,8},{28,12},{1,17},{... | collective-permute-start | bytes 1769480 | tf_op jit(solution)/shard_map/ppermute | solution.py:1647
  89.1 27.1 %collective-permute-start.14 = (bf16[384,768]{1,0:T(8,128)(2,1)S(1)}, bf16[384,768]{1,0:T(8,128)(2,1)}, u32[]{:S(2)}, u32[]{:S(2)}) collective-permute-start(bf16[384,768]{1,0:T(8,128)(2,1)S(1)} %copy-done.47), channel_id=1, source_target_pairs={{0,24},{4,28},{8,16},{12,20},{16,8},{20,12},{24,0},{28,4},{1,25},{... | collective-permute-start | bytes 1769480 | tf_op jit(solution)/shard_map/ppermute | solution.py:1647
  90.4 15.5 %collective-permute-start.11 = (bf16[768,384]{1,0:T(8,128)(2,1)S(1)}, bf16[768,384]{1,0:T(8,128)(2,1)S(1)}, u32[]{:S(2)}, u32[]{:S(2)}) collective-permute-start(bf16[768,384]{1,0:T(8,128)(2,1)S(1)} %bitcast.43), channel_id=1, source_target_pairs={{0,4},{4,0},{8,12},{12,8},{16,20},{20,16},{24,28},{28,24},{1,5},{5... | collective-permute-start | bytes 1769480 | tf_op jit(solution)/shard_map/ppermute | solution.py:1650
  122.3 30.0 %collective-permute-start.18 = (bf16[4,2304,256]{2,1,0:T(8,128)(2,1)}, bf16[4,2304,256]{2,1,0:T(8,128)(2,1)S(1)}, u32[]{:S(2)}, u32[]{:S(2)}) collective-permute-start(bf16[4,2304,256]{2,1,0:T(8,128)(2,1)} %bitcast.38), channel_id=1, source_target_pairs={{0,4},{4,0},{8,12},{12,8},{16,20},{20,16},{24,28},{28,24},{1,5},{5... | collective-permute-start | bytes 14155784 | tf_op jit(solution)/shard_map/ppermute | solution.py:1650
  122.3 18.2 %collective-permute-start.15 = (bf16[400,768]{1,0:T(8,128)(2,1)}, bf16[400,768]{1,0:T(8,128)(2,1)S(1)}, u32[]{:S(2)}, u32[]{:S(2)}) collective-permute-start(bf16[400,768]{1,0:T(8,128)(2,1)} %get-tuple-element.162), channel_id=1, source_target_pairs={{0,8},{4,12},{8,0},{12,4},{16,24},{20,28},{24,16},{28,20},{1,9},{5... | collective-permute-start | bytes 1843208 | tf_op jit(solution)/shard_map/ppermute | solution.py:1647
  123.0 17.5 %collective-permute-start.16 = (bf16[400,768]{1,0:T(8,128)(2,1)}, bf16[400,768]{1,0:T(8,128)(2,1)S(1)}, u32[]{:S(2)}, u32[]{:S(2)}) collective-permute-start(bf16[400,768]{1,0:T(8,128)(2,1)} %get-tuple-element.163), channel_id=1, source_target_pairs={{0,16},{4,20},{8,24},{12,28},{16,0},{20,4},{24,8},{28,12},{1,17},{... | collective-permute-start | bytes 1843208 | tf_op jit(solution)/shard_map/ppermute | solution.py:1647
  124.3 28.0 %collective-permute-start.17 = (bf16[400,768]{1,0:T(8,128)(2,1)}, bf16[400,768]{1,0:T(8,128)(2,1)}, u32[]{:S(2)}, u32[]{:S(2)}) collective-permute-start(bf16[400,768]{1,0:T(8,128)(2,1)} %get-tuple-element.164), channel_id=1, source_target_pairs={{0,24},{4,28},{8,16},{12,20},{16,8},{20,12},{24,0},{28,4},{1,25},{... | collective-permute-start | bytes 1843208 | tf_op jit(solution)/shard_map/ppermute | solution.py:1647
  182.9 24.3 %collective-permute-start.25 = (bf16[4,1152,256]{2,1,0:T(8,128)(2,1)}, bf16[4,1152,256]{2,1,0:T(8,128)(2,1)S(1)}, u32[]{:S(2)}, u32[]{:S(2)}) collective-permute-start(bf16[4,1152,256]{2,1,0:T(8,128)(2,1)} %get-tuple-element.187), channel_id=1, source_target_pairs={{0,4},{4,0},{8,12},{12,8},{16,20},{20,16},{24,28},{28,24},{1,5},{5... | collective-permute-start | bytes 7077896 | tf_op jit(solution)/shard_map/ppermute | solution.py:1650
  209.2 110.2 %reduce-scatter.5.cloned.1.call-start = ((), (), s32[]{:S(2)}) async-start(), calls=%async_computation.3 | async-start | bytes 2949120 | tf_op jit(solution)/shard_map/reduce_scatter | solution.py:1757
  210.3 18.4 %collective-permute-start.19 = (bf16[400,768]{1,0:T(8,128)(2,1)S(1)}, bf16[400,768]{1,0:T(8,128)(2,1)S(1)}, u32[]{:S(2)}, u32[]{:S(2)}) collective-permute-start(bf16[400,768]{1,0:T(8,128)(2,1)S(1)} %copy-done.42), channel_id=1, source_target_pairs={{0,8},{4,12},{8,0},{12,4},{16,24},{20,28},{24,16},{28,20},{1,9},{5... | collective-permute-start | bytes 1843208 | tf_op jit(solution)/shard_map/ppermute | solution.py:1647
  212.5 29.1 %collective-permute-start.20 = (bf16[400,768]{1,0:T(8,128)(2,1)S(1)}, bf16[400,768]{1,0:T(8,128)(2,1)S(1)}, u32[]{:S(2)}, u32[]{:S(2)}) collective-permute-start(bf16[400,768]{1,0:T(8,128)(2,1)S(1)} %copy-done.41), channel_id=1, source_target_pairs={{0,16},{4,20},{8,24},{12,28},{16,0},{20,4},{24,8},{28,12},{1,17},{... | collective-permute-start | bytes 1843208 | tf_op jit(solution)/shard_map/ppermute | solution.py:1647
  213.2 28.4 %collective-permute-start.21 = (bf16[400,768]{1,0:T(8,128)(2,1)S(1)}, bf16[400,768]{1,0:T(8,128)(2,1)}, u32[]{:S(2)}, u32[]{:S(2)}) collective-permute-start(bf16[400,768]{1,0:T(8,128)(2,1)S(1)} %copy-done.40), channel_id=1, source_target_pairs={{0,24},{4,28},{8,16},{12,20},{16,8},{20,12},{24,0},{28,4},{1,25},{... | collective-permute-start | bytes 1843208 | tf_op jit(solution)/shard_map/ppermute | solution.py:1647
  228.6 30.7 %collective-permute-start.29 = (bf16[4,1152,256]{2,1,0:T(8,128)(2,1)}, bf16[4,1152,256]{2,1,0:T(8,128)(2,1)S(1)}, u32[]{:S(2)}, u32[]{:S(2)}) collective-permute-start(bf16[4,1152,256]{2,1,0:T(8,128)(2,1)} %get-tuple-element.208), channel_id=1, source_target_pairs={{0,4},{4,0},{8,12},{12,8},{16,20},{20,16},{24,28},{28,24},{1,5},{5... | collective-permute-start | bytes 7077896 | tf_op jit(solution)/shard_map/ppermute | solution.py:1650
  261.3 31.5 %collective-permute-start.22 = (bf16[384,768]{1,0:T(8,128)(2,1)}, bf16[384,768]{1,0:T(8,128)(2,1)S(1)}, u32[]{:S(2)}, u32[]{:S(2)}) collective-permute-start(bf16[384,768]{1,0:T(8,128)(2,1)} %get-tuple-element.182), channel_id=1, source_target_pairs={{0,8},{4,12},{8,0},{12,4},{16,24},{20,28},{24,16},{28,20},{1,9},{5... | collective-permute-start | bytes 1769480 | tf_op jit(solution)/shard_map/ppermute | solution.py:1647
  262.3 30.4 %collective-permute-start.23 = (bf16[384,768]{1,0:T(8,128)(2,1)S(1)}, bf16[384,768]{1,0:T(8,128)(2,1)S(1)}, u32[]{:S(2)}, u32[]{:S(2)}) collective-permute-start(bf16[384,768]{1,0:T(8,128)(2,1)S(1)} %copy-done.46), channel_id=1, source_target_pairs={{0,16},{4,20},{8,24},{12,28},{16,0},{20,4},{24,8},{28,12},{1,17},{... | collective-permute-start | bytes 1769480 | tf_op jit(solution)/shard_map/ppermute | solution.py:1647
  263.4 29.4 %collective-permute-start.24 = (bf16[384,768]{1,0:T(8,128)(2,1)S(1)}, bf16[384,768]{1,0:T(8,128)(2,1)S(1)}, u32[]{:S(2)}, u32[]{:S(2)}) collective-permute-start(bf16[384,768]{1,0:T(8,128)(2,1)S(1)} %copy-done.45), channel_id=1, source_target_pairs={{0,24},{4,28},{8,16},{12,20},{16,8},{20,12},{24,0},{28,4},{1,25},{... | collective-permute-start | bytes 1769480 | tf_op jit(solution)/shard_map/ppermute | solution.py:1647
  264.9 36.7 %collective-permute-start.27 = (bf16[1152,256]{1,0:T(8,128)(2,1)}, bf16[1152,256]{1,0:T(8,128)(2,1)S(1)}, u32[]{:S(2)}, u32[]{:S(2)}) collective-permute-start(bf16[1152,256]{1,0:T(8,128)(2,1)} %bitcast.47), channel_id=1, source_target_pairs={{0,16},{4,20},{8,24},{12,28},{16,0},{20,4},{24,8},{28,12},{1,17},{... | collective-permute-start | bytes 1769480 | tf_op jit(solution)/shard_map/ppermute | solution.py:1647
  265.8 35.8 %collective-permute-start.26 = (bf16[1152,256]{1,0:T(8,128)(2,1)}, bf16[1152,256]{1,0:T(8,128)(2,1)S(1)}, u32[]{:S(2)}, u32[]{:S(2)}) collective-permute-start(bf16[1152,256]{1,0:T(8,128)(2,1)} %bitcast.48), channel_id=1, source_target_pairs={{0,8},{4,12},{8,0},{12,4},{16,24},{20,28},{24,16},{28,20},{1,9},{5... | collective-permute-start | bytes 1769480 | tf_op jit(solution)/shard_map/ppermute | solution.py:1647
  310.0 9.4 %collective-permute-start.28 = (bf16[768,1536]{1,0:T(8,128)(2,1)}, bf16[768,1536]{1,0:T(8,128)(2,1)S(1)}, u32[]{:S(2)}, u32[]{:S(2)}) collective-permute-start(bf16[768,1536]{1,0:T(8,128)(2,1)} %dense_others.1), channel_id=1, source_target_pairs={{0,4},{4,0},{8,12},{12,8},{16,20},{20,16},{24,28},{28,24},{1,5},{5... | collective-permute-start | bytes 7077896 | tf_op jit(solution)/shard_map/ppermute | solution.py:1650
  310.0 19.7 %collective-permute-start.33 = (bf16[1152,256]{1,0:T(8,128)(2,1)S(1)}, bf16[1152,256]{1,0:T(8,128)(2,1)}, u32[]{:S(2)}, u32[]{:S(2)}) collective-permute-start(bf16[1152,256]{1,0:T(8,128)(2,1)S(1)} %bitcast.49), channel_id=1, source_target_pairs={{0,24},{4,28},{8,16},{12,20},{16,8},{20,12},{24,0},{28,4},{1,25},{... | collective-permute-start | bytes 1769480 | tf_op jit(solution)/shard_map/ppermute | solution.py:1647
  331.1 15.0 %collective-permute-start.34 = (bf16[4,1152,256]{2,1,0:T(8,128)(2,1)S(1)}, bf16[4,1152,256]{2,1,0:T(8,128)(2,1)S(1)}, u32[]{:S(2)}, u32[]{:S(2)}) collective-permute-start(bf16[4,1152,256]{2,1,0:T(8,128)(2,1)S(1)} %pad_maximum_fusion.refs_1_.refs_3_), channel_id=1, source_target_pairs={{0,4},{4,0},{8,12},{12,8},{16,20},{20,16},{24,28},{28,24},{1,5},{5... | collective-permute-start | bytes 7077896 | tf_op jit(solution)/shard_map/ppermute | solution.py:1650
  331.3 27.7 %collective-permute-start.30 = (bf16[4,48,1536]{2,1,0:T(8,128)(2,1)}, bf16[4,48,1536]{2,1,0:T(8,128)(2,1)}, u32[]{:S(2)}, u32[]{:S(2)}) collective-permute-start(bf16[4,48,1536]{2,1,0:T(8,128)(2,1)} %get-tuple-element.213), channel_id=1, source_target_pairs={{0,8},{4,12},{8,0},{12,4},{16,24},{20,28},{24,16},{28,20},{1,9},{5... | collective-permute-start | bytes 1769480 | tf_op jit(solution)/shard_map/ppermute | solution.py:1647
  332.1 28.7 %collective-permute-start.31 = (bf16[4,48,1536]{2,1,0:T(8,128)(2,1)}, bf16[4,48,1536]{2,1,0:T(8,128)(2,1)}, u32[]{:S(2)}, u32[]{:S(2)}) collective-permute-start(bf16[4,48,1536]{2,1,0:T(8,128)(2,1)} %get-tuple-element.214), channel_id=1, source_target_pairs={{0,16},{4,20},{8,24},{12,28},{16,0},{20,4},{24,8},{28,12},{1,17},{... | collective-permute-start | bytes 1769480 | tf_op jit(solution)/shard_map/ppermute | solution.py:1647
  333.3 27.6 %collective-permute-start.32 = (bf16[4,48,1536]{2,1,0:T(8,128)(2,1)}, bf16[4,48,1536]{2,1,0:T(8,128)(2,1)}, u32[]{:S(2)}, u32[]{:S(2)}) collective-permute-start(bf16[4,48,1536]{2,1,0:T(8,128)(2,1)} %get-tuple-element.215), channel_id=1, source_target_pairs={{0,24},{4,28},{8,16},{12,20},{16,8},{20,12},{24,0},{28,4},{1,25},{... | collective-permute-start | bytes 1769480 | tf_op jit(solution)/shard_map/ppermute | solution.py:1647
  345.3 40.2 %collective-permute-start.42 = (bf16[1152,256]{1,0:T(8,128)(2,1)S(1)}, bf16[1152,256]{1,0:T(8,128)(2,1)S(1)}, u32[]{:S(2)}, u32[]{:S(2)}) collective-permute-start(bf16[1152,256]{1,0:T(8,128)(2,1)S(1)} %bitcast.44), channel_id=1, source_target_pairs={{0,16},{4,20},{8,24},{12,28},{16,0},{20,4},{24,8},{28,12},{1,17},{... | collective-permute-start | bytes 1769480 | tf_op jit(solution)/shard_map/ppermute | solution.py:1647
  346.1 42.2 %collective-permute-start.41 = (bf16[1152,256]{1,0:T(8,128)(2,1)S(1)}, bf16[1152,256]{1,0:T(8,128)(2,1)S(1)}, u32[]{:S(2)}, u32[]{:S(2)}) collective-permute-start(bf16[1152,256]{1,0:T(8,128)(2,1)S(1)} %bitcast.45), channel_id=1, source_target_pairs={{0,8},{4,12},{8,0},{12,4},{16,24},{20,28},{24,16},{28,20},{1,9},{5... | collective-permute-start | bytes 1769480 | tf_op jit(solution)/shard_map/ppermute | solution.py:1647
  363.5 28.3 %collective-permute-start.43 = (bf16[1152,256]{1,0:T(8,128)(2,1)S(1)}, bf16[1152,256]{1,0:T(8,128)(2,1)S(1)}, u32[]{:S(2)}, u32[]{:S(2)}) collective-permute-start(bf16[1152,256]{1,0:T(8,128)(2,1)S(1)} %bitcast.46), channel_id=1, source_target_pairs={{0,24},{4,28},{8,16},{12,20},{16,8},{20,12},{24,0},{28,4},{1,25},{... | collective-permute-start | bytes 1769480 | tf_op jit(solution)/shard_map/ppermute | solution.py:1647
  364.8 23.5 %collective-permute-start.35 = (bf16[64,1536]{1,0:T(8,128)(2,1)}, bf16[64,1536]{1,0:T(8,128)(2,1)S(1)}, u32[]{:S(2)}, u32[]{:S(2)}) collective-permute-start(bf16[64,1536]{1,0:T(8,128)(2,1)} %get-tuple-element.231), channel_id=1, source_target_pairs={{0,1},{1,2},{2,3},{3,0},{4,5},{5,6},{6,7},{7,4},{8,9},{9,10},{10,1... | collective-permute-start | bytes 589832 | tf_op jit(solution)/shard_map/ppermute | solution.py:1653
  367.2 21.1 %collective-permute-start.36 = (bf16[64,1536]{1,0:T(8,128)(2,1)}, bf16[64,1536]{1,0:T(8,128)(2,1)S(1)}, u32[]{:S(2)}, u32[]{:S(2)}) collective-permute-start(bf16[64,1536]{1,0:T(8,128)(2,1)} %get-tuple-element.232), channel_id=1, source_target_pairs={{0,2},{1,3},{2,0},{3,1},{4,6},{5,7},{6,4},{7,5},{8,10},{9,11},{10,... | collective-permute-start | bytes 589832 | tf_op jit(solution)/shard_map/ppermute | solution.py:1653
  385.5 6.3 %collective-permute-start.37 = (bf16[64,1536]{1,0:T(8,128)(2,1)}, bf16[64,1536]{1,0:T(8,128)(2,1)S(1)}, u32[]{:S(2)}, u32[]{:S(2)}) collective-permute-start(bf16[64,1536]{1,0:T(8,128)(2,1)} %get-tuple-element.233), channel_id=1, source_target_pairs={{0,3},{1,0},{2,1},{3,2},{4,7},{5,4},{6,5},{7,6},{8,11},{9,8},{10,9... | collective-permute-start | bytes 589832 | tf_op jit(solution)/shard_map/ppermute | solution.py:1653
  392.8 6.3 %collective-permute-start.44 = (bf16[4,1152,256]{2,1,0:T(8,128)(2,1)S(1)}, bf16[4,1152,256]{2,1,0:T(8,128)(2,1)S(1)}, u32[]{:S(2)}, u32[]{:S(2)}) collective-permute-start(bf16[4,1152,256]{2,1,0:T(8,128)(2,1)S(1)} %pad_maximum_fusion.1.refs_1_.refs_3_), channel_id=1, source_target_pairs={{0,4},{4,0},{8,12},{12,8},{16,20},{20,16},{24,28},{28,24},{1,5},{5... | collective-permute-start | bytes 7077896 | tf_op jit(solution)/shard_map/ppermute | solution.py:1650
  395.6 16.4 %collective-permute-start.40 = (bf16[64,1536]{1,0:T(8,128)(2,1)}, bf16[64,1536]{1,0:T(8,128)(2,1)S(1)}, u32[]{:S(2)}, u32[]{:S(2)}) collective-permute-start(bf16[64,1536]{1,0:T(8,128)(2,1)} %fold_shards.1.refs_1_), channel_id=1, source_target_pairs={{0,24},{4,28},{8,16},{12,20},{16,8},{20,12},{24,0},{28,4},{1,25},{... | collective-permute-start | bytes 589832 | tf_op jit(solution)/shard_map/ppermute | solution.py:1647
  397.0 15.0 %collective-permute-start.39 = (bf16[64,1536]{1,0:T(8,128)(2,1)}, bf16[64,1536]{1,0:T(8,128)(2,1)S(1)}, u32[]{:S(2)}, u32[]{:S(2)}) collective-permute-start(bf16[64,1536]{1,0:T(8,128)(2,1)} %fold_shards.1.refs_1_), channel_id=1, source_target_pairs={{0,16},{4,20},{8,24},{12,28},{16,0},{20,4},{24,8},{28,12},{1,17},{... | collective-permute-start | bytes 589832 | tf_op jit(solution)/shard_map/ppermute | solution.py:1647
  398.3 13.8 %collective-permute-start.38 = (bf16[64,1536]{1,0:T(8,128)(2,1)}, bf16[64,1536]{1,0:T(8,128)(2,1)S(1)}, u32[]{:S(2)}, u32[]{:S(2)}) collective-permute-start(bf16[64,1536]{1,0:T(8,128)(2,1)} %fold_shards.1.refs_1_), channel_id=1, source_target_pairs={{0,8},{4,12},{8,0},{12,4},{16,24},{20,28},{24,16},{28,20},{1,9},{5... | collective-permute-start | bytes 589832 | tf_op jit(solution)/shard_map/ppermute | solution.py:1647
  415.0 2.3 collective-permute-start.45
  (51 other events, 285.9 us)
Sparse Core Ops, SparseCore 0:
  30.2 90.0 all-gather.2
  209.3 48.5 reduce-scatter.2
  261.4 47.4 reduce-scatter.4
